TPU v7x, 32 devices: a whole 2x2x4 slice. The times are simulated.
32 devices in a mesh: grp: 2 (over y), gx: 4 (over z), gy: 2 (over x), gz: 2 (over core).
Axes of the slice: x: 2, y: 2, z: 4, core: 2. Of those that a mesh axis runs over, the one named last changes fastest.
Arguments:
- parent_old: float32 [8, 384, 512], P(None, ('grp', 'gx', 'gz'), 'gy'), parts along dimension 1, may hold values from -6 to 6
- parent_source: float32 [8, 384, 512], P(None, ('grp', 'gx', 'gz'), 'gy'), parts along dimension 1, may hold values from -4 to 4
- parent_coefs: float32 [2, 8], replicated, may hold values from 0.02 to 0.1
- nest_old: float32 [8, 1152, 768], P(None, ('grp', 'gx', 'gz'), 'gy'), parts along dimension 1, may hold values from -6 to 6
- nest_source: float32 [8, 1152, 768], P(None, ('grp', 'gx', 'gz'), 'gy'), parts along dimension 1, may hold values from -2 to 2
- nest_coefs: float32 [2, 8], replicated, may hold values from 0.02 to 0.1
- offset_x: int32 [2], P('grp'), parts along dimension 0, may hold values from 1 to 23
- offset_y: int32 [2], P('grp'), parts along dimension 0, may hold values from 1 to 255
Outputs:
- parent_new: float32 [8, 384, 512], P(None, ('grp', 'gx', 'gz'), 'gy'), parts along dimension 1
- nest_new: float32 [8, 1152, 768], P(None, ('grp', 'gx', 'gz'), 'gy'), parts along dimension 1
There are 2 independent parts, one for each index of `grp`. A program takes and returns all parts, laid end to end along the dimension named above; an argument that names none is the same for every part. Nothing has to cross between parts.
All inputs are finite; a program needn't handle non-finite values.
Results may differ from a plain program's by a relative error of at most 0.00002.
Values sent between devices are 32-bit elements; how exact they have to be, the bound alone decides.
No kernel may reach another device: no remote copies, remote signals or barrier semaphores. Data moves between devices by JAX's collectives and lax.ppermute only.
A program may use at most 128 MiB of HBM per device.

v0:
```python
import functools

import jax
import jax.numpy as jnp
from jax import lax
from jax.experimental import pallas as pl
from jax.experimental.pallas import tpu as pltpu
from jax.sharding import PartitionSpec as P

RATIO = 3
SUBSTEPS = 3
RIM = 6
LANES = 128
STRIDE = 16
SOURCE_AT = 3
PARENT_AT = 6
STRIP_AT = 8
STRIP_SOURCE_AT = 12
SOURCE_ROW = 24
TAIL_ROW = 40
FIXED = 8
LEFT_AT = 3
RIGHT_OWN = STRIDE - 3
VMEM = pltpu.VMEM
LIMIT = 24 * 1024 * 1024
MOST = 54 * 1024 * 1024
HIGHEST = lax.Precision.HIGHEST


def iota(shape, dim):
    return lax.broadcasted_iota(jnp.int32, shape, dim)


def whole():
    return pl.BlockSpec(memory_space=VMEM)


def scalars():
    return pl.BlockSpec(memory_space=pltpu.SMEM)


def params(limit=LIMIT):
    return pltpu.CompilerParams(vmem_limit_bytes=limit)


def cost(flops, moved):
    return pl.CostEstimate(flops=flops, bytes_accessed=moved, transcendentals=0)


def tile(ref, level, index):
    return ref[level, :, index * LANES : (index + 1) * LANES]


def turned(value, lanes):
    lanes = lanes % LANES
    return pltpu.roll(value, lanes, 1) if lanes else value


def edge_strip(dest, band, oy, parent, parent_source):
    levels, rows, cols = parent.shape
    lane = iota((rows, LANES), 1)
    base = jnp.where(dest == 0, oy - 1, oy + band - 3) - lax.axis_index("gy") * cols
    total = jnp.zeros(lane.shape, jnp.float32)
    for ref, first in ((parent, STRIP_AT), (parent_source, STRIP_SOURCE_AT)):
        for level in range(levels):
            found = jnp.zeros(lane.shape, jnp.float32)
            for at in range(cols // LANES):
                place = lane + (at * LANES - base)
                found = jnp.where((place >= 0) & (place < 4), tile(ref, level, at), found)
            turn = (16384 + first + STRIDE * level - base) & (LANES - 1)
            total = total + pltpu.roll(found, turn, 1)
    return total


def pack_pair(nest, source, parent, parent_source, out, fine_buf, coarse_buf, sems):
    levels, rows, cols = nest.shape
    parent_rows, parent_cols = parent.shape[1:]
    right = lax.axis_index("gy") == 0
    loads = []
    for at, (ref, buf) in enumerate(
        (
            (parent, coarse_buf.at[0]),
            (parent_source, coarse_buf.at[1]),
            (nest, fine_buf.at[0]),
            (source, fine_buf.at[1]),
        )
    ):
        start = pl.multiple_of(jnp.where(right, ref.shape[2] - LANES, 0), LANES)
        loads.append(pltpu.make_async_copy(ref.at[:, :, pl.ds(start, LANES)], buf, sems.at[at]))
    for copy in loads:
        copy.start()

    def columns(value, count, to):
        first = jnp.where(right, LANES - count, 0)
        place = iota(value.shape, 1) - first
        value = jnp.where((place >= 0) & (place < count), value, 0.0)
        return pltpu.roll(value, (LANES + to - first) & (LANES - 1), 1)

    part = jnp.zeros((parent_rows, LANES), jnp.float32)
    loads[0].wait()
    loads[1].wait()
    for level in range(levels):
        base = STRIDE * level
        part = part + columns(coarse_buf[0, level], 1, base + PARENT_AT)
        part = part + columns(coarse_buf[0, level], 2, base + STRIP_AT)
        part = part + columns(coarse_buf[1, level], 2, base + STRIP_SOURCE_AT)
    total = jnp.zeros((rows, LANES), jnp.float32)
    loads[2].wait()
    loads[3].wait()
    for level in range(levels):
        base = STRIDE * level
        total = total + columns(fine_buf[0, level], 3, base)
        total = total + columns(fine_buf[1, level], 3, base + SOURCE_AT)
    out[...] = total
    out[:parent_rows, :] += part


def across_border(message, oy, parent_cols, me):
    c = iota(message.shape, 1) & (STRIDE - 1)
    place = jnp.where(me == 0, parent_cols + 1, 1) - oy
    total = jnp.zeros(message.shape, jnp.float32)
    for turn in (-1, 0, 2, 3):
        at = jnp.where(c >= STRIP_SOURCE_AT, c - STRIP_SOURCE_AT, c - STRIP_AT) - turn
        fits = (c >= STRIP_AT) & (at >= 0) & (at < 2) & (place == turn)
        total = total + jnp.where(fits, turned(message, turn), 0.0)
    return total


def pack_columns(parts, band, oy_hbm, nest, source, parent_hbm, parent_source_hbm, *rest):
    outs = rest[: parts - 1]
    old_buf, src_buf, parent, parent_source, oy_ref, sems, field_sems = rest[parts - 1 :]
    levels, rows, cols = nest.shape
    parent_cols = parent.shape[2]
    me = lax.axis_index("gy")
    sides = [1] if parts == 2 else [1, parts - 1]
    fields = [
        pltpu.make_async_copy(ref, buf, field_sems.at[at])
        for at, (ref, buf) in enumerate(
            ((oy_hbm, oy_ref), (parent_hbm, parent), (parent_source_hbm, parent_source))
        )
    ]
    for copy in fields:
        copy.start()
    copies = []
    for at, step in enumerate(sides):
        right = (me == 0) if parts == 2 else jnp.bool_(step == 1)
        start = pl.multiple_of(jnp.where(right, cols - LANES, 0), LANES)
        pair = [
            pltpu.make_async_copy(
                ref.at[:, :, pl.ds(start, LANES)], buf.at[at], sems.at[at, which]
            )
            for which, (ref, buf) in enumerate(((nest, old_buf), (source, src_buf)))
        ]
        for copy in pair:
            copy.start()
        copies.append((right, pair))
    for copy in fields:
        copy.wait()
    oy = oy_ref[0]
    lane = iota((parent.shape[1], LANES), 1)
    for step in range(1, parts):
        out = outs[step - 1]
        part = edge_strip(lax.rem(me + step, parts), band, oy, parent, parent_source)
        if step not in sides:
            out[...] = part
            continue
        at = sides.index(step)
        right, pair = copies[at]
        first = jnp.where(right, LANES - 3, 0)
        outer = jnp.where(right, LANES - 1, 0)
        for level in range(levels):
            edge = jnp.where(
                right, tile(parent, level, parent_cols // LANES - 1), tile(parent, level, 0)
            )
            edge = jnp.where(lane == outer, edge, 0.0)
            turn = (LANES + PARENT_AT + STRIDE * level - outer) & (LANES - 1)
            part = part + pltpu.roll(edge, turn, 1)
        for copy in pair:
            copy.wait()
        fine = iota((rows, LANES), 1) - first
        wanted = (fine >= 0) & (fine < 3)
        total = jnp.zeros((rows, LANES), jnp.float32)
        for level in range(levels):
            for buf, shift in ((old_buf, 0), (src_buf, SOURCE_AT)):
                value = jnp.where(wanted, buf[at, level], 0.0)
                turn = (LANES + STRIDE * level + shift - first) & (LANES - 1)
                total = total + pltpu.roll(value, turn, 1)
        out[...] = total
        out[: part.shape[0], :] += part


def sum_rows(ref):
    count = ref.shape[0] // RATIO
    first, second, third = (ref[pl.ds(at, count, RATIO), :] for at in range(RATIO))
    return first + second + third


def inner_substep(coefs, here, source, there):
    levels, rows, cols = here.shape
    sub = iota((8, cols), 0)
    tiles = rows // 8

    def one_level(level):
        ch = coefs[0, level]
        cv = coefs[1, level]
        centre = 1.0 - 4.0 * ch - 2.0 * cv
        below = jnp.maximum(level - 1, 0)
        above = jnp.minimum(level + 1, levels - 1)
        cv_below = jnp.where(level > 0, cv, 0.0)
        cv_above = jnp.where(level < levels - 1, cv, 0.0)

        def row_tile(t):
            t = t % tiles
            return here[level, 8 * t : 8 * t + 8, :]

        down_before = pltpu.roll(row_tile(-1), 1, 0)
        now = row_tile(0)
        up_now = pltpu.roll(now, 7, 0)
        for t in range(tiles):
            following = row_tile(t + 1)
            down_now = pltpu.roll(now, 1, 0)
            up_next = pltpu.roll(following, 7, 0)
            around = jnp.where(sub == 0, down_before, down_now) + jnp.where(
                sub == 7, up_next, up_now
            )
            around = around + (pltpu.roll(now, 1, 1) + pltpu.roll(now, cols - 1, 1))
            span = slice(8 * t, 8 * t + 8)
            stacked = cv_below * here[below, span, :] + cv_above * here[above, span, :]
            there[level, span, :] = centre * now + ch * around + (stacked + source[level, span, :])
            down_before, now, up_now = down_now, following, up_next

    def two_levels(pair, carry):
        one_level(2 * pair)
        one_level(2 * pair + 1)
        return carry

    lax.fori_loop(0, levels // 2, two_levels, 0)


def spread_coefs(parent_coefs, coefs, out):
    levels = out.shape[2]
    lane = iota((levels, LANES), 1)
    row = iota((levels, LANES), 0)
    for at, ref in enumerate((parent_coefs, coefs)):
        for which in range(2):
            packed = jnp.full(lane.shape, ref[which, 0], jnp.float32)
            rows = packed
            for level in range(1, levels):
                packed = jnp.where(lane >= STRIDE * level, ref[which, level], packed)
                rows = jnp.where(row == level, ref[which, level], rows)
            out[0, 2 * at + which] = packed
            out[1, 2 * at + which] = rows


def inner_first(
    band,
    oy_ref,
    parent_coefs,
    coefs,
    nest,
    source,
    parent,
    parent_source,
    strip,
    first,
    spread,
    oy_rows,
):
    oy = oy_ref[0]
    oy_rows[...] = jnp.full(oy_rows.shape, oy, jnp.int32)
    spread_coefs(parent_coefs, coefs, spread)
    strip[...] = edge_strip(lax.axis_index("gy"), band, oy, parent, parent_source)
    inner_substep(coefs, nest, source, first)


def inner_rest(coefs, nest, first, source, after_pack, third, packs, sums, second, split):
    levels, rows, cols = nest.shape
    lane = iota((rows, LANES), 1)
    for at, ref in enumerate((nest, source)):
        left = jnp.zeros(lane.shape, jnp.float32)
        right = jnp.zeros(lane.shape, jnp.float32)
        for level in range(levels):
            value = jnp.where(lane < RIGHT_OWN, tile(ref, level, 0), 0.0)
            left = left + turned(value, STRIDE * level + LEFT_AT)
            value = jnp.where(lane >= LANES - RIGHT_OWN, tile(ref, level, cols // LANES - 1), 0.0)
            right = right + turned(value, STRIDE * level + RIGHT_OWN)
        packs[2 * at] = left
        packs[2 * at + 1] = right
    inner_substep(coefs, first, source, second)
    inner_substep(coefs, second, source, third)
    for level in range(levels):
        for piece in range(cols // LANES):
            split[piece, level * rows : (level + 1) * rows, :] = tile(third, level, piece)
    for piece in range(cols // LANES):
        sums[piece] = sum_rows(split.at[piece])


def with_columns(tiles, left, right, me, parts, place):
    lane = iota(left.shape, 1)
    from_right = turned(right, -place)
    from_left = turned(left, -3 - place)
    if parts == 2:
        tiles[0] = jnp.where((lane < 3) & (me == 0), from_right, tiles[0])
        tiles[-1] = jnp.where((lane >= LANES - 3) & (me == 1), from_left, tiles[-1])
        return tiles
    extra = jnp.where(lane < 3, from_right, jnp.where(lane >= LANES - 3, from_left, 0.0))
    return tiles + [extra]


def pack_rows(
    parts, old_top, old_end, src_top, src_end, par_top, par_end, own_strip, oy_rows, *rest
):
    columns = rest[: parts - 1]
    across, within, far, strip_out, both = rest[parts - 1 :]
    core = lax.axis_index("gz")
    up, down = both.at[core], both.at[1 - core]
    levels, _, cols = old_top.shape
    me = lax.axis_index("gy")
    left, right = columns[0], columns[-1]
    rows = left.shape[0]
    strip_rows = own_strip.shape[0]
    lane = iota((strip_rows, LANES), 1)
    strips = own_strip[...]
    if parts == 2:
        oy = jnp.concatenate([oy_rows[...]] * (strip_rows // 8), axis=0)
        strips = strips + across_border(left[:strip_rows, :], oy, par_top.shape[2], me)
    else:
        for message in columns:
            strips = strips + message[:strip_rows, :]
    c = lane & (STRIDE - 1)
    strips = jnp.where(c >= STRIP_AT, strips, 0.0)
    strips = jnp.where(c == PARENT_AT, left[:strip_rows, :], strips)
    strips = jnp.where(c == PARENT_AT + 1, turned(right[:strip_rows, :], 1), strips)
    strip_out[...] = strips
    far[...] = strips[:8]
    pieces = cols // LANES
    for out, old, src, first, at, src_at in (
        (up, old_end, src_end, rows - 8, 5, 6),
        (down, old_top, src_top, 0, 0, 0),
    ):
        y_left = left[first : first + 8, :]
        y_right = right[first : first + 8, :]
        for level in range(levels):
            for ref, shift, row, count, base in (
                (old, 0, at, 3, 0),
                (src, SOURCE_AT, src_at, 2, SOURCE_ROW),
            ):
                tiles = [tile(ref, level, piece) for piece in range(pieces)]
                tiles = with_columns(
                    tiles, y_left, y_right, me, parts, STRIDE * level + shift
                )
                for piece, value in enumerate(tiles):
                    out[
                        base + count * level : base + count * (level + 1),
                        piece * LANES : (piece + 1) * LANES,
                    ] = value[row : row + count]
    parent_cols = par_top.shape[2]
    for level in range(levels):
        up[TAIL_ROW + level : TAIL_ROW + level + 1, :parent_cols] = par_end[level, 7:8, :]
        down[TAIL_ROW + level : TAIL_ROW + level + 1, :parent_cols] = par_top[level, 0:1, :]
    up[TAIL_ROW : TAIL_ROW + 8, parent_cols : parent_cols + LANES] = strips[strip_rows - 8 :]
    down[TAIL_ROW : TAIL_ROW + 8, parent_cols : parent_cols + LANES] = strips[:8]
    down[TAIL_ROW + 8 : TAIL_ROW + 16, :LANES] = strips[8:16]
    down[TAIL_ROW + 8 : TAIL_ROW + 16, LANES : 2 * LANES] = strips[16:24]
    within[...] = both[0]
    across[...] = both[1]


def edges(
    parts,
    parent_cols,
    ox_ref,
    spread,
    nest,
    source,
    sums,
    packs,
    strips,
    across,
    within,
    far,
    y_left,
    y_right,
    sides,
    windows,
    coarse_out,
    far_out,
    both,
    ping,
    pong,
    src,
):
    levels, rows, cols = nest.shape
    width = ping.shape[3]
    pieces = cols // LANES
    me = lax.axis_index("gy")
    core = lax.axis_index("gz")
    both[0] = within[...]
    both[1] = across[...]
    before, after = both.at[1 - core], both.at[core]
    is_south = me == 0
    is_north = me == parts - 1

    far_out[...] = far[...]
    sub = iota((8, LANES), 0)
    old = jnp.concatenate(
        [
            strips[...],
            after[TAIL_ROW : TAIL_ROW + 8, parent_cols : parent_cols + LANES],
            after[TAIL_ROW + 8 : TAIL_ROW + 16, :LANES],
            after[TAIL_ROW + 8 : TAIL_ROW + 16, LANES : 2 * LANES],
            jnp.where(
                sub == 7,
                before[TAIL_ROW : TAIL_ROW + 8, parent_cols : parent_cols + LANES],
                0.0,
            ),
        ],
        axis=0,
    )
    count = old.shape[0]

    def packed_coef(which, height):
        return jnp.concatenate([spread[0, which]] * (height // 8), axis=0)

    def stacked(value):
        lane = iota(value.shape, 1)
        below = jnp.where(lane >= STRIDE, turned(value, STRIDE), 0.0)
        return below + jnp.where(lane < STRIDE * (levels - 1), turned(value, -STRIDE), 0.0)

    def around(value):
        return (
            pltpu.roll(value, 1, 0)
            + pltpu.roll(value, value.shape[0] - 1, 0)
            + turned(value, 1)
            + turned(value, -1)
        )

    diff = (
        packed_coef(0, count) * (around(old) - 4.0 * old)
        + packed_coef(1, count) * (stacked(old) - 2.0 * old)
        + turned(old, STRIP_AT - STRIP_SOURCE_AT)
    )
    index = iota((rows + 16, count), 0)
    nest_row = jnp.where(index < rows, index, jnp.where(index < rows + 8, index - rows - 3, index - 13))
    parent_row = ((nest_row + 3) * 171 >> 9) - 1 + ox_ref[0]
    pick = (iota((rows + 16, count), 1) == parent_row).astype(jnp.float32)
    picked = jnp.dot(
        pick,
        jnp.concatenate([old, diff], axis=1),
        precision=HIGHEST,
        preferred_element_type=jnp.float32,
    )
    picked_old, picked_diff = picked[:, :LANES], picked[:, LANES:]

    lane = iota((rows, LANES), 1)
    c = lane & (STRIDE - 1)
    rim_first = jnp.where(is_south, LEFT_AT, RIGHT_OWN - RIM)
    in_rim = (c >= rim_first) & (c < rim_first + RIM)
    at = lane - c + STRIP_AT + jnp.where(c >= rim_first + 3, 2, 1)
    rim_old = jnp.take_along_axis(picked_old[:rows], at, axis=1)
    rim_diff = jnp.take_along_axis(picked_diff[:rows], at, axis=1)
    ch = packed_coef(2, rows)
    cv = packed_coef(3, rows)
    centre = 1.0 - 4.0 * ch - 2.0 * cv
    left = jnp.where(c < 3, y_left[...], packs[0])
    left_src = jnp.where(c < 3, turned(y_left[...], -SOURCE_AT), packs[2])
    right = jnp.where(c >= RIGHT_OWN, turned(y_right[...], RIGHT_OWN), packs[1])
    right_src = jnp.where(c >= RIGHT_OWN, turned(y_right[...], RIGHT_OWN - SOURCE_AT), packs[3])
    for side, (value, forcing, rim) in enumerate(
        (
            (left, left_src, in_rim & is_south),
            (right, right_src, in_rim & is_north),
        )
    ):
        for substep in range(1, SUBSTEPS + 1):
            value = centre * value + ch * around(value) + (cv * stacked(value) + forcing)
            value = jnp.where(rim, rim_old + (substep / SUBSTEPS) * rim_diff, value)
        sides[side] = value

    sub = iota((8, width), 0)
    lane = iota((8, LANES), 1)
    for level in range(levels):
        for buf, field, shift, n, base in (
            (ping, nest, 0, 3, 0),
            (src, source, SOURCE_AT, 2, SOURCE_ROW),
        ):
            for window, first, turn, at, message in (
                (0, 0, 3, 3 - n, before),
                (1, rows - 8, 5, 5, after),
            ):
                tiles = [
                    field[level, first : first + 8, piece * LANES : (piece + 1) * LANES]
                    for piece in range(pieces)
                ]
                tiles = with_columns(
                    tiles,
                    y_left[first : first + 8, :],
                    y_right[first : first + 8, :],
                    me,
                    parts,
                    STRIDE * level + shift,
                )
                for piece, value in enumerate(tiles):
                    value = pltpu.roll(value, turn, 0)
                    span = slice(piece * LANES, (piece + 1) * LANES)
                    buf[level, window, :, span] = value
                    if n == 3:
                        pong[level, window, :, span] = value
                buf[level, window, at : at + n, :] = message[
                    base + n * level : base + n * (level + 1), :
                ]
    rim_first = jnp.where(is_south, 0, LANES - RIM)
    column = STRIP_AT + jnp.where((lane >= rim_first + 3) & (lane < rim_first + RIM), 2, 1)
    rims = {}
    for level in range(levels):
        for window in range(2):
            span = slice(rows + 8 * window, rows + 8 * window + 8)
            at = column + STRIDE * level
            rims[level, window] = (
                jnp.take_along_axis(picked_old[span], at, axis=1),
                jnp.take_along_axis(picked_diff[span], at, axis=1),
            )
    for substep in range(1, SUBSTEPS + 1):
        here, there = (ping, pong) if substep % 2 else (pong, ping)
        there = windows if substep == SUBSTEPS else there
        low = 0 if substep == SUBSTEPS or parts > 2 else 3
        south = (lane >= low) & (lane < RIM) & is_south
        north = (lane >= LANES - RIM) & (lane < LANES - low) & is_north
        weight = substep / SUBSTEPS
        for level in range(levels):
            c_h, c_v = (
                jnp.concatenate([spread[1, which, level : level + 1, :]] * (width // LANES), axis=1)
                for which in (2, 3)
            )
            c_0 = 1.0 - 4.0 * c_h - 2.0 * c_v
            for window in range(2):
                now = here[level, window]
                up = pltpu.roll(now, 1, 0)
                down = pltpu.roll(now, 7, 0)
                if substep == 1:
                    beyond_row = pong[level, window]
                    if window == 0:
                        down = jnp.where(sub == 7, pltpu.roll(beyond_row, 7, 0), down)
                    else:
                        up = jnp.where(sub == 0, pltpu.roll(beyond_row, 1, 0), up)
                beside = pltpu.roll(now, 1, 1) + pltpu.roll(now, width - 1, 1)
                value = c_0 * now + c_h * ((up + down) + beside) + src[level, window]
                if level > 0:
                    value = value + c_v * here[level - 1, window]
                if level < levels - 1:
                    value = value + c_v * here[level + 1, window]
                rim_o, rim_d = rims[level, window]
                rim = rim_o + weight * rim_d
                for piece in range(width // LANES):
                    span = slice(piece * LANES, (piece + 1) * LANES)
                    part = value[:, span]
                    if piece == 0:
                        part = jnp.where(south, rim, part)
                    if piece == pieces - 1:
                        part = jnp.where(north, rim, part)
                    there[level, window, :, span] = part

    parent_rows = rows // RATIO
    lane = iota((parent_rows, LANES), 1)
    row = iota((parent_rows, LANES), 0)
    side_sums = [sum_rows(sides.at[side]) for side in range(2)]
    replaced = [[] for _ in range(pieces)]
    for level in range(levels):
        span = slice(level * parent_rows, (level + 1) * parent_rows)
        top = windows[level, 0, 3:4, :] + windows[level, 0, 4:5, :] + windows[level, 0, 5:6, :]
        end = windows[level, 1, 2:3, :] + windows[level, 1, 3:4, :] + windows[level, 1, 4:5, :]
        for piece in range(pieces):
            value = sums[piece, span, :]
            if piece == 0:
                fixed = turned(side_sums[0], -STRIDE * level - LEFT_AT)
                value = jnp.where(lane < FIXED, fixed, value)
            if piece == pieces - 1:
                fixed = turned(side_sums[1], -STRIDE * level - RIGHT_OWN)
                value = jnp.where(lane >= LANES - FIXED, fixed, value)
            across_piece = slice(piece * LANES, (piece + 1) * LANES)
            value = jnp.where(row == 0, top[:, across_piece], value)
            value = jnp.where(row == parent_rows - 1, end[:, across_piece], value)
            replaced[piece].append(value)
    foot = cols // RATIO
    offset = iota((cols, foot), 0) - RATIO * iota((cols, foot), 1)
    gather = ((offset >= 0) & (offset < RATIO)).astype(jnp.float32)
    means = jnp.dot(
        jnp.concatenate([jnp.concatenate(values, axis=0) for values in replaced], axis=1),
        gather,
        precision=HIGHEST,
        preferred_element_type=jnp.float32,
    ) * (1.0 / 9.0)
    coarse_out[...] = means.reshape(coarse_out.shape)


def put_together(third, sides, windows, result):
    levels, rows, cols = third.shape
    pieces = cols // LANES
    lane = iota((rows, LANES), 1)
    sub = iota((8, cols), 0)
    for level in range(levels):
        fixed = turned(sides[0], -STRIDE * level - LEFT_AT)
        result[level, :, :LANES] = jnp.where(lane < FIXED, fixed, tile(third, level, 0))
        for piece in range(1, pieces - 1):
            result[level, :, piece * LANES : (piece + 1) * LANES] = tile(third, level, piece)
        fixed = turned(sides[1], -STRIDE * level - RIGHT_OWN)
        result[level, :, cols - LANES :] = jnp.where(
            lane >= LANES - FIXED, fixed, tile(third, level, pieces - 1)
        )
        top = pltpu.roll(windows[level, 0, :, :cols], 5, 0)
        result[level, :8, :] = jnp.where(sub < 3, top, result[level, :8, :])
        end = pltpu.roll(windows[level, 1, :, :cols], 3, 0)
        result[level, rows - 8 :, :] = jnp.where(sub >= 5, end, result[level, rows - 8 :, :])


def parent_step(
    parts,
    band,
    ox_ref,
    oy_ref,
    spread,
    third,
    sides,
    windows,
    parent,
    source,
    within,
    across,
    y_left,
    y_right,
    out,
    nest_out,
    late,
    tail,
    result,
    sem,
):
    put_together(third, sides, windows, result)
    store = pltpu.make_async_copy(result, nest_out, sem)
    store.start()
    core = lax.axis_index("gz")
    levels, rows, cols = parent.shape
    tail[0] = within[TAIL_ROW : TAIL_ROW + levels, : cols + LANES]
    tail[1] = across[TAIL_ROW : TAIL_ROW + levels, : cols + LANES]
    me = lax.axis_index("gy")
    is_last = ox_ref[0] == rows - 1
    wide = iota((1, cols), 1)
    south = (wide == oy_ref[0] + 2 - me * cols) & is_last
    north = (wide == oy_ref[0] + band - 3 - me * cols) & is_last
    row = iota((rows, cols), 0)
    lane = iota((rows, cols), 1)
    has_left = me > 0
    has_right = me < parts - 1
    left = y_left[:rows, :]
    right = y_right[:rows, :]
    zero = jnp.zeros((rows, cols), jnp.float32)
    for level in range(levels):
        now = parent[level]
        at = STRIDE * level + PARENT_AT
        from_left = left[:, at : at + 1]
        from_right = right[:, at : at + 1]
        top = tail[1 - core, level : level + 1, :cols]
        end = tail[core, level : level + 1, :cols]
        around = (
            jnp.where(row == 0, top, pltpu.roll(now, 1, 0))
            + jnp.where(row == rows - 1, end, pltpu.roll(now, rows - 1, 0))
            + jnp.where(
                lane == 0, jnp.where(has_left, from_left, 0.0), pltpu.roll(now, 1, 1)
            )
            + jnp.where(
                lane == cols - 1,
                jnp.where(has_right, from_right, 0.0),
                pltpu.roll(now, cols - 1, 1),
            )
        )
        stacked = (parent[level - 1] if level > 0 else zero) + (
            parent[level + 1] if level < levels - 1 else zero
        )
        ch, cv = (
            jnp.concatenate([spread[1, which, level : level + 1, :]] * (cols // LANES), axis=1)
            for which in (0, 1)
        )
        out[level] = (
            (1.0 - 4.0 * ch - 2.0 * cv) * now + ch * around + (cv * stacked + source[level])
        )
        at = cols + STRIDE * level + PARENT_AT
        before_end = jnp.where(
            wide == 0, tail[core, 0:1, at : at + 1], pltpu.roll(end, 1, 1)
        )
        after_end = jnp.where(
            wide == cols - 1, tail[core, 0:1, at + 1 : at + 2], pltpu.roll(end, cols - 1, 1)
        )
        nest_ch = spread[1, 2, level : level + 1, :]
        nest_ch = jnp.concatenate([nest_ch] * (cols // LANES), axis=1)
        share = nest_ch * nest_ch * ch * (1.0 / SUBSTEPS)
        late[level : level + 1, :] = (share * (1.0 / (RATIO * RATIO))) * (
            jnp.where(south, before_end, 0.0) + jnp.where(north, after_end, 0.0)
        )
    store.wait()


def merge(parts, band, ox_ref, oy_ref, late, step, nest, spread, beyond, *rest):
    own, previous = rest[:parts], rest[parts : 2 * parts]
    out, nest_out, joined, corner, sem = rest[2 * parts :]
    levels, rows, cols = step.shape
    foot = own[0].shape[2]
    me = lax.axis_index("gy")

    @pl.when((ox_ref[0] == rows - 1) & ((me == 0) | (me == parts - 1)))
    def _():
        nest_rows, nest_cols = nest.shape[1:]
        first = pl.multiple_of(jnp.where(me == 0, 0, nest_cols - LANES), LANES)
        place = (slice(None), pl.ds(nest_rows - 8, 8), pl.ds(first, LANES))
        load = pltpu.make_async_copy(nest_out.at[place], corner, sem)
        load.start()
        load.wait()
        sub = iota((8, LANES), 0)
        lane = iota((8, LANES), 1)
        cell = (sub == 7) & (lane == jnp.where(me == 0, RIM, LANES - RIM - 1))
        for level in range(levels):
            at = STRIDE * level + STRIP_AT
            value = jnp.where(me == 0, beyond[0:1, at + 2 : at + 3], beyond[0:1, at + 1 : at + 2])
            nest_ch = spread[1, 2, level : level + 1, :]
            share = nest_ch * nest_ch * spread[1, 0, level : level + 1, :] * (1.0 / SUBSTEPS)
            corner[level] += jnp.where(cell, share * value, 0.0)
        again = pltpu.make_async_copy(corner, nest_out.at[place], sem)
        again.start()
        again.wait()

    ox = ox_ref[0]
    oy = oy_ref[0]
    for k in range(parts):
        joined[k, :, :rows, :] = previous[k][...]
        joined[k, :, rows:, :] = own[k][...]
    lane = iota((rows, LANES), 1)
    row = iota((rows, LANES), 0)
    for level in range(levels):
        values = [tile(step, level, piece) for piece in range(cols // LANES)]
        for k in range(parts):
            source = lax.rem(me + parts - k, parts)
            block = joined[k, level, pl.ds(rows - ox, rows), :]
            begin = oy + source * foot - me * cols
            block = pltpu.roll(block, (16384 + begin) & (LANES - 1), 1)
            low = jnp.maximum(source * foot, 2)
            high = jnp.minimum((source + 1) * foot, band - 2)
            for piece in range(cols // LANES):
                at = lane + (piece * LANES + me * cols - oy)
                values[piece] = jnp.where((at >= low) & (at < high), block, values[piece])
        for piece, value in enumerate(values):
            term = late[level : level + 1, piece * LANES : (piece + 1) * LANES]
            value = value + jnp.where(row == rows - 2, term, 0.0)
            out[level, :, piece * LANES : (piece + 1) * LANES] = value


def shifted(value, axis, steps):
    count = lax.axis_size(axis)
    pairs = [(source, (source + steps) % count) for source in range(count)]
    return lax.ppermute(value, axis, pairs)


def shards(
    parent_old, parent_source, parent_coefs, nest_old, nest_source, nest_coefs, offset_x, offset_y
):
    parts = lax.axis_size("gy")
    along = ("gx", "gz")
    levels, parent_rows, parent_cols = parent_old.shape
    _, rows, cols = nest_old.shape
    foot = cols // RATIO
    band = foot * parts
    width = cols if parts == 2 else cols + LANES
    height = TAIL_ROW + 16
    f32 = jnp.float32
    shape = jax.ShapeDtypeStruct
    anywhere = pl.BlockSpec(memory_space=pl.ANY)
    in_hbm = pl.BlockSpec(memory_space=pltpu.HBM)
    sides = 1 if parts == 2 else 2
    if parts == 2:
        packed = [
            pl.pallas_call(
                pack_pair,
                out_shape=VMEM((rows, LANES), f32),
                in_specs=[in_hbm] * 4,
                out_specs=whole(),
                scratch_shapes=[
                    VMEM((2, levels, rows, LANES), f32),
                    VMEM((2, levels, parent_rows, LANES), f32),
                    pltpu.SemaphoreType.DMA((4,)),
                ],
                compiler_params=params(MOST),
                cost_estimate=cost(200000, 800000),
                name="pack_pair",
            )(nest_old, nest_source, parent_old, parent_source)
        ]
    else:
        packed = pl.pallas_call(
            functools.partial(pack_columns, parts, band),
            out_shape=[
                shape((rows if k in (1, parts - 1) else parent_rows, LANES), f32)
                for k in range(1, parts)
            ],
            in_specs=[in_hbm] * 5,
            out_specs=[whole()] * (parts - 1),
            scratch_shapes=[
                VMEM((sides, levels, rows, LANES), f32),
                VMEM((sides, levels, rows, LANES), f32),
                VMEM(parent_old.shape, f32),
                VMEM(parent_old.shape, f32),
                pltpu.SMEM(offset_y.shape, jnp.int32),
                pltpu.SemaphoreType.DMA((sides, 2)),
                pltpu.SemaphoreType.DMA((3,)),
            ],
            compiler_params=params(MOST),
            cost_estimate=cost(200000, 1000000),
            name="pack_columns",
        )(offset_y, nest_old, nest_source, parent_old, parent_source)
    columns = [shifted(packed[k - 1], "gy", k) for k in range(1, parts)]
    own_strip, first, spread, oy_rows = pl.pallas_call(
        functools.partial(inner_first, band),
        out_shape=[
            shape((parent_rows, LANES), f32),
            shape(nest_old.shape, f32),
            shape((2, 4, levels, LANES), f32),
            shape((8, LANES), jnp.int32),
        ],
        in_specs=[scalars()] * 3 + [whole()] * 4,
        out_specs=[whole()] * 4,
        compiler_params=params(),
        cost_estimate=cost(4000000, 3000000),
        name="inner_first",
    )(
        offset_y,
        parent_coefs,
        nest_coefs,
        nest_old,
        nest_source,
        parent_old,
        parent_source,
    )

    def block(ref, last):
        count = ref.shape[1] // 8 - 1 if last else 0
        return pl.BlockSpec((levels, 8, ref.shape[2]), lambda i, c=count: (0, c, 0))

    def full(extent):
        return pl.BlockSpec(extent, lambda i: (0,) * len(extent))

    outs = [
        shape((height, width), f32),
        shape((height, width), f32),
        shape((8, LANES), f32),
        shape((parent_rows, LANES), f32),
    ]
    across, within, far, strips = pl.pallas_call(
        functools.partial(pack_rows, parts),
        out_shape=outs,
        grid=(1,),
        in_specs=[
            block(nest_old, False),
            block(nest_old, True),
            block(nest_old, False),
            block(nest_old, True),
            block(parent_old, False),
            block(parent_old, True),
            full(own_strip.shape),
            full(oy_rows.shape),
        ]
        + [full(message.shape) for message in columns],
        out_specs=[full(out.shape) for out in outs],
        scratch_shapes=[VMEM((2, height, width), f32)],
        compiler_params=params(),
        cost_estimate=cost(100000, 700000),
        name="pack_rows",
    )(nest_old, nest_old, nest_source, nest_source, parent_old, parent_old, own_strip, oy_rows, *columns)
    across = swapped(across, 1)
    within = swapped(within, 0)
    third, packs, sums = pl.pallas_call(
        inner_rest,
        out_shape=[
            shape(nest_old.shape, f32),
            shape((4, rows, LANES), f32),
            shape((cols // LANES, levels * parent_rows, LANES), f32),
        ],
        in_specs=[scalars()] + [whole()] * 3 + [anywhere],
        out_specs=[whole()] * 3,
        scratch_shapes=[
            VMEM(nest_old.shape, f32),
            VMEM((cols // LANES, levels * rows, LANES), f32),
        ],
        compiler_params=params(),
        cost_estimate=cost(8000000, 6000000),
        name="inner_rest",
    )(nest_coefs, nest_old, first, nest_source, strips)
    sides, windows, coarse, far = pl.pallas_call(
        functools.partial(edges, parts, parent_cols),
        out_shape=[
            shape((2, rows, LANES), f32),
            shape((levels, 2, 8, width), f32),
            shape((levels, parent_rows, foot), f32),
            shape((8, LANES), f32),
        ],
        in_specs=[scalars()] + [whole()] * 11,
        out_specs=[whole()] * 4,
        scratch_shapes=[
            VMEM((2, height, width), f32),
            VMEM((levels, 2, 8, width), f32),
            VMEM((levels, 2, 8, width), f32),
            VMEM((levels, 2, 8, width), f32),
        ],
        compiler_params=params(),
        cost_estimate=cost(4000000, 3000000),
        name="edges",
    )(
        offset_x,
        spread,
        nest_old,
        nest_source,
        sums,
        packs,
        strips,
        across,
        within,
        far,
        columns[0],
        columns[-1],
    )
    previous = [shifted(coarse, along, 1)] + [
        shifted_both(coarse, k) for k in range(1, parts)
    ]
    own = [coarse] + [shifted(coarse, "gy", k) for k in range(1, parts)]
    beyond = shifted(far, along, -2)
    step, nest_stored, late = pl.pallas_call(
        functools.partial(parent_step, parts, band),
        out_shape=[
            shape(parent_old.shape, f32),
            shape(nest_old.shape, f32),
            shape((levels, parent_cols), f32),
        ],
        in_specs=[scalars()] * 2 + [whole()] * 10,
        out_specs=[whole(), in_hbm, whole()],
        scratch_shapes=[
            VMEM((2, levels, parent_cols + LANES), f32),
            VMEM(nest_old.shape, f32),
            pltpu.SemaphoreType.DMA,
        ],
        compiler_params=params(),
        cost_estimate=cost(800000, 2500000),
        name="parent_step",
    )(
        offset_x,
        offset_y,
        spread,
        third,
        sides,
        windows,
        parent_old,
        parent_source,
        within,
        across,
        columns[0],
        columns[-1],
    )
    parent_new, nest_new = pl.pallas_call(
        functools.partial(merge, parts, band),
        out_shape=[shape(parent_old.shape, f32), shape(nest_old.shape, f32)],
        in_specs=[scalars()] * 2 + [whole()] * 2 + [in_hbm] + [whole()] * (2 + 2 * parts),
        out_specs=[whole(), in_hbm],
        scratch_shapes=[
            VMEM((parts, levels, 2 * parent_rows, foot), f32),
            VMEM((levels, 8, LANES), f32),
            pltpu.SemaphoreType.DMA,
        ],
        input_output_aliases={4: 1},
        compiler_params=params(),
        cost_estimate=cost(200000, 800000),
        name="merge",
    )(offset_x, offset_y, late, step, nest_stored, spread, beyond, *own, *previous)
    return (parent_new, nest_new)


def swapped(value, first):
    along = ("gx", "gz")
    count = lax.axis_size(along)
    pairs = []
    for at in range(first, count, 2):
        pairs += [(at, (at + 1) % count), ((at + 1) % count, at)]
    return lax.ppermute(value, along, pairs)


def shifted_both(value, steps):
    sizes = [lax.axis_size(axis) for axis in ("gx", "gy", "gz")]
    gx, gy, gz = sizes
    pairs = []
    for x in range(gx):
        for y in range(gy):
            for z in range(gz):
                place = (x * gz + z + 1) % (gx * gz)
                target = (place // gz * gy + (y + steps) % gy) * gz + place % gz
                pairs.append(((x * gy + y) * gz + z, target))
    return lax.ppermute(value, ("gx", "gy", "gz"), pairs)


def solution(mesh):
    return jax.shard_map(
        shards,
        mesh=mesh,
        in_specs=(
            P(None, ("grp", "gx", "gz"), "gy"),
            P(None, ("grp", "gx", "gz"), "gy"),
            P(),
            P(None, ("grp", "gx", "gz"), "gy"),
            P(None, ("grp", "gx", "gz"), "gy"),
            P(),
            P("grp"),
            P("grp"),
        ),
        out_specs=(P(None, ("grp", "gx", "gz"), "gy"), P(None, ("grp", "gx", "gz"), "gy")),
        check_vma=False,
    )
```

profile of v0, /device:TPU:0, one launch (start us, length us, event | category | flops | bytes accessed | tf_op | source)
XLA Modules:
  0.0 24.5 jit_solution(10751167460462639519)
XLA Ops:
  0.6 0.0 copy-start.1
  0.6 0.0 copy-start
  0.7 0.0 copy-start.2
  0.7 0.0 copy-start.3
  0.7 0.0 copy-start.5
  0.7 1.6 %pack_pair.1 = f32[72,128]{1,0:T(8,128)S(1)} custom-call(f32[8,72,384]{2,1,0:T(8,128)} %nest.7, f32[8,72,384]{2,1,0:T(8,128)} %source.8, f32[8,24,256]{2,1,0:T(8,128)} %parent.5, f32[8,24,256]{2,1,0:T(8,128)} %source.9), custom_call_target="tpu_custom_call" | custom-call | flops 200000 | bytes 800000 | tf_op jit(solution)/shard_map/pack_pair/pallas_call | solution.py:779
  2.2 0.0 copy-start.4
  2.3 3.0 %collective-permute-start = (f32[72,128]{1,0:T(8,128)S(1)}, f32[72,128]{1,0:T(8,128)S(1)}, u32[]{:S(2)}, u32[]{:S(2)}) collective-permute-start(f32[72,128]{1,0:T(8,128)S(1)} %pack_pair.1), channel_id=1, source_target_pairs={{0,2},{2,0},{1,3},{3,1},{4,6},{6,4},{5,7},{7,5},{8,10},{10,8},{9,1... | collective-permute-start | bytes 110600 | tf_op jit(solution)/shard_map/ppermute | solution.py:758
  5.9 0.0 copy-done.1
  5.9 0.0 copy-done
  5.9 0.0 copy-done.2
  5.9 0.0 copy-done.3
  6.0 0.0 copy-done.5
  6.0 0.0 copy-done.4
  6.0 1.5 %inner_first.1 = (f32[24,128]{1,0:T(8,128)S(1)}, f32[8,72,384]{2,1,0:T(8,128)S(1)}, f32[2,4,8,128]{3,2,1,0:T(8,128)S(1)}, s32[8,128]{1,0:T(8,128)S(1)}) custom-call(s32[1]{0:T(128)S(6)} %copy.13.oy_ref, f32[2,8]{1,0:T(2,128)S(1)} %copy-done.5, f32[2,8]{1,0:T(2,128)S(1)} %copy-done.4, f32[8,72,384]{2,1,0:T(8,128)S(1)} %copy-done, ...), custom_call_target="tpu_custom_call" | custom-call | flops 4000000 | bytes 3000000 | tf_op jit(solution)/shard_map/inner_first/pallas_call | solution.py:817
  7.5 0.0 collective-permute-done.rest_0_.y_left.y_right
  7.5 0.1 pack_rows.1
  7.7 2.8 %collective-permute-start.1 = (f32[56,384]{1,0:T(8,128)S(1)}, f32[56,384]{1,0:T(8,128)S(1)}, u32[]{:S(2)}, u32[]{:S(2)}) collective-permute-start(f32[56,384]{1,0:T(8,128)S(1)} %get-tuple-element.28), channel_id=1, source_target_pairs={{1,4},{4,1},{5,8},{8,5},{9,12},{12,9},{13,0},{0,13},{3,6},{6,3},{7... | collective-permute-start | bytes 258056 | tf_op jit(solution)/shard_map/ppermute | solution.py:986
  10.5 0.0 collective-permute-start.2
  11.1 2.7 %inner_rest.1 = (f32[8,72,384]{2,1,0:T(8,128)S(1)}, f32[4,72,128]{2,1,0:T(8,128)S(1)}, f32[3,192,128]{2,1,0:T(8,128)S(1)}) custom-call(f32[2,8]{1,0:T(2,128)S(1)} %copy-done.4, f32[8,72,384]{2,1,0:T(8,128)S(1)} %copy-done, f32[8,72,384]{2,1,0:T(8,128)S(1)} %get-tuple-element.21.first, f32[8,72,384]{2,1,0:T(8,128)S(1)} %copy-done.1, ...), custom_call_target="tpu_custom_call" | custom-call | flops 8000000 | bytes 6000000 | tf_op jit(solution)/shard_map/inner_rest/pallas_call | solution.py:876
  13.8 0.0 collective-permute-done.1.across
  13.8 0.0 collective-permute-done.2.within
  13.8 1.4 %edges.1 = (f32[2,72,128]{2,1,0:T(8,128)S(1)}, f32[8,2,8,384]{3,2,1,0:T(8,128)S(1)}, f32[8,24,128]{2,1,0:T(8,128)S(1)}, f32[8,128]{1,0:T(8,128)S(1)}) custom-call(s32[1]{0:T(128)S(6)} %copy.12.ox_ref, f32[2,4,8,128]{3,2,1,0:T(8,128)S(1)} %get-tuple-element.20.spread, f32[8,72,384]{2,1,0:T(8,128)S(1)} %copy-done, f32[8,72,384]{2,1,0:T(8,128)S(1)} %copy-done.1, ...), custom_call_target="tpu_custom_call" | custom-call | flops 4000000 | bytes 3000000 | tf_op jit(solution)/shard_map/edges/pallas_call | solution.py:893
  15.3 1.0 %collective-permute-start.6 = (f32[8,24,128]{2,1,0:T(8,128)S(1)}, f32[8,24,128]{2,1,0:T(8,128)S(1)}, u32[]{:S(2)}, u32[]{:S(2)}) collective-permute-start(f32[8,24,128]{2,1,0:T(8,128)S(1)} %get-tuple-element.37.rest_0_), channel_id=1, source_target_pairs={{0,3},{1,6},{2,1},{3,4},{4,7},{5,10},{6,5},{7,8},{8,11},{9,14},{10... | collective-permute-start | bytes 294920 | tf_op jit(solution)/shard_map/ppermute | solution.py:999
  16.3 0.8 %collective-permute-start.5 = (f32[8,24,128]{2,1,0:T(8,128)S(1)}, f32[8,24,128]{2,1,0:T(8,128)S(1)}, u32[]{:S(2)}, u32[]{:S(2)}) collective-permute-start(f32[8,24,128]{2,1,0:T(8,128)S(1)} %get-tuple-element.37.rest_0_), channel_id=1, source_target_pairs={{0,1},{1,4},{4,5},{5,8},{8,9},{9,12},{12,13},{13,0},{2,3},{3,6},{6... | collective-permute-start | bytes 294920 | tf_op jit(solution)/shard_map/ppermute | solution.py:758
  17.1 0.5 %collective-permute-start.4 = (f32[8,24,128]{2,1,0:T(8,128)S(1)}, f32[8,24,128]{2,1,0:T(8,128)S(1)}, u32[]{:S(2)}, u32[]{:S(2)}) collective-permute-start(f32[8,24,128]{2,1,0:T(8,128)S(1)} %get-tuple-element.37.rest_0_), channel_id=1, source_target_pairs={{0,2},{2,0},{1,3},{3,1},{4,6},{6,4},{5,7},{7,5},{8,10},{10,8},{9,1... | collective-permute-start | bytes 294920 | tf_op jit(solution)/shard_map/ppermute | solution.py:758
  17.6 3.1 %collective-permute-start.3 = (f32[8,128]{1,0:T(8,128)S(1)}, f32[8,128]{1,0:T(8,128)S(1)}, u32[]{:S(2)}, u32[]{:S(2)}) collective-permute-start(f32[8,128]{1,0:T(8,128)S(1)} %get-tuple-element.36), channel_id=1, source_target_pairs={{0,12},{1,13},{4,0},{5,1},{8,4},{9,5},{12,8},{13,9},{2,14},{3,15},... | collective-permute-start | bytes 12296 | tf_op jit(solution)/shard_map/ppermute | solution.py:758
  20.8 1.4 %parent_step.1 = (f32[8,24,256]{2,1,0:T(8,128)S(1)}, f32[8,72,384]{2,1,0:T(8,128)}, f32[8,256]{1,0:T(8,128)S(1)}) custom-call(s32[1]{0:T(128)S(6)} %copy.12.ox_ref, s32[1]{0:T(128)S(6)} %copy.13.oy_ref, f32[2,4,8,128]{3,2,1,0:T(8,128)S(1)} %get-tuple-element.20.spread, f32[8,72,384]{2,1,0:T(8,128)S(1)} %get-tuple-element.25.third, ...), custom_call_target="tpu_custom_call" | custom-call | flops 800000 | bytes 2500000 | tf_op jit(solution)/shard_map/parent_step/pallas_call | solution.py:931
  22.1 0.0 collective-permute-done.3.beyond
  22.1 0.0 collective-permute-done.6.rest_3_
  22.2 1.5 %collective-permute-done.5.rest_2_ = f32[8,24,128]{2,1,0:T(8,128)S(1)} collective-permute-done((f32[8,24,128]{2,1,0:T(8,128)S(1)}, f32[8,24,128]{2,1,0:T(8,128)S(1)}, u32[]{:S(2)}, u32[]{:S(2)}) %collective-permute-start.5) | collective-permute-done | bytes 98336 | tf_op jit(solution)/shard_map/ppermute | solution.py:758
  23.7 0.0 collective-permute-done.4.rest_1_
  23.7 0.8 %merge.1 = (f32[8,24,256]{2,1,0:T(8,128)}, f32[8,72,384]{2,1,0:T(8,128)}) custom-call(s32[1]{0:T(128)S(6)} %copy.12.ox_ref, s32[1]{0:T(128)S(6)} %copy.13.oy_ref, f32[8,256]{1,0:T(8,128)S(1)} %get-tuple-element.33.late, f32[8,24,256]{2,1,0:T(8,128)S(1)} %get-tuple-element.34.step, ...), custom_call_target="tpu_custom_call", output_to_operand_aliasing={{1}: (4, {})} | custom-call | flops 200000 | bytes 800000 | tf_op jit(solution)/shard_map/merge/pallas_call | solution.py:962
Async XLA Ops:
  0.6 5.3 %copy-start.1 = (f32[8,72,384]{2,1,0:T(8,128)S(1)}, f32[8,72,384]{2,1,0:T(8,128)}, u32[]{:S(2)}) copy-start(f32[8,72,384]{2,1,0:T(8,128)} %source.8) | copy-start | bytes 2654212
  0.6 5.3 %copy-start = (f32[8,72,384]{2,1,0:T(8,128)S(1)}, f32[8,72,384]{2,1,0:T(8,128)}, u32[]{:S(2)}) copy-start(f32[8,72,384]{2,1,0:T(8,128)} %nest.7) | copy-start | bytes 2654212
  0.7 5.3 %copy-start.2 = (f32[8,24,256]{2,1,0:T(8,128)S(1)}, f32[8,24,256]{2,1,0:T(8,128)}, u32[]{:S(2)}) copy-start(f32[8,24,256]{2,1,0:T(8,128)} %parent.5) | copy-start | bytes 589828
  0.7 5.3 %copy-start.3 = (f32[8,24,256]{2,1,0:T(8,128)S(1)}, f32[8,24,256]{2,1,0:T(8,128)}, u32[]{:S(2)}) copy-start(f32[8,24,256]{2,1,0:T(8,128)} %source.9) | copy-start | bytes 589828
  0.7 5.3 %copy-start.5 = (f32[2,8]{1,0:T(2,128)S(1)}, f32[2,8]{1,0:T(2,128)}, u32[]{:S(2)}) copy-start(f32[2,8]{1,0:T(2,128)} %parent_coefs.1) | copy-start | bytes 196
  2.2 3.7 %copy-start.4 = (f32[2,8]{1,0:T(2,128)S(1)}, f32[2,8]{1,0:T(2,128)}, u32[]{:S(2)}) copy-start(f32[2,8]{1,0:T(2,128)} %coefs.3) | copy-start | bytes 196
  2.3 5.2 %collective-permute-start = (f32[72,128]{1,0:T(8,128)S(1)}, f32[72,128]{1,0:T(8,128)S(1)}, u32[]{:S(2)}, u32[]{:S(2)}) collective-permute-start(f32[72,128]{1,0:T(8,128)S(1)} %pack_pair.1), channel_id=1, source_target_pairs={{0,2},{2,0},{1,3},{3,1},{4,6},{6,4},{5,7},{7,5},{8,10},{10,8},{9,1... | collective-permute-start | bytes 110600 | tf_op jit(solution)/shard_map/ppermute | solution.py:758
  7.7 6.2 %collective-permute-start.1 = (f32[56,384]{1,0:T(8,128)S(1)}, f32[56,384]{1,0:T(8,128)S(1)}, u32[]{:S(2)}, u32[]{:S(2)}) collective-permute-start(f32[56,384]{1,0:T(8,128)S(1)} %get-tuple-element.28), channel_id=1, source_target_pairs={{1,4},{4,1},{5,8},{8,5},{9,12},{12,9},{13,0},{0,13},{3,6},{6,3},{7... | collective-permute-start | bytes 258056 | tf_op jit(solution)/shard_map/ppermute | solution.py:986
  10.5 3.4 %collective-permute-start.2 = (f32[56,384]{1,0:T(8,128)S(1)}, f32[56,384]{1,0:T(8,128)S(1)}, u32[]{:S(2)}, u32[]{:S(2)}) collective-permute-start(f32[56,384]{1,0:T(8,128)S(1)} %get-tuple-element.29), channel_id=1, source_target_pairs={{0,1},{1,0},{4,5},{5,4},{8,9},{9,8},{12,13},{13,12},{2,3},{3,2},{6... | collective-permute-start | bytes 258056 | tf_op jit(solution)/shard_map/ppermute | solution.py:986
  15.3 6.9 %collective-permute-start.6 = (f32[8,24,128]{2,1,0:T(8,128)S(1)}, f32[8,24,128]{2,1,0:T(8,128)S(1)}, u32[]{:S(2)}, u32[]{:S(2)}) collective-permute-start(f32[8,24,128]{2,1,0:T(8,128)S(1)} %get-tuple-element.37.rest_0_), channel_id=1, source_target_pairs={{0,3},{1,6},{2,1},{3,4},{4,7},{5,10},{6,5},{7,8},{8,11},{9,14},{10... | collective-permute-start | bytes 294920 | tf_op jit(solution)/shard_map/ppermute | solution.py:999
  16.3 7.4 %collective-permute-start.5 = (f32[8,24,128]{2,1,0:T(8,128)S(1)}, f32[8,24,128]{2,1,0:T(8,128)S(1)}, u32[]{:S(2)}, u32[]{:S(2)}) collective-permute-start(f32[8,24,128]{2,1,0:T(8,128)S(1)} %get-tuple-element.37.rest_0_), channel_id=1, source_target_pairs={{0,1},{1,4},{4,5},{5,8},{8,9},{9,12},{12,13},{13,0},{2,3},{3,6},{6... | collective-permute-start | bytes 294920 | tf_op jit(solution)/shard_map/ppermute | solution.py:758
  17.1 6.6 %collective-permute-start.4 = (f32[8,24,128]{2,1,0:T(8,128)S(1)}, f32[8,24,128]{2,1,0:T(8,128)S(1)}, u32[]{:S(2)}, u32[]{:S(2)}) collective-permute-start(f32[8,24,128]{2,1,0:T(8,128)S(1)} %get-tuple-element.37.rest_0_), channel_id=1, source_target_pairs={{0,2},{2,0},{1,3},{3,1},{4,6},{6,4},{5,7},{7,5},{8,10},{10,8},{9,1... | collective-permute-start | bytes 294920 | tf_op jit(solution)/shard_map/ppermute | solution.py:758
  17.6 4.5 %collective-permute-start.3 = (f32[8,128]{1,0:T(8,128)S(1)}, f32[8,128]{1,0:T(8,128)S(1)}, u32[]{:S(2)}, u32[]{:S(2)}) collective-permute-start(f32[8,128]{1,0:T(8,128)S(1)} %get-tuple-element.36), channel_id=1, source_target_pairs={{0,12},{1,13},{4,0},{5,1},{8,4},{9,5},{12,8},{13,9},{2,14},{3,15},... | collective-permute-start | bytes 12296 | tf_op jit(solution)/shard_map/ppermute | solution.py:758
where the time goes:
time: 24.7 us; the launch traced here: 24.5 us
  starting transfers between devices  11.3 us (46%)
  Pallas kernels  9.49 us (38%)
  between operations  2.09 us (8%)
  waiting for transfers between devices  1.58 us (6%)
    ppermute x4, starting transfers between devices, shifted(): return lax.ppermute(value, axis, pairs)  7.48 us
    ppermute x2, starting transfers between devices, swapped(): return lax.ppermute(value, along, pairs)  2.83 us
    pallas_call x1, Pallas kernels, shards(): pl.pallas_call(inner_rest, out_shape=[shape(nest_old.shape, f32), shape((...  2.65 us
    pallas_call x1, Pallas kernels, shards(): pl.pallas_call(pack_pair, out_shape=VMEM((rows, LANES), f32), in_specs=[i...  1.56 us
    pallas_call x1, Pallas kernels, shards(): pl.pallas_call(functools.partial(inner_first, band), out_shape=[shape((pa...  1.51 us
    ppermute x4, waiting for transfers between devices, shifted(): return lax.ppermute(value, axis, pairs)  1.5 us
    pallas_call x1, Pallas kernels, shards(): pl.pallas_call(functools.partial(edges, parts, parent_cols), out_shape=[s...  1.43 us
    pallas_call x1, Pallas kernels, shards(): pl.pallas_call(functools.partial(parent_step, parts, band), out_shape=[sh...  1.36 us
  transfers between devices with their start and end apart: 7, of which 1 were waited for; matrix products, arithmetic and copies ran while one was open for 0% of the time, Pallas kernels for 23%

commit v1 on v0

--- a/solution.py
+++ b/solution.py
@@ -24,7 +24,6 @@
 VMEM = pltpu.VMEM
 LIMIT = 24 * 1024 * 1024
 MOST = 54 * 1024 * 1024
-HIGHEST = lax.Precision.HIGHEST
 
 
 def iota(shape, dim):
@@ -187,6 +186,33 @@
                 total = total + pltpu.roll(value, turn, 1)
         out[...] = total
         out[: part.shape[0], :] += part
+
+
+def three_terms(value):
+    terms = []
+    for _ in range(3):
+        term = value.astype(jnp.bfloat16)
+        terms.append(term)
+        value = value - term.astype(jnp.float32)
+    return terms
+
+
+def select_rows(selector, value):
+    selector = selector.astype(jnp.bfloat16)
+    high, middle, low = (
+        jnp.dot(selector, term, preferred_element_type=jnp.float32)
+        for term in three_terms(value)
+    )
+    return high + (middle + low)
+
+
+def select_columns(value, selector):
+    selector = selector.astype(jnp.bfloat16)
+    high, middle, low = (
+        jnp.dot(term, selector, preferred_element_type=jnp.float32)
+        for term in three_terms(value)
+    )
+    return high + (middle + low)
 
 
 def sum_rows(ref):
@@ -444,12 +470,7 @@
     nest_row = jnp.where(index < rows, index, jnp.where(index < rows + 8, index - rows - 3, index - 13))
     parent_row = ((nest_row + 3) * 171 >> 9) - 1 + ox_ref[0]
     pick = (iota((rows + 16, count), 1) == parent_row).astype(jnp.float32)
-    picked = jnp.dot(
-        pick,
-        jnp.concatenate([old, diff], axis=1),
-        precision=HIGHEST,
-        preferred_element_type=jnp.float32,
-    )
+    picked = select_rows(pick, jnp.concatenate([old, diff], axis=1))
     picked_old, picked_diff = picked[:, :LANES], picked[:, LANES:]
 
     lane = iota((rows, LANES), 1)
@@ -584,11 +605,8 @@
     foot = cols // RATIO
     offset = iota((cols, foot), 0) - RATIO * iota((cols, foot), 1)
     gather = ((offset >= 0) & (offset < RATIO)).astype(jnp.float32)
-    means = jnp.dot(
-        jnp.concatenate([jnp.concatenate(values, axis=0) for values in replaced], axis=1),
-        gather,
-        precision=HIGHEST,
-        preferred_element_type=jnp.float32,
+    means = select_columns(
+        jnp.concatenate([jnp.concatenate(values, axis=0) for values in replaced], axis=1), gather
     ) * (1.0 / 9.0)
     coarse_out[...] = means.reshape(coarse_out.shape)
 
@@ -700,7 +718,8 @@
 
 
 def merge(parts, band, ox_ref, oy_ref, late, step, nest, spread, beyond, *rest):
-    own, previous = rest[:parts], rest[parts : 2 * parts]
+    own = rest[:parts]
+    previous = rest[2 * parts - 1 : 2 * parts] + rest[parts : 2 * parts - 1]
     out, nest_out, joined, corner, sem = rest[2 * parts :]
     levels, rows, cols = step.shape
     foot = own[0].shape[2]
@@ -923,9 +942,7 @@
         columns[0],
         columns[-1],
     )
-    previous = [shifted(coarse, along, 1)] + [
-        shifted_both(coarse, k) for k in range(1, parts)
-    ]
+    previous = [shifted_both(coarse, k) for k in range(1, parts)] + [shifted(coarse, along, 1)]
     own = [coarse] + [shifted(coarse, "gy", k) for k in range(1, parts)]
     beyond = shifted(far, along, -2)
     step, nest_stored, late = pl.pallas_call(

time: 24.7 us -> 24.5 us (level)
    ppermute x4, waiting for transfers between devices: 1.5 us -> 0.01 us  [shifted(): return lax.ppermute(value, axis, pairs)]
    ppermute x1, waiting for transfers between devices: 0.04 us -> 1.42 us  [shifted_both(): return lax.ppermute(value, ('gx', 'gy', 'gz'), pairs)]
    ppermute x1, starting transfers between devices: 0.99 us -> 1.43 us  [shifted_both(): return lax.ppermute(value, ('gx', 'gy', 'gz'), pairs)]
    ppermute x4, starting transfers between devices: 7.48 us -> 7.19 us  [shifted(): return lax.ppermute(value, axis, pairs)]
where the time goes in v1:
time: 24.5 us; the launch traced here: 24.4 us
  starting transfers between devices  11.5 us (47%)
  Pallas kernels  9.33 us (38%)
  between operations  2.1 us (9%)
  waiting for transfers between devices  1.47 us (6%)
    ppermute x4, starting transfers between devices, shifted(): return lax.ppermute(value, axis, pairs)  7.19 us
    ppermute x2, starting transfers between devices, swapped(): return lax.ppermute(value, along, pairs)  2.83 us
    pallas_call x1, Pallas kernels, shards(): pl.pallas_call(inner_rest, out_shape=[shape(nest_old.shape, f32), shape((...  2.65 us
    pallas_call x1, Pallas kernels, shards(): pl.pallas_call(pack_pair, out_shape=VMEM((rows, LANES), f32), in_specs=[i...  1.56 us
    pallas_call x1, Pallas kernels, shards(): pl.pallas_call(functools.partial(inner_first, band), out_shape=[shape((pa...  1.51 us
    ppermute x1, starting transfers between devices, shifted_both(): return lax.ppermute(value, ('gx', 'gy', 'gz'), pairs)  1.43 us
    ppermute x1, waiting for transfers between devices, shifted_both(): return lax.ppermute(value, ('gx', 'gy', 'gz'), pairs)  1.42 us
    pallas_call x1, Pallas kernels, shards(): pl.pallas_call(functools.partial(parent_step, parts, band), out_shape=[sh...  1.36 us
  transfers between devices with their start and end apart: 7, of which 1 were waited for; matrix products, arithmetic and copies ran while one was open for 0% of the time, Pallas kernels for 23%

profile of v1, /device:TPU:0, one launch (start us, length us, event | category | flops | bytes accessed | tf_op | source)
XLA Modules:
  0.0 24.4 jit_solution(11808544979411609401)
XLA Ops:
  0.6 0.0 copy-start.1
  0.6 0.0 copy-start
  0.7 0.0 copy-start.2
  0.7 0.0 copy-start.3
  0.7 0.0 copy-start.5
  0.7 1.6 %pack_pair.1 = f32[72,128]{1,0:T(8,128)S(1)} custom-call(f32[8,72,384]{2,1,0:T(8,128)} %nest.7, f32[8,72,384]{2,1,0:T(8,128)} %source.8, f32[8,24,256]{2,1,0:T(8,128)} %parent.5, f32[8,24,256]{2,1,0:T(8,128)} %source.9), custom_call_target="tpu_custom_call" | custom-call | flops 200000 | bytes 800000 | tf_op jit(solution)/shard_map/pack_pair/pallas_call | solution.py:798
  2.2 0.0 copy-start.4
  2.3 3.0 %collective-permute-start = (f32[72,128]{1,0:T(8,128)S(1)}, f32[72,128]{1,0:T(8,128)S(1)}, u32[]{:S(2)}, u32[]{:S(2)}) collective-permute-start(f32[72,128]{1,0:T(8,128)S(1)} %pack_pair.1), channel_id=1, source_target_pairs={{0,2},{2,0},{1,3},{3,1},{4,6},{6,4},{5,7},{7,5},{8,10},{10,8},{9,1... | collective-permute-start | bytes 110600 | tf_op jit(solution)/shard_map/ppermute | solution.py:777
  5.9 0.0 copy-done.1
  5.9 0.0 copy-done
  5.9 0.0 copy-done.2
  5.9 0.0 copy-done.3
  6.0 0.0 copy-done.5
  6.0 0.0 copy-done.4
  6.0 1.5 %inner_first.1 = (f32[24,128]{1,0:T(8,128)S(1)}, f32[8,72,384]{2,1,0:T(8,128)S(1)}, f32[2,4,8,128]{3,2,1,0:T(8,128)S(1)}, s32[8,128]{1,0:T(8,128)S(1)}) custom-call(s32[1]{0:T(128)S(6)} %copy.13.oy_ref, f32[2,8]{1,0:T(2,128)S(1)} %copy-done.5, f32[2,8]{1,0:T(2,128)S(1)} %copy-done.4, f32[8,72,384]{2,1,0:T(8,128)S(1)} %copy-done, ...), custom_call_target="tpu_custom_call" | custom-call | flops 4000000 | bytes 3000000 | tf_op jit(solution)/shard_map/inner_first/pallas_call | solution.py:836
  7.5 0.0 collective-permute-done.rest_0_.y_left.y_right
  7.5 0.1 pack_rows.1
  7.7 2.8 %collective-permute-start.1 = (f32[56,384]{1,0:T(8,128)S(1)}, f32[56,384]{1,0:T(8,128)S(1)}, u32[]{:S(2)}, u32[]{:S(2)}) collective-permute-start(f32[56,384]{1,0:T(8,128)S(1)} %get-tuple-element.28), channel_id=1, source_target_pairs={{1,4},{4,1},{5,8},{8,5},{9,12},{12,9},{13,0},{0,13},{3,6},{6,3},{7... | collective-permute-start | bytes 258056 | tf_op jit(solution)/shard_map/ppermute | solution.py:1003
  10.5 0.0 collective-permute-start.2
  11.1 2.7 %inner_rest.1 = (f32[8,72,384]{2,1,0:T(8,128)S(1)}, f32[4,72,128]{2,1,0:T(8,128)S(1)}, f32[3,192,128]{2,1,0:T(8,128)S(1)}) custom-call(f32[2,8]{1,0:T(2,128)S(1)} %copy-done.4, f32[8,72,384]{2,1,0:T(8,128)S(1)} %copy-done, f32[8,72,384]{2,1,0:T(8,128)S(1)} %get-tuple-element.21.first, f32[8,72,384]{2,1,0:T(8,128)S(1)} %copy-done.1, ...), custom_call_target="tpu_custom_call" | custom-call | flops 8000000 | bytes 6000000 | tf_op jit(solution)/shard_map/inner_rest/pallas_call | solution.py:895
  13.8 0.0 collective-permute-done.1.across
  13.8 0.0 collective-permute-done.2.within
  13.8 1.3 %edges.1 = (f32[2,72,128]{2,1,0:T(8,128)S(1)}, f32[8,2,8,384]{3,2,1,0:T(8,128)S(1)}, f32[8,24,128]{2,1,0:T(8,128)S(1)}, f32[8,128]{1,0:T(8,128)S(1)}) custom-call(s32[1]{0:T(128)S(6)} %copy.12.ox_ref, f32[2,4,8,128]{3,2,1,0:T(8,128)S(1)} %get-tuple-element.20.spread, f32[8,72,384]{2,1,0:T(8,128)S(1)} %copy-done, f32[8,72,384]{2,1,0:T(8,128)S(1)} %copy-done.1, ...), custom_call_target="tpu_custom_call" | custom-call | flops 4000000 | bytes 3000000 | tf_op jit(solution)/shard_map/edges/pallas_call | solution.py:912
  15.1 0.5 %collective-permute-start.6 = (f32[8,24,128]{2,1,0:T(8,128)S(1)}, f32[8,24,128]{2,1,0:T(8,128)S(1)}, u32[]{:S(2)}, u32[]{:S(2)}) collective-permute-start(f32[8,24,128]{2,1,0:T(8,128)S(1)} %get-tuple-element.37.rest_0_), channel_id=1, source_target_pairs={{0,1},{1,4},{4,5},{5,8},{8,9},{9,12},{12,13},{13,0},{2,3},{3,6},{6... | collective-permute-start | bytes 294920 | tf_op jit(solution)/shard_map/ppermute | solution.py:777
  15.7 1.4 %collective-permute-start.5 = (f32[8,24,128]{2,1,0:T(8,128)S(1)}, f32[8,24,128]{2,1,0:T(8,128)S(1)}, u32[]{:S(2)}, u32[]{:S(2)}) collective-permute-start(f32[8,24,128]{2,1,0:T(8,128)S(1)} %get-tuple-element.37.rest_0_), channel_id=1, source_target_pairs={{0,3},{1,6},{2,1},{3,4},{4,7},{5,10},{6,5},{7,8},{8,11},{9,14},{10... | collective-permute-start | bytes 294920 | tf_op jit(solution)/shard_map/ppermute | solution.py:1016
  17.1 0.5 %collective-permute-start.4 = (f32[8,24,128]{2,1,0:T(8,128)S(1)}, f32[8,24,128]{2,1,0:T(8,128)S(1)}, u32[]{:S(2)}, u32[]{:S(2)}) collective-permute-start(f32[8,24,128]{2,1,0:T(8,128)S(1)} %get-tuple-element.37.rest_0_), channel_id=1, source_target_pairs={{0,2},{2,0},{1,3},{3,1},{4,6},{6,4},{5,7},{7,5},{8,10},{10,8},{9,1... | collective-permute-start | bytes 294920 | tf_op jit(solution)/shard_map/ppermute | solution.py:777
  17.6 3.1 %collective-permute-start.3 = (f32[8,128]{1,0:T(8,128)S(1)}, f32[8,128]{1,0:T(8,128)S(1)}, u32[]{:S(2)}, u32[]{:S(2)}) collective-permute-start(f32[8,128]{1,0:T(8,128)S(1)} %get-tuple-element.36), channel_id=1, source_target_pairs={{0,12},{1,13},{4,0},{5,1},{8,4},{9,5},{12,8},{13,9},{2,14},{3,15},... | collective-permute-start | bytes 12296 | tf_op jit(solution)/shard_map/ppermute | solution.py:777
  20.7 1.4 %parent_step.1 = (f32[8,24,256]{2,1,0:T(8,128)S(1)}, f32[8,72,384]{2,1,0:T(8,128)}, f32[8,256]{1,0:T(8,128)S(1)}) custom-call(s32[1]{0:T(128)S(6)} %copy.12.ox_ref, s32[1]{0:T(128)S(6)} %copy.13.oy_ref, f32[2,4,8,128]{3,2,1,0:T(8,128)S(1)} %get-tuple-element.20.spread, f32[8,72,384]{2,1,0:T(8,128)S(1)} %get-tuple-element.25.third, ...), custom_call_target="tpu_custom_call" | custom-call | flops 800000 | bytes 2500000 | tf_op jit(solution)/shard_map/parent_step/pallas_call | solution.py:948
  22.1 0.0 collective-permute-done.3.beyond
  22.1 0.0 collective-permute-done.6.rest_3_
  22.1 1.4 %collective-permute-done.5.rest_2_ = f32[8,24,128]{2,1,0:T(8,128)S(1)} collective-permute-done((f32[8,24,128]{2,1,0:T(8,128)S(1)}, f32[8,24,128]{2,1,0:T(8,128)S(1)}, u32[]{:S(2)}, u32[]{:S(2)}) %collective-permute-start.5) | collective-permute-done | bytes 98336 | tf_op jit(solution)/shard_map/ppermute | solution.py:1016
  23.5 0.0 collective-permute-done.4.rest_1_
  23.5 0.8 %merge.1 = (f32[8,24,256]{2,1,0:T(8,128)}, f32[8,72,384]{2,1,0:T(8,128)}) custom-call(s32[1]{0:T(128)S(6)} %copy.12.ox_ref, s32[1]{0:T(128)S(6)} %copy.13.oy_ref, f32[8,256]{1,0:T(8,128)S(1)} %get-tuple-element.33.late, f32[8,24,256]{2,1,0:T(8,128)S(1)} %get-tuple-element.34.step, ...), custom_call_target="tpu_custom_call", output_to_operand_aliasing={{1}: (4, {})} | custom-call | flops 200000 | bytes 800000 | tf_op jit(solution)/shard_map/merge/pallas_call | solution.py:979
Async XLA Ops:
  0.6 5.3 %copy-start.1 = (f32[8,72,384]{2,1,0:T(8,128)S(1)}, f32[8,72,384]{2,1,0:T(8,128)}, u32[]{:S(2)}) copy-start(f32[8,72,384]{2,1,0:T(8,128)} %source.8) | copy-start | bytes 2654212
  0.6 5.3 %copy-start = (f32[8,72,384]{2,1,0:T(8,128)S(1)}, f32[8,72,384]{2,1,0:T(8,128)}, u32[]{:S(2)}) copy-start(f32[8,72,384]{2,1,0:T(8,128)} %nest.7) | copy-start | bytes 2654212
  0.7 5.3 %copy-start.2 = (f32[8,24,256]{2,1,0:T(8,128)S(1)}, f32[8,24,256]{2,1,0:T(8,128)}, u32[]{:S(2)}) copy-start(f32[8,24,256]{2,1,0:T(8,128)} %parent.5) | copy-start | bytes 589828
  0.7 5.3 %copy-start.3 = (f32[8,24,256]{2,1,0:T(8,128)S(1)}, f32[8,24,256]{2,1,0:T(8,128)}, u32[]{:S(2)}) copy-start(f32[8,24,256]{2,1,0:T(8,128)} %source.9) | copy-start | bytes 589828
  0.7 5.3 %copy-start.5 = (f32[2,8]{1,0:T(2,128)S(1)}, f32[2,8]{1,0:T(2,128)}, u32[]{:S(2)}) copy-start(f32[2,8]{1,0:T(2,128)} %parent_coefs.1) | copy-start | bytes 196
  2.2 3.7 %copy-start.4 = (f32[2,8]{1,0:T(2,128)S(1)}, f32[2,8]{1,0:T(2,128)}, u32[]{:S(2)}) copy-start(f32[2,8]{1,0:T(2,128)} %coefs.3) | copy-start | bytes 196
  2.3 5.2 %collective-permute-start = (f32[72,128]{1,0:T(8,128)S(1)}, f32[72,128]{1,0:T(8,128)S(1)}, u32[]{:S(2)}, u32[]{:S(2)}) collective-permute-start(f32[72,128]{1,0:T(8,128)S(1)} %pack_pair.1), channel_id=1, source_target_pairs={{0,2},{2,0},{1,3},{3,1},{4,6},{6,4},{5,7},{7,5},{8,10},{10,8},{9,1... | collective-permute-start | bytes 110600 | tf_op jit(solution)/shard_map/ppermute | solution.py:777
  7.7 6.2 %collective-permute-start.1 = (f32[56,384]{1,0:T(8,128)S(1)}, f32[56,384]{1,0:T(8,128)S(1)}, u32[]{:S(2)}, u32[]{:S(2)}) collective-permute-start(f32[56,384]{1,0:T(8,128)S(1)} %get-tuple-element.28), channel_id=1, source_target_pairs={{1,4},{4,1},{5,8},{8,5},{9,12},{12,9},{13,0},{0,13},{3,6},{6,3},{7... | collective-permute-start | bytes 258056 | tf_op jit(solution)/shard_map/ppermute | solution.py:1003
  10.5 3.4 %collective-permute-start.2 = (f32[56,384]{1,0:T(8,128)S(1)}, f32[56,384]{1,0:T(8,128)S(1)}, u32[]{:S(2)}, u32[]{:S(2)}) collective-permute-start(f32[56,384]{1,0:T(8,128)S(1)} %get-tuple-element.29), channel_id=1, source_target_pairs={{0,1},{1,0},{4,5},{5,4},{8,9},{9,8},{12,13},{13,12},{2,3},{3,2},{6... | collective-permute-start | bytes 258056 | tf_op jit(solution)/shard_map/ppermute | solution.py:1003
  15.1 7.0 %collective-permute-start.6 = (f32[8,24,128]{2,1,0:T(8,128)S(1)}, f32[8,24,128]{2,1,0:T(8,128)S(1)}, u32[]{:S(2)}, u32[]{:S(2)}) collective-permute-start(f32[8,24,128]{2,1,0:T(8,128)S(1)} %get-tuple-element.37.rest_0_), channel_id=1, source_target_pairs={{0,1},{1,4},{4,5},{5,8},{8,9},{9,12},{12,13},{13,0},{2,3},{3,6},{6... | collective-permute-start | bytes 294920 | tf_op jit(solution)/shard_map/ppermute | solution.py:777
  15.7 7.9 %collective-permute-start.5 = (f32[8,24,128]{2,1,0:T(8,128)S(1)}, f32[8,24,128]{2,1,0:T(8,128)S(1)}, u32[]{:S(2)}, u32[]{:S(2)}) collective-permute-start(f32[8,24,128]{2,1,0:T(8,128)S(1)} %get-tuple-element.37.rest_0_), channel_id=1, source_target_pairs={{0,3},{1,6},{2,1},{3,4},{4,7},{5,10},{6,5},{7,8},{8,11},{9,14},{10... | collective-permute-start | bytes 294920 | tf_op jit(solution)/shard_map/ppermute | solution.py:1016
  17.1 6.5 %collective-permute-start.4 = (f32[8,24,128]{2,1,0:T(8,128)S(1)}, f32[8,24,128]{2,1,0:T(8,128)S(1)}, u32[]{:S(2)}, u32[]{:S(2)}) collective-permute-start(f32[8,24,128]{2,1,0:T(8,128)S(1)} %get-tuple-element.37.rest_0_), channel_id=1, source_target_pairs={{0,2},{2,0},{1,3},{3,1},{4,6},{6,4},{5,7},{7,5},{8,10},{10,8},{9,1... | collective-permute-start | bytes 294920 | tf_op jit(solution)/shard_map/ppermute | solution.py:777
  17.6 4.5 %collective-permute-start.3 = (f32[8,128]{1,0:T(8,128)S(1)}, f32[8,128]{1,0:T(8,128)S(1)}, u32[]{:S(2)}, u32[]{:S(2)}) collective-permute-start(f32[8,128]{1,0:T(8,128)S(1)} %get-tuple-element.36), channel_id=1, source_target_pairs={{0,12},{1,13},{4,0},{5,1},{8,4},{9,5},{12,8},{13,9},{2,14},{3,15},... | collective-permute-start | bytes 12296 | tf_op jit(solution)/shard_map/ppermute | solution.py:777

commit v2 on v1

--- a/solution.py
+++ b/solution.py
@@ -718,9 +718,8 @@
 
 
 def merge(parts, band, ox_ref, oy_ref, late, step, nest, spread, beyond, *rest):
-    own = rest[:parts]
-    previous = rest[2 * parts - 1 : 2 * parts] + rest[parts : 2 * parts - 1]
-    out, nest_out, joined, corner, sem = rest[2 * parts :]
+    own, arrived = rest[:parts], rest[parts:-5]
+    out, nest_out, joined, corner, sem = rest[-5:]
     levels, rows, cols = step.shape
     foot = own[0].shape[2]
     me = lax.axis_index("gy")
@@ -749,7 +748,11 @@
     ox = ox_ref[0]
     oy = oy_ref[0]
     for k in range(parts):
-        joined[k, :, :rows, :] = previous[k][...]
+        if parts == 2 and k == 1:
+            to_north, to_south = arrived[0], arrived[2]
+            joined[k, :, :rows, :] = jnp.where(me == 0, to_south[...], to_north[...])
+        else:
+            joined[k, :, :rows, :] = arrived[1 if parts == 2 else k][...]
         joined[k, :, rows:, :] = own[k][...]
     lane = iota((rows, LANES), 1)
     row = iota((rows, LANES), 0)
@@ -942,7 +945,14 @@
         columns[0],
         columns[-1],
     )
-    previous = [shifted_both(coarse, k) for k in range(1, parts)] + [shifted(coarse, along, 1)]
+    if parts == 2:
+        arrived = [
+            shifted_both(coarse, 1, 1),
+            shifted(coarse, along, 1),
+            shifted_both(coarse, 1, 0),
+        ]
+    else:
+        arrived = [shifted_both(coarse, k) for k in range(parts)]
     own = [coarse] + [shifted(coarse, "gy", k) for k in range(1, parts)]
     beyond = shifted(far, along, -2)
     step, nest_stored, late = pl.pallas_call(
@@ -979,7 +989,7 @@
     parent_new, nest_new = pl.pallas_call(
         functools.partial(merge, parts, band),
         out_shape=[shape(parent_old.shape, f32), shape(nest_old.shape, f32)],
-        in_specs=[scalars()] * 2 + [whole()] * 2 + [in_hbm] + [whole()] * (2 + 2 * parts),
+        in_specs=[scalars()] * 2 + [whole()] * 2 + [in_hbm] + [whole()] * (2 + parts + len(arrived)),
         out_specs=[whole(), in_hbm],
         scratch_shapes=[
             VMEM((parts, levels, 2 * parent_rows, foot), f32),
@@ -990,7 +1000,7 @@
         compiler_params=params(),
         cost_estimate=cost(200000, 800000),
         name="merge",
-    )(offset_x, offset_y, late, step, nest_stored, spread, beyond, *own, *previous)
+    )(offset_x, offset_y, late, step, nest_stored, spread, beyond, *own, *arrived)
     return (parent_new, nest_new)
 
 
@@ -1003,7 +1013,7 @@
     return lax.ppermute(value, along, pairs)
 
 
-def shifted_both(value, steps):
+def shifted_both(value, steps, only=None):
     sizes = [lax.axis_size(axis) for axis in ("gx", "gy", "gz")]
     gx, gy, gz = sizes
     pairs = []
@@ -1012,6 +1022,8 @@
             for z in range(gz):
                 place = (x * gz + z + 1) % (gx * gz)
                 target = (place // gz * gy + (y + steps) % gy) * gz + place % gz
+                if only is not None and (y + steps) % gy != only:
+                    continue
                 pairs.append(((x * gy + y) * gz + z, target))
     return lax.ppermute(value, ("gx", "gy", "gz"), pairs)
 

time: 24.5 us -> 27.5 us (1.12)
  starting transfers between devices: 11.5 us -> 15.5 us
  waiting for transfers between devices: 1.47 us -> 0.35 us
    ppermute x1 -> x2, starting transfers between devices: 1.43 us -> 5.38 us  [shifted_both(): return lax.ppermute(value, ('gx', 'gy', 'gz'), pairs)]
    ppermute x1 -> x2, waiting for transfers between devices: 1.42 us -> 0.01 us  [shifted_both(): return lax.ppermute(value, ('gx', 'gy', 'gz'), pairs)]
    ppermute x4, waiting for transfers between devices: 0.01 us -> 0.31 us  [shifted(): return lax.ppermute(value, axis, pairs)]
  transfers between devices with their start and end apart: 7 -> 8, of which waited for: 1 -> 1; matrix products, arithmetic and copies ran while one was open for 0% -> 0% of each run, Pallas kernels for 23% -> 20%
where the time goes in v2:
time: 27.5 us; the launch traced here: 27.3 us
  starting transfers between devices  15.5 us (56%)
  Pallas kernels  9.33 us (34%)
  between operations  2.14 us (8%)
  waiting for transfers between devices  0.35 us (1%)
    ppermute x4, starting transfers between devices, shifted(): return lax.ppermute(value, axis, pairs)  7.27 us
    ppermute x2, starting transfers between devices, shifted_both(): return lax.ppermute(value, ('gx', 'gy', 'gz'), pairs)  5.38 us
    ppermute x2, starting transfers between devices, swapped(): return lax.ppermute(value, along, pairs)  2.83 us
    pallas_call x1, Pallas kernels, shards(): pl.pallas_call(inner_rest, out_shape=[shape(nest_old.shape, f32), shape((...  2.65 us
    pallas_call x1, Pallas kernels, shards(): pl.pallas_call(pack_pair, out_shape=VMEM((rows, LANES), f32), in_specs=[i...  1.56 us
    pallas_call x1, Pallas kernels, shards(): pl.pallas_call(functools.partial(inner_first, band), out_shape=[shape((pa...  1.51 us
    pallas_call x1, Pallas kernels, shards(): pl.pallas_call(functools.partial(parent_step, parts, band), out_shape=[sh...  1.36 us
    pallas_call x1, Pallas kernels, shards(): pl.pallas_call(functools.partial(edges, parts, parent_cols), out_shape=[s...  1.27 us
  transfers between devices with their start and end apart: 8, of which 1 were waited for; matrix products, arithmetic and copies ran while one was open for 0% of the time, Pallas kernels for 20%

profile of v2, /device:TPU:0, one launch (start us, length us, event | category | flops | bytes accessed | tf_op | source)
XLA Modules:
  0.0 27.3 jit_solution(10628188966907936280)
XLA Ops:
  0.6 0.0 copy-start.1
  0.6 0.0 copy-start
  0.7 0.0 copy-start.2
  0.7 0.0 copy-start.3
  0.7 0.0 copy-start.5
  0.7 1.6 %pack_pair.1 = f32[72,128]{1,0:T(8,128)S(1)} custom-call(f32[8,72,384]{2,1,0:T(8,128)} %nest.7, f32[8,72,384]{2,1,0:T(8,128)} %source.8, f32[8,24,256]{2,1,0:T(8,128)} %parent.5, f32[8,24,256]{2,1,0:T(8,128)} %source.9), custom_call_target="tpu_custom_call" | custom-call | flops 200000 | bytes 800000 | tf_op jit(solution)/shard_map/pack_pair/pallas_call | solution.py:801
  2.2 0.0 copy-start.4
  2.3 3.0 %collective-permute-start = (f32[72,128]{1,0:T(8,128)S(1)}, f32[72,128]{1,0:T(8,128)S(1)}, u32[]{:S(2)}, u32[]{:S(2)}) collective-permute-start(f32[72,128]{1,0:T(8,128)S(1)} %pack_pair.1), channel_id=1, source_target_pairs={{0,2},{2,0},{1,3},{3,1},{4,6},{6,4},{5,7},{7,5},{8,10},{10,8},{9,1... | collective-permute-start | bytes 110600 | tf_op jit(solution)/shard_map/ppermute | solution.py:780
  5.9 0.0 copy-done.1
  5.9 0.0 copy-done
  5.9 0.0 copy-done.2
  5.9 0.0 copy-done.3
  6.0 0.0 copy-done.5
  6.0 0.0 copy-done.4
  6.0 1.5 %inner_first.1 = (f32[24,128]{1,0:T(8,128)S(1)}, f32[8,72,384]{2,1,0:T(8,128)S(1)}, f32[2,4,8,128]{3,2,1,0:T(8,128)S(1)}, s32[8,128]{1,0:T(8,128)S(1)}) custom-call(s32[1]{0:T(128)S(6)} %copy.13.oy_ref, f32[2,8]{1,0:T(2,128)S(1)} %copy-done.5, f32[2,8]{1,0:T(2,128)S(1)} %copy-done.4, f32[8,72,384]{2,1,0:T(8,128)S(1)} %copy-done, ...), custom_call_target="tpu_custom_call" | custom-call | flops 4000000 | bytes 3000000 | tf_op jit(solution)/shard_map/inner_first/pallas_call | solution.py:839
  7.5 0.0 collective-permute-done.rest_0_.y_left.y_right
  7.5 0.1 pack_rows.1
  7.7 2.8 %collective-permute-start.1 = (f32[56,384]{1,0:T(8,128)S(1)}, f32[56,384]{1,0:T(8,128)S(1)}, u32[]{:S(2)}, u32[]{:S(2)}) collective-permute-start(f32[56,384]{1,0:T(8,128)S(1)} %get-tuple-element.28), channel_id=1, source_target_pairs={{1,4},{4,1},{5,8},{8,5},{9,12},{12,9},{13,0},{0,13},{3,6},{6,3},{7... | collective-permute-start | bytes 258056 | tf_op jit(solution)/shard_map/ppermute | solution.py:1013
  10.5 0.0 collective-permute-start.2
  11.1 2.7 %inner_rest.1 = (f32[8,72,384]{2,1,0:T(8,128)S(1)}, f32[4,72,128]{2,1,0:T(8,128)S(1)}, f32[3,192,128]{2,1,0:T(8,128)S(1)}) custom-call(f32[2,8]{1,0:T(2,128)S(1)} %copy-done.4, f32[8,72,384]{2,1,0:T(8,128)S(1)} %copy-done, f32[8,72,384]{2,1,0:T(8,128)S(1)} %get-tuple-element.21.first, f32[8,72,384]{2,1,0:T(8,128)S(1)} %copy-done.1, ...), custom_call_target="tpu_custom_call" | custom-call | flops 8000000 | bytes 6000000 | tf_op jit(solution)/shard_map/inner_rest/pallas_call | solution.py:898
  13.8 0.0 collective-permute-done.1.across
  13.8 0.0 collective-permute-done.2.within
  13.8 1.3 %edges.1 = (f32[2,72,128]{2,1,0:T(8,128)S(1)}, f32[8,2,8,384]{3,2,1,0:T(8,128)S(1)}, f32[8,24,128]{2,1,0:T(8,128)S(1)}, f32[8,128]{1,0:T(8,128)S(1)}) custom-call(s32[1]{0:T(128)S(6)} %copy.12.ox_ref, f32[2,4,8,128]{3,2,1,0:T(8,128)S(1)} %get-tuple-element.20.spread, f32[8,72,384]{2,1,0:T(8,128)S(1)} %copy-done, f32[8,72,384]{2,1,0:T(8,128)S(1)} %copy-done.1, ...), custom_call_target="tpu_custom_call" | custom-call | flops 4000000 | bytes 3000000 | tf_op jit(solution)/shard_map/edges/pallas_call | solution.py:915
  15.1 1.3 %collective-permute-start.7 = (f32[8,24,128]{2,1,0:T(8,128)S(1)}, f32[8,24,128]{2,1,0:T(8,128)S(1)}, u32[]{:S(2)}, u32[]{:S(2)}) collective-permute-start(f32[8,24,128]{2,1,0:T(8,128)S(1)} %get-tuple-element.37.rest_0_), channel_id=1, source_target_pairs={{2,1},{3,4},{6,5},{7,8},{10,9},{11,12},{14,13},{15,0},{18,17},{19,... | collective-permute-start | bytes 294920 | tf_op jit(solution)/shard_map/ppermute | solution.py:1028
  16.4 0.5 %collective-permute-start.6 = (f32[8,24,128]{2,1,0:T(8,128)S(1)}, f32[8,24,128]{2,1,0:T(8,128)S(1)}, u32[]{:S(2)}, u32[]{:S(2)}) collective-permute-start(f32[8,24,128]{2,1,0:T(8,128)S(1)} %get-tuple-element.37.rest_0_), channel_id=1, source_target_pairs={{0,1},{1,4},{4,5},{5,8},{8,9},{9,12},{12,13},{13,0},{2,3},{3,6},{6... | collective-permute-start | bytes 294920 | tf_op jit(solution)/shard_map/ppermute | solution.py:780
  17.0 4.1 %collective-permute-start.5 = (f32[8,24,128]{2,1,0:T(8,128)S(1)}, f32[8,24,128]{2,1,0:T(8,128)S(1)}, u32[]{:S(2)}, u32[]{:S(2)}) collective-permute-start(f32[8,24,128]{2,1,0:T(8,128)S(1)} %get-tuple-element.37.rest_0_), channel_id=1, source_target_pairs={{0,3},{1,6},{4,7},{5,10},{8,11},{9,14},{12,15},{13,2},{16,19},{17,... | collective-permute-start | bytes 294920 | tf_op jit(solution)/shard_map/ppermute | solution.py:1028
  21.1 0.1 collective-permute-start.4
  21.1 3.7 %collective-permute-start.3 = (f32[8,128]{1,0:T(8,128)S(1)}, f32[8,128]{1,0:T(8,128)S(1)}, u32[]{:S(2)}, u32[]{:S(2)}) collective-permute-start(f32[8,128]{1,0:T(8,128)S(1)} %get-tuple-element.36), channel_id=1, source_target_pairs={{0,12},{1,13},{4,0},{5,1},{8,4},{9,5},{12,8},{13,9},{2,14},{3,15},... | collective-permute-start | bytes 12296 | tf_op jit(solution)/shard_map/ppermute | solution.py:780
  24.8 1.4 %parent_step.1 = (f32[8,24,256]{2,1,0:T(8,128)S(1)}, f32[8,72,384]{2,1,0:T(8,128)}, f32[8,256]{1,0:T(8,128)S(1)}) custom-call(s32[1]{0:T(128)S(6)} %copy.12.ox_ref, s32[1]{0:T(128)S(6)} %copy.13.oy_ref, f32[2,4,8,128]{3,2,1,0:T(8,128)S(1)} %get-tuple-element.20.spread, f32[8,72,384]{2,1,0:T(8,128)S(1)} %get-tuple-element.25.third, ...), custom_call_target="tpu_custom_call" | custom-call | flops 800000 | bytes 2500000 | tf_op jit(solution)/shard_map/parent_step/pallas_call | solution.py:958
  26.2 0.0 collective-permute-done.3.beyond
  26.2 0.0 collective-permute-done.7.rest_4_
  26.2 0.0 collective-permute-done.6.rest_3_
  26.2 0.0 collective-permute-done.5.rest_2_
  26.2 0.3 %collective-permute-done.4.rest_1_ = f32[8,24,128]{2,1,0:T(8,128)S(1)} collective-permute-done((f32[8,24,128]{2,1,0:T(8,128)S(1)}, f32[8,24,128]{2,1,0:T(8,128)S(1)}, u32[]{:S(2)}, u32[]{:S(2)}) %collective-permute-start.4) | collective-permute-done | bytes 98336 | tf_op jit(solution)/shard_map/ppermute | solution.py:780
  26.5 0.8 %merge.1 = (f32[8,24,256]{2,1,0:T(8,128)}, f32[8,72,384]{2,1,0:T(8,128)}) custom-call(s32[1]{0:T(128)S(6)} %copy.12.ox_ref, s32[1]{0:T(128)S(6)} %copy.13.oy_ref, f32[8,256]{1,0:T(8,128)S(1)} %get-tuple-element.33.late, f32[8,24,256]{2,1,0:T(8,128)S(1)} %get-tuple-element.34.step, ...), custom_call_target="tpu_custom_call", output_to_operand_aliasing={{1}: (4, {})} | custom-call | flops 200000 | bytes 800000 | tf_op jit(solution)/shard_map/merge/pallas_call | solution.py:989
Async XLA Ops:
  0.6 5.3 %copy-start.1 = (f32[8,72,384]{2,1,0:T(8,128)S(1)}, f32[8,72,384]{2,1,0:T(8,128)}, u32[]{:S(2)}) copy-start(f32[8,72,384]{2,1,0:T(8,128)} %source.8) | copy-start | bytes 2654212
  0.6 5.3 %copy-start = (f32[8,72,384]{2,1,0:T(8,128)S(1)}, f32[8,72,384]{2,1,0:T(8,128)}, u32[]{:S(2)}) copy-start(f32[8,72,384]{2,1,0:T(8,128)} %nest.7) | copy-start | bytes 2654212
  0.7 5.3 %copy-start.2 = (f32[8,24,256]{2,1,0:T(8,128)S(1)}, f32[8,24,256]{2,1,0:T(8,128)}, u32[]{:S(2)}) copy-start(f32[8,24,256]{2,1,0:T(8,128)} %parent.5) | copy-start | bytes 589828
  0.7 5.3 %copy-start.3 = (f32[8,24,256]{2,1,0:T(8,128)S(1)}, f32[8,24,256]{2,1,0:T(8,128)}, u32[]{:S(2)}) copy-start(f32[8,24,256]{2,1,0:T(8,128)} %source.9) | copy-start | bytes 589828
  0.7 5.3 %copy-start.5 = (f32[2,8]{1,0:T(2,128)S(1)}, f32[2,8]{1,0:T(2,128)}, u32[]{:S(2)}) copy-start(f32[2,8]{1,0:T(2,128)} %parent_coefs.1) | copy-start | bytes 196
  2.2 3.7 %copy-start.4 = (f32[2,8]{1,0:T(2,128)S(1)}, f32[2,8]{1,0:T(2,128)}, u32[]{:S(2)}) copy-start(f32[2,8]{1,0:T(2,128)} %coefs.3) | copy-start | bytes 196
  2.3 5.2 %collective-permute-start = (f32[72,128]{1,0:T(8,128)S(1)}, f32[72,128]{1,0:T(8,128)S(1)}, u32[]{:S(2)}, u32[]{:S(2)}) collective-permute-start(f32[72,128]{1,0:T(8,128)S(1)} %pack_pair.1), channel_id=1, source_target_pairs={{0,2},{2,0},{1,3},{3,1},{4,6},{6,4},{5,7},{7,5},{8,10},{10,8},{9,1... | collective-permute-start | bytes 110600 | tf_op jit(solution)/shard_map/ppermute | solution.py:780
  7.7 6.2 %collective-permute-start.1 = (f32[56,384]{1,0:T(8,128)S(1)}, f32[56,384]{1,0:T(8,128)S(1)}, u32[]{:S(2)}, u32[]{:S(2)}) collective-permute-start(f32[56,384]{1,0:T(8,128)S(1)} %get-tuple-element.28), channel_id=1, source_target_pairs={{1,4},{4,1},{5,8},{8,5},{9,12},{12,9},{13,0},{0,13},{3,6},{6,3},{7... | collective-permute-start | bytes 258056 | tf_op jit(solution)/shard_map/ppermute | solution.py:1013
  10.5 3.4 %collective-permute-start.2 = (f32[56,384]{1,0:T(8,128)S(1)}, f32[56,384]{1,0:T(8,128)S(1)}, u32[]{:S(2)}, u32[]{:S(2)}) collective-permute-start(f32[56,384]{1,0:T(8,128)S(1)} %get-tuple-element.29), channel_id=1, source_target_pairs={{0,1},{1,0},{4,5},{5,4},{8,9},{9,8},{12,13},{13,12},{2,3},{3,2},{6... | collective-permute-start | bytes 258056 | tf_op jit(solution)/shard_map/ppermute | solution.py:1013
  15.1 11.1 %collective-permute-start.7 = (f32[8,24,128]{2,1,0:T(8,128)S(1)}, f32[8,24,128]{2,1,0:T(8,128)S(1)}, u32[]{:S(2)}, u32[]{:S(2)}) collective-permute-start(f32[8,24,128]{2,1,0:T(8,128)S(1)} %get-tuple-element.37.rest_0_), channel_id=1, source_target_pairs={{2,1},{3,4},{6,5},{7,8},{10,9},{11,12},{14,13},{15,0},{18,17},{19,... | collective-permute-start | bytes 294920 | tf_op jit(solution)/shard_map/ppermute | solution.py:1028
  16.4 9.8 %collective-permute-start.6 = (f32[8,24,128]{2,1,0:T(8,128)S(1)}, f32[8,24,128]{2,1,0:T(8,128)S(1)}, u32[]{:S(2)}, u32[]{:S(2)}) collective-permute-start(f32[8,24,128]{2,1,0:T(8,128)S(1)} %get-tuple-element.37.rest_0_), channel_id=1, source_target_pairs={{0,1},{1,4},{4,5},{5,8},{8,9},{9,12},{12,13},{13,0},{2,3},{3,6},{6... | collective-permute-start | bytes 294920 | tf_op jit(solution)/shard_map/ppermute | solution.py:780
  17.0 9.2 %collective-permute-start.5 = (f32[8,24,128]{2,1,0:T(8,128)S(1)}, f32[8,24,128]{2,1,0:T(8,128)S(1)}, u32[]{:S(2)}, u32[]{:S(2)}) collective-permute-start(f32[8,24,128]{2,1,0:T(8,128)S(1)} %get-tuple-element.37.rest_0_), channel_id=1, source_target_pairs={{0,3},{1,6},{4,7},{5,10},{8,11},{9,14},{12,15},{13,2},{16,19},{17,... | collective-permute-start | bytes 294920 | tf_op jit(solution)/shard_map/ppermute | solution.py:1028
  21.1 5.4 %collective-permute-start.4 = (f32[8,24,128]{2,1,0:T(8,128)S(1)}, f32[8,24,128]{2,1,0:T(8,128)S(1)}, u32[]{:S(2)}, u32[]{:S(2)}) collective-permute-start(f32[8,24,128]{2,1,0:T(8,128)S(1)} %get-tuple-element.37.rest_0_), channel_id=1, source_target_pairs={{0,2},{2,0},{1,3},{3,1},{4,6},{6,4},{5,7},{7,5},{8,10},{10,8},{9,1... | collective-permute-start | bytes 294920 | tf_op jit(solution)/shard_map/ppermute | solution.py:780
  21.1 5.0 %collective-permute-start.3 = (f32[8,128]{1,0:T(8,128)S(1)}, f32[8,128]{1,0:T(8,128)S(1)}, u32[]{:S(2)}, u32[]{:S(2)}) collective-permute-start(f32[8,128]{1,0:T(8,128)S(1)} %get-tuple-element.36), channel_id=1, source_target_pairs={{0,12},{1,13},{4,0},{5,1},{8,4},{9,5},{12,8},{13,9},{2,14},{3,15},... | collective-permute-start | bytes 12296 | tf_op jit(solution)/shard_map/ppermute | solution.py:780

commit v3 on v1

--- a/solution.py
+++ b/solution.py
@@ -299,8 +299,50 @@
     inner_substep(coefs, nest, source, first)
 
 
-def inner_rest(coefs, nest, first, source, after_pack, third, packs, sums, second, split):
+def own_windows(parts, nest, source, y_left, y_right, window_old, window_src):
     levels, rows, cols = nest.shape
+    pieces = cols // LANES
+    me = lax.axis_index("gy")
+    for level in range(levels):
+        for buf, field, shift in ((window_old, nest, 0), (window_src, source, SOURCE_AT)):
+            for window, first, turn in ((0, 0, 3), (1, rows - 8, 5)):
+                tiles = [
+                    field[level, first : first + 8, piece * LANES : (piece + 1) * LANES]
+                    for piece in range(pieces)
+                ]
+                tiles = with_columns(
+                    tiles,
+                    y_left[first : first + 8, :],
+                    y_right[first : first + 8, :],
+                    me,
+                    parts,
+                    STRIDE * level + shift,
+                )
+                for piece, value in enumerate(tiles):
+                    buf[level, window, :, piece * LANES : (piece + 1) * LANES] = pltpu.roll(
+                        value, turn, 0
+                    )
+
+
+def inner_rest(
+    parts,
+    coefs,
+    nest,
+    first,
+    source,
+    y_left,
+    y_right,
+    after_pack,
+    third,
+    packs,
+    window_old,
+    window_src,
+    sums,
+    second,
+    split,
+):
+    levels, rows, cols = nest.shape
+    own_windows(parts, nest, source, y_left, y_right, window_old, window_src)
     lane = iota((rows, LANES), 1)
     for at, ref in enumerate((nest, source)):
         left = jnp.zeros(lane.shape, jnp.float32)
@@ -397,10 +439,10 @@
     parent_cols,
     ox_ref,
     spread,
-    nest,
-    source,
     sums,
     packs,
+    window_old,
+    window_src,
     strips,
     across,
     within,
@@ -416,8 +458,10 @@
     pong,
     src,
 ):
-    levels, rows, cols = nest.shape
+    levels = ping.shape[0]
     width = ping.shape[3]
+    rows = sides.shape[1]
+    cols = sums.shape[0] * LANES
     pieces = cols // LANES
     me = lax.axis_index("gy")
     core = lax.axis_index("gz")
@@ -500,36 +544,13 @@
 
     sub = iota((8, width), 0)
     lane = iota((8, LANES), 1)
+    ping[...] = window_old[...]
+    src[...] = window_src[...]
     for level in range(levels):
-        for buf, field, shift, n, base in (
-            (ping, nest, 0, 3, 0),
-            (src, source, SOURCE_AT, 2, SOURCE_ROW),
-        ):
-            for window, first, turn, at, message in (
-                (0, 0, 3, 3 - n, before),
-                (1, rows - 8, 5, 5, after),
-            ):
-                tiles = [
-                    field[level, first : first + 8, piece * LANES : (piece + 1) * LANES]
-                    for piece in range(pieces)
-                ]
-                tiles = with_columns(
-                    tiles,
-                    y_left[first : first + 8, :],
-                    y_right[first : first + 8, :],
-                    me,
-                    parts,
-                    STRIDE * level + shift,
-                )
-                for piece, value in enumerate(tiles):
-                    value = pltpu.roll(value, turn, 0)
-                    span = slice(piece * LANES, (piece + 1) * LANES)
-                    buf[level, window, :, span] = value
-                    if n == 3:
-                        pong[level, window, :, span] = value
-                buf[level, window, at : at + n, :] = message[
-                    base + n * level : base + n * (level + 1), :
-                ]
+        for buf, n, base in ((ping, 3, 0), (src, 2, SOURCE_ROW)):
+            rows_of = slice(base + n * level, base + n * (level + 1))
+            buf[level, 0, 3 - n : 3, :] = before[rows_of, :]
+            buf[level, 1, 5 : 5 + n, :] = after[rows_of, :]
     rim_first = jnp.where(is_south, 0, LANES - RIM)
     column = STRIP_AT + jnp.where((lane >= rim_first + 3) & (lane < rim_first + RIM), 2, 1)
     rims = {}
@@ -559,7 +580,7 @@
                 up = pltpu.roll(now, 1, 0)
                 down = pltpu.roll(now, 7, 0)
                 if substep == 1:
-                    beyond_row = pong[level, window]
+                    beyond_row = window_old[level, window]
                     if window == 0:
                         down = jnp.where(sub == 7, pltpu.roll(beyond_row, 7, 0), down)
                     else:
@@ -718,9 +739,9 @@
 
 
 def merge(parts, band, ox_ref, oy_ref, late, step, nest, spread, beyond, *rest):
-    own = rest[:parts]
-    previous = rest[2 * parts - 1 : 2 * parts] + rest[parts : 2 * parts - 1]
-    out, nest_out, joined, corner, sem = rest[2 * parts :]
+    previous = rest[1 : parts + 1]
+    own = rest[:1] + rest[parts + 1 : 2 * parts]
+    out, nest_out, joined, corner, sem, merged, out_sems = rest[2 * parts :]
     levels, rows, cols = step.shape
     foot = own[0].shape[2]
     me = lax.axis_index("gy")
@@ -753,6 +774,7 @@
         joined[k, :, rows:, :] = own[k][...]
     lane = iota((rows, LANES), 1)
     row = iota((rows, LANES), 0)
+    stores = []
     for level in range(levels):
         values = [tile(step, level, piece) for piece in range(cols // LANES)]
         for k in range(parts):
@@ -768,7 +790,11 @@
         for piece, value in enumerate(values):
             term = late[level : level + 1, piece * LANES : (piece + 1) * LANES]
             value = value + jnp.where(row == rows - 2, term, 0.0)
-            out[level, :, piece * LANES : (piece + 1) * LANES] = value
+            merged[level, :, piece * LANES : (piece + 1) * LANES] = value
+        stores.append(pltpu.make_async_copy(merged.at[level], out.at[level], out_sems.at[level]))
+        stores[-1].start()
+    for copy in stores:
+        copy.wait()
 
 
 def shifted(value, axis, steps):
@@ -892,15 +918,17 @@
     )(nest_old, nest_old, nest_source, nest_source, parent_old, parent_old, own_strip, oy_rows, *columns)
     across = swapped(across, 1)
     within = swapped(within, 0)
-    third, packs, sums = pl.pallas_call(
-        inner_rest,
+    third, packs, window_old, window_src, sums = pl.pallas_call(
+        functools.partial(inner_rest, parts),
         out_shape=[
             shape(nest_old.shape, f32),
             shape((4, rows, LANES), f32),
+            shape((levels, 2, 8, width), f32),
+            shape((levels, 2, 8, width), f32),
             shape((cols // LANES, levels * parent_rows, LANES), f32),
         ],
-        in_specs=[scalars()] + [whole()] * 3 + [anywhere],
-        out_specs=[whole()] * 3,
+        in_specs=[scalars()] + [whole()] * 5 + [anywhere],
+        out_specs=[whole()] * 5,
         scratch_shapes=[
             VMEM(nest_old.shape, f32),
             VMEM((cols // LANES, levels * rows, LANES), f32),
@@ -908,7 +936,7 @@
         compiler_params=params(),
         cost_estimate=cost(8000000, 6000000),
         name="inner_rest",
-    )(nest_coefs, nest_old, first, nest_source, strips)
+    )(nest_coefs, nest_old, first, nest_source, columns[0], columns[-1], strips)
     sides, windows, coarse, far = pl.pallas_call(
         functools.partial(edges, parts, parent_cols),
         out_shape=[
@@ -931,10 +959,10 @@
     )(
         offset_x,
         spread,
-        nest_old,
-        nest_source,
         sums,
         packs,
+        window_old,
+        window_src,
         strips,
         across,
         within,
@@ -942,8 +970,8 @@
         columns[0],
         columns[-1],
     )
-    previous = [shifted_both(coarse, k) for k in range(1, parts)] + [shifted(coarse, along, 1)]
-    own = [coarse] + [shifted(coarse, "gy", k) for k in range(1, parts)]
+    previous = [shifted(coarse, along, 1)] + [shifted_both(coarse, k) for k in range(1, parts)]
+    beside = [shifted(coarse, "gy", k) for k in range(1, parts)]
     beyond = shifted(far, along, -2)
     step, nest_stored, late = pl.pallas_call(
         functools.partial(parent_step, parts, band),
@@ -980,17 +1008,19 @@
         functools.partial(merge, parts, band),
         out_shape=[shape(parent_old.shape, f32), shape(nest_old.shape, f32)],
         in_specs=[scalars()] * 2 + [whole()] * 2 + [in_hbm] + [whole()] * (2 + 2 * parts),
-        out_specs=[whole(), in_hbm],
+        out_specs=[in_hbm, in_hbm],
         scratch_shapes=[
             VMEM((parts, levels, 2 * parent_rows, foot), f32),
             VMEM((levels, 8, LANES), f32),
             pltpu.SemaphoreType.DMA,
+            VMEM(parent_old.shape, f32),
+            pltpu.SemaphoreType.DMA((levels,)),
         ],
         input_output_aliases={4: 1},
         compiler_params=params(),
         cost_estimate=cost(200000, 800000),
         name="merge",
-    )(offset_x, offset_y, late, step, nest_stored, spread, beyond, *own, *previous)
+    )(offset_x, offset_y, late, step, nest_stored, spread, beyond, coarse, *previous, *beside)
     return (parent_new, nest_new)
 
 

time: 24.5 us -> 24.5 us (level)
  no operation moved by 1% of the time
where the time goes in v3:
time: 24.5 us; the launch traced here: 24.3 us
  starting transfers between devices  11.5 us (47%)
  Pallas kernels  9.32 us (38%)
  between operations  2.12 us (9%)
  waiting for transfers between devices  1.39 us (6%)
    ppermute x4, starting transfers between devices, shifted(): return lax.ppermute(value, axis, pairs)  7.19 us
    ppermute x2, starting transfers between devices, swapped(): return lax.ppermute(value, along, pairs)  2.83 us
    pallas_call x1, Pallas kernels, shards(): pl.pallas_call(functools.partial(inner_rest, parts), out_shape=[shape(nes...  2.71 us
    pallas_call x1, Pallas kernels, shards(): pl.pallas_call(pack_pair, out_shape=VMEM((rows, LANES), f32), in_specs=[i...  1.56 us
    pallas_call x1, Pallas kernels, shards(): pl.pallas_call(functools.partial(inner_first, band), out_shape=[shape((pa...  1.51 us
    ppermute x1, starting transfers between devices, shifted_both(): return lax.ppermute(value, ('gx', 'gy', 'gz'), pairs)  1.44 us
    ppermute x1, waiting for transfers between devices, shifted_both(): return lax.ppermute(value, ('gx', 'gy', 'gz'), pairs)  1.38 us
    pallas_call x1, Pallas kernels, shards(): pl.pallas_call(functools.partial(parent_step, parts, band), out_shape=[sh...  1.36 us
  transfers between devices with their start and end apart: 7, of which 1 were waited for; matrix products, arithmetic and copies ran while one was open for 0% of the time, Pallas kernels for 23%

profile of v3, /device:TPU:0, one launch (start us, length us, event | category | flops | bytes accessed | tf_op | source)
XLA Modules:
  0.0 24.3 jit_solution(5231576394280984604)
XLA Ops:
  0.6 0.0 copy-start
  0.6 0.0 copy-start.1
  0.7 0.0 copy-start.2
  0.7 0.0 copy-start.3
  0.7 0.0 copy-start.5
  0.7 1.6 %pack_pair.1 = f32[72,128]{1,0:T(8,128)S(1)} custom-call(f32[8,72,384]{2,1,0:T(8,128)} %nest.5, f32[8,72,384]{2,1,0:T(8,128)} %source.6, f32[8,24,256]{2,1,0:T(8,128)} %parent.5, f32[8,24,256]{2,1,0:T(8,128)} %source.7), custom_call_target="tpu_custom_call" | custom-call | flops 200000 | bytes 800000 | tf_op jit(solution)/shard_map/pack_pair/pallas_call | solution.py:824
  2.2 0.0 copy-start.4
  2.3 3.0 %collective-permute-start = (f32[72,128]{1,0:T(8,128)S(1)}, f32[72,128]{1,0:T(8,128)S(1)}, u32[]{:S(2)}, u32[]{:S(2)}) collective-permute-start(f32[72,128]{1,0:T(8,128)S(1)} %pack_pair.1), channel_id=1, source_target_pairs={{0,2},{2,0},{1,3},{3,1},{4,6},{6,4},{5,7},{7,5},{8,10},{10,8},{9,1... | collective-permute-start | bytes 110600 | tf_op jit(solution)/shard_map/ppermute | solution.py:803
  5.9 0.0 copy-done
  5.9 0.0 copy-done.1
  5.9 0.0 copy-done.2
  5.9 0.0 copy-done.3
  6.0 0.0 copy-done.5
  6.0 0.0 copy-done.4
  6.0 1.5 %inner_first.1 = (f32[24,128]{1,0:T(8,128)S(1)}, f32[8,72,384]{2,1,0:T(8,128)S(1)}, f32[2,4,8,128]{3,2,1,0:T(8,128)S(1)}, s32[8,128]{1,0:T(8,128)S(1)}) custom-call(s32[1]{0:T(128)S(6)} %copy.13.oy_ref, f32[2,8]{1,0:T(2,128)S(1)} %copy-done.5, f32[2,8]{1,0:T(2,128)S(1)} %copy-done.4, f32[8,72,384]{2,1,0:T(8,128)S(1)} %copy-done, ...), custom_call_target="tpu_custom_call" | custom-call | flops 4000000 | bytes 3000000 | tf_op jit(solution)/shard_map/inner_first/pallas_call | solution.py:862
  7.5 0.0 collective-permute-done.rest_0_.y_left.y_right
  7.5 0.1 pack_rows.1
  7.7 2.8 %collective-permute-start.1 = (f32[56,384]{1,0:T(8,128)S(1)}, f32[56,384]{1,0:T(8,128)S(1)}, u32[]{:S(2)}, u32[]{:S(2)}) collective-permute-start(f32[56,384]{1,0:T(8,128)S(1)} %get-tuple-element.32), channel_id=1, source_target_pairs={{1,4},{4,1},{5,8},{8,5},{9,12},{12,9},{13,0},{0,13},{3,6},{6,3},{7... | collective-permute-start | bytes 258056 | tf_op jit(solution)/shard_map/ppermute | solution.py:1033
  10.5 0.0 collective-permute-start.2
  11.1 2.7 %inner_rest.1 = (f32[8,72,384]{2,1,0:T(8,128)S(1)}, f32[4,72,128]{2,1,0:T(8,128)S(1)}, f32[8,2,8,384]{3,2,1,0:T(8,128)S(1)}, f32[8,2,8,384]{3,2,1,0:T(8,128)S(1)}, f32[3,192,128]{2,1,0:T(8,128)S(1)}) custom-call(f32[2,8]{1,0:T(2,128)S(1)} %copy-done.4, f32[8,72,384]{2,1,0:T(8,128)S(1)} %copy-done, f32[8,72,384]{2,1,0:T(8,128)S(1)} %get-tuple-element.23.first, ...), custom_call_target="tpu_custom_call" | custom-call | flops 8000000 | bytes 6000000 | tf_op jit(solution)/shard_map/inner_rest/pallas_call | solution.py:921
  13.9 0.0 collective-permute-done.1.across
  13.9 0.0 collective-permute-done.2.within
  13.9 1.2 %edges.1 = (f32[2,72,128]{2,1,0:T(8,128)S(1)}, f32[8,2,8,384]{3,2,1,0:T(8,128)S(1)}, f32[8,24,128]{2,1,0:T(8,128)S(1)}, f32[8,128]{1,0:T(8,128)S(1)}) custom-call(s32[1]{0:T(128)S(6)} %copy.12.ox_ref, f32[2,4,8,128]{3,2,1,0:T(8,128)S(1)} %get-tuple-element.22.spread, f32[3,192,128]{2,1,0:T(8,128)S(1)} %get-tuple-element.28.sums, ...), custom_call_target="tpu_custom_call" | custom-call | flops 4000000 | bytes 3000000 | tf_op jit(solution)/shard_map/edges/pallas_call | solution.py:940
  15.1 0.6 %collective-permute-start.4 = (f32[8,24,128]{2,1,0:T(8,128)S(1)}, f32[8,24,128]{2,1,0:T(8,128)S(1)}, u32[]{:S(2)}, u32[]{:S(2)}) collective-permute-start(f32[8,24,128]{2,1,0:T(8,128)S(1)} %get-tuple-element.41.rest_0_), channel_id=1, source_target_pairs={{0,1},{1,4},{4,5},{5,8},{8,9},{9,12},{12,13},{13,0},{2,3},{3,6},{6... | collective-permute-start | bytes 294920 | tf_op jit(solution)/shard_map/ppermute | solution.py:803
  15.6 1.4 %collective-permute-start.5 = (f32[8,24,128]{2,1,0:T(8,128)S(1)}, f32[8,24,128]{2,1,0:T(8,128)S(1)}, u32[]{:S(2)}, u32[]{:S(2)}) collective-permute-start(f32[8,24,128]{2,1,0:T(8,128)S(1)} %get-tuple-element.41.rest_0_), channel_id=1, source_target_pairs={{0,3},{1,6},{2,1},{3,4},{4,7},{5,10},{6,5},{7,8},{8,11},{9,14},{10... | collective-permute-start | bytes 294920 | tf_op jit(solution)/shard_map/ppermute | solution.py:1046
  17.1 0.5 %collective-permute-start.6 = (f32[8,24,128]{2,1,0:T(8,128)S(1)}, f32[8,24,128]{2,1,0:T(8,128)S(1)}, u32[]{:S(2)}, u32[]{:S(2)}) collective-permute-start(f32[8,24,128]{2,1,0:T(8,128)S(1)} %get-tuple-element.41.rest_0_), channel_id=1, source_target_pairs={{0,2},{2,0},{1,3},{3,1},{4,6},{6,4},{5,7},{7,5},{8,10},{10,8},{9,1... | collective-permute-start | bytes 294920 | tf_op jit(solution)/shard_map/ppermute | solution.py:803
  17.6 3.1 %collective-permute-start.3 = (f32[8,128]{1,0:T(8,128)S(1)}, f32[8,128]{1,0:T(8,128)S(1)}, u32[]{:S(2)}, u32[]{:S(2)}) collective-permute-start(f32[8,128]{1,0:T(8,128)S(1)} %get-tuple-element.40), channel_id=1, source_target_pairs={{0,12},{1,13},{4,0},{5,1},{8,4},{9,5},{12,8},{13,9},{2,14},{3,15},... | collective-permute-start | bytes 12296 | tf_op jit(solution)/shard_map/ppermute | solution.py:803
  20.7 1.4 %parent_step.1 = (f32[8,24,256]{2,1,0:T(8,128)S(1)}, f32[8,72,384]{2,1,0:T(8,128)}, f32[8,256]{1,0:T(8,128)S(1)}) custom-call(s32[1]{0:T(128)S(6)} %copy.12.ox_ref, s32[1]{0:T(128)S(6)} %copy.13.oy_ref, f32[2,4,8,128]{3,2,1,0:T(8,128)S(1)} %get-tuple-element.22.spread, f32[8,72,384]{2,1,0:T(8,128)S(1)} %get-tuple-element.27.third, ...), custom_call_target="tpu_custom_call" | custom-call | flops 800000 | bytes 2500000 | tf_op jit(solution)/shard_map/parent_step/pallas_call | solution.py:976
  22.1 0.0 collective-permute-done.3.beyond
  22.1 0.0 collective-permute-done.4.rest_1_
  22.1 1.4 %collective-permute-done.5.rest_2_ = f32[8,24,128]{2,1,0:T(8,128)S(1)} collective-permute-done((f32[8,24,128]{2,1,0:T(8,128)S(1)}, f32[8,24,128]{2,1,0:T(8,128)S(1)}, u32[]{:S(2)}, u32[]{:S(2)}) %collective-permute-start.5) | collective-permute-done | bytes 98336 | tf_op jit(solution)/shard_map/ppermute | solution.py:1046
  23.5 0.0 collective-permute-done.6.rest_3_
  23.5 0.8 %merge.1 = (f32[8,24,256]{2,1,0:T(8,128)}, f32[8,72,384]{2,1,0:T(8,128)}) custom-call(s32[1]{0:T(128)S(6)} %copy.12.ox_ref, s32[1]{0:T(128)S(6)} %copy.13.oy_ref, f32[8,256]{1,0:T(8,128)S(1)} %get-tuple-element.37.late, f32[8,24,256]{2,1,0:T(8,128)S(1)} %get-tuple-element.38.step, ...), custom_call_target="tpu_custom_call", output_to_operand_aliasing={{1}: (4, {})} | custom-call | flops 200000 | bytes 800000 | tf_op jit(solution)/shard_map/merge/pallas_call | solution.py:1007
Async XLA Ops:
  0.6 5.3 %copy-start = (f32[8,72,384]{2,1,0:T(8,128)S(1)}, f32[8,72,384]{2,1,0:T(8,128)}, u32[]{:S(2)}) copy-start(f32[8,72,384]{2,1,0:T(8,128)} %nest.5) | copy-start | bytes 2654212
  0.6 5.3 %copy-start.1 = (f32[8,72,384]{2,1,0:T(8,128)S(1)}, f32[8,72,384]{2,1,0:T(8,128)}, u32[]{:S(2)}) copy-start(f32[8,72,384]{2,1,0:T(8,128)} %source.6) | copy-start | bytes 2654212
  0.7 5.3 %copy-start.2 = (f32[8,24,256]{2,1,0:T(8,128)S(1)}, f32[8,24,256]{2,1,0:T(8,128)}, u32[]{:S(2)}) copy-start(f32[8,24,256]{2,1,0:T(8,128)} %parent.5) | copy-start | bytes 589828
  0.7 5.3 %copy-start.3 = (f32[8,24,256]{2,1,0:T(8,128)S(1)}, f32[8,24,256]{2,1,0:T(8,128)}, u32[]{:S(2)}) copy-start(f32[8,24,256]{2,1,0:T(8,128)} %source.7) | copy-start | bytes 589828
  0.7 5.3 %copy-start.5 = (f32[2,8]{1,0:T(2,128)S(1)}, f32[2,8]{1,0:T(2,128)}, u32[]{:S(2)}) copy-start(f32[2,8]{1,0:T(2,128)} %parent_coefs.1) | copy-start | bytes 196
  2.2 3.7 %copy-start.4 = (f32[2,8]{1,0:T(2,128)S(1)}, f32[2,8]{1,0:T(2,128)}, u32[]{:S(2)}) copy-start(f32[2,8]{1,0:T(2,128)} %coefs.3) | copy-start | bytes 196
  2.3 5.2 %collective-permute-start = (f32[72,128]{1,0:T(8,128)S(1)}, f32[72,128]{1,0:T(8,128)S(1)}, u32[]{:S(2)}, u32[]{:S(2)}) collective-permute-start(f32[72,128]{1,0:T(8,128)S(1)} %pack_pair.1), channel_id=1, source_target_pairs={{0,2},{2,0},{1,3},{3,1},{4,6},{6,4},{5,7},{7,5},{8,10},{10,8},{9,1... | collective-permute-start | bytes 110600 | tf_op jit(solution)/shard_map/ppermute | solution.py:803
  7.7 6.2 %collective-permute-start.1 = (f32[56,384]{1,0:T(8,128)S(1)}, f32[56,384]{1,0:T(8,128)S(1)}, u32[]{:S(2)}, u32[]{:S(2)}) collective-permute-start(f32[56,384]{1,0:T(8,128)S(1)} %get-tuple-element.32), channel_id=1, source_target_pairs={{1,4},{4,1},{5,8},{8,5},{9,12},{12,9},{13,0},{0,13},{3,6},{6,3},{7... | collective-permute-start | bytes 258056 | tf_op jit(solution)/shard_map/ppermute | solution.py:1033
  10.5 3.4 %collective-permute-start.2 = (f32[56,384]{1,0:T(8,128)S(1)}, f32[56,384]{1,0:T(8,128)S(1)}, u32[]{:S(2)}, u32[]{:S(2)}) collective-permute-start(f32[56,384]{1,0:T(8,128)S(1)} %get-tuple-element.33), channel_id=1, source_target_pairs={{0,1},{1,0},{4,5},{5,4},{8,9},{9,8},{12,13},{13,12},{2,3},{3,2},{6... | collective-permute-start | bytes 258056 | tf_op jit(solution)/shard_map/ppermute | solution.py:1033
  15.1 7.0 %collective-permute-start.4 = (f32[8,24,128]{2,1,0:T(8,128)S(1)}, f32[8,24,128]{2,1,0:T(8,128)S(1)}, u32[]{:S(2)}, u32[]{:S(2)}) collective-permute-start(f32[8,24,128]{2,1,0:T(8,128)S(1)} %get-tuple-element.41.rest_0_), channel_id=1, source_target_pairs={{0,1},{1,4},{4,5},{5,8},{8,9},{9,12},{12,13},{13,0},{2,3},{3,6},{6... | collective-permute-start | bytes 294920 | tf_op jit(solution)/shard_map/ppermute | solution.py:803
  15.6 7.8 %collective-permute-start.5 = (f32[8,24,128]{2,1,0:T(8,128)S(1)}, f32[8,24,128]{2,1,0:T(8,128)S(1)}, u32[]{:S(2)}, u32[]{:S(2)}) collective-permute-start(f32[8,24,128]{2,1,0:T(8,128)S(1)} %get-tuple-element.41.rest_0_), channel_id=1, source_target_pairs={{0,3},{1,6},{2,1},{3,4},{4,7},{5,10},{6,5},{7,8},{8,11},{9,14},{10... | collective-permute-start | bytes 294920 | tf_op jit(solution)/shard_map/ppermute | solution.py:1046
  17.1 6.4 %collective-permute-start.6 = (f32[8,24,128]{2,1,0:T(8,128)S(1)}, f32[8,24,128]{2,1,0:T(8,128)S(1)}, u32[]{:S(2)}, u32[]{:S(2)}) collective-permute-start(f32[8,24,128]{2,1,0:T(8,128)S(1)} %get-tuple-element.41.rest_0_), channel_id=1, source_target_pairs={{0,2},{2,0},{1,3},{3,1},{4,6},{6,4},{5,7},{7,5},{8,10},{10,8},{9,1... | collective-permute-start | bytes 294920 | tf_op jit(solution)/shard_map/ppermute | solution.py:803
  17.6 4.5 %collective-permute-start.3 = (f32[8,128]{1,0:T(8,128)S(1)}, f32[8,128]{1,0:T(8,128)S(1)}, u32[]{:S(2)}, u32[]{:S(2)}) collective-permute-start(f32[8,128]{1,0:T(8,128)S(1)} %get-tuple-element.40), channel_id=1, source_target_pairs={{0,12},{1,13},{4,0},{5,1},{8,4},{9,5},{12,8},{13,9},{2,14},{3,15},... | collective-permute-start | bytes 12296 | tf_op jit(solution)/shard_map/ppermute | solution.py:803

commit v4 on v3

--- a/solution.py
+++ b/solution.py
@@ -739,11 +739,10 @@
 
 
 def merge(parts, band, ox_ref, oy_ref, late, step, nest, spread, beyond, *rest):
-    previous = rest[1 : parts + 1]
-    own = rest[:1] + rest[parts + 1 : 2 * parts]
+    arrived = rest[1 : 2 * parts]
     out, nest_out, joined, corner, sem, merged, out_sems = rest[2 * parts :]
     levels, rows, cols = step.shape
-    foot = own[0].shape[2]
+    foot = rest[0].shape[2]
     me = lax.axis_index("gy")
 
     @pl.when((ox_ref[0] == rows - 1) & ((me == 0) | (me == parts - 1)))
@@ -769,9 +768,17 @@
 
     ox = ox_ref[0]
     oy = oy_ref[0]
-    for k in range(parts):
-        joined[k, :, :rows, :] = previous[k][...]
-        joined[k, :, rows:, :] = own[k][...]
+    joined[0, :, rows:, :] = rest[0][...]
+    if parts == 2:
+        mixed, straight, other = arrived
+        joined[0, :, :rows, :] = straight[...]
+        joined[1, :, :rows, :] = jnp.where(me == 0, mixed[...], other[...])
+        joined[1, :, rows:, :] = jnp.where(me == 0, other[...], mixed[...])
+    else:
+        for k in range(parts):
+            joined[k, :, :rows, :] = arrived[k][...]
+        for k in range(1, parts):
+            joined[k, :, rows:, :] = arrived[parts + k - 1][...]
     lane = iota((rows, LANES), 1)
     row = iota((rows, LANES), 0)
     stores = []
@@ -970,8 +977,16 @@
         columns[0],
         columns[-1],
     )
-    previous = [shifted(coarse, along, 1)] + [shifted_both(coarse, k) for k in range(1, parts)]
-    beside = [shifted(coarse, "gy", k) for k in range(1, parts)]
+    if parts == 2:
+        arrived = [
+            shifted_both(coarse, 1, (0, 1)),
+            shifted(coarse, along, 1),
+            shifted_both(coarse, 1, (1, 0)),
+        ]
+    else:
+        arrived = [shifted(coarse, along, 1)]
+        arrived += [shifted_both(coarse, k) for k in range(1, parts)]
+        arrived += [shifted(coarse, "gy", k) for k in range(1, parts)]
     beyond = shifted(far, along, -2)
     step, nest_stored, late = pl.pallas_call(
         functools.partial(parent_step, parts, band),
@@ -1020,7 +1035,7 @@
         compiler_params=params(),
         cost_estimate=cost(200000, 800000),
         name="merge",
-    )(offset_x, offset_y, late, step, nest_stored, spread, beyond, coarse, *previous, *beside)
+    )(offset_x, offset_y, late, step, nest_stored, spread, beyond, coarse, *arrived)
     return (parent_new, nest_new)
 
 
@@ -1033,14 +1048,14 @@
     return lax.ppermute(value, along, pairs)
 
 
-def shifted_both(value, steps):
+def shifted_both(value, steps, rows=None):
     sizes = [lax.axis_size(axis) for axis in ("gx", "gy", "gz")]
     gx, gy, gz = sizes
     pairs = []
     for x in range(gx):
         for y in range(gy):
             for z in range(gz):
-                place = (x * gz + z + 1) % (gx * gz)
+                place = (x * gz + z + (1 if rows is None else rows[y])) % (gx * gz)
                 target = (place // gz * gy + (y + steps) % gy) * gz + place % gz
                 pairs.append(((x * gy + y) * gz + z, target))
     return lax.ppermute(value, ("gx", "gy", "gz"), pairs)

time: 24.5 us -> 24.3 us (level)
  waiting for transfers between devices: 1.39 us -> 1.06 us
    ppermute x1 -> x2, waiting for transfers between devices: 1.38 us -> 0.3 us  [shifted_both(): return lax.ppermute(value, ('gx', 'gy', 'gz'), pairs)]
    ppermute x4 -> x3, waiting for transfers between devices: 0.01 us -> 0.75 us  [shifted(): return lax.ppermute(value, axis, pairs)]
    ppermute x1 -> x2, starting transfers between devices: 1.44 us -> 2.13 us  [shifted_both(): return lax.ppermute(value, ('gx', 'gy', 'gz'), pairs)]
    ppermute x4 -> x3, starting transfers between devices: 7.19 us -> 6.61 us  [shifted(): return lax.ppermute(value, axis, pairs)]
  transfers between devices with their start and end apart: 7 -> 7, of which waited for: 1 -> 2; matrix products, arithmetic and copies ran while one was open for 0% -> 0% of each run, Pallas kernels for 23% -> 23%
where the time goes in v4:
time: 24.3 us; the launch traced here: 24.1 us
  starting transfers between devices  11.6 us (48%)
  Pallas kernels  9.33 us (38%)
  between operations  2.12 us (9%)
  waiting for transfers between devices  1.06 us (4%)
    ppermute x3, starting transfers between devices, shifted(): return lax.ppermute(value, axis, pairs)  6.61 us
    ppermute x2, starting transfers between devices, swapped(): return lax.ppermute(value, along, pairs)  2.83 us
    pallas_call x1, Pallas kernels, shards(): pl.pallas_call(functools.partial(inner_rest, parts), out_shape=[shape(nes...  2.71 us
    ppermute x2, starting transfers between devices, shifted_both(): return lax.ppermute(value, ('gx', 'gy', 'gz'), pairs)  2.13 us
    pallas_call x1, Pallas kernels, shards(): pl.pallas_call(pack_pair, out_shape=VMEM((rows, LANES), f32), in_specs=[i...  1.56 us
    pallas_call x1, Pallas kernels, shards(): pl.pallas_call(functools.partial(inner_first, band), out_shape=[shape((pa...  1.51 us
    pallas_call x1, Pallas kernels, shards(): pl.pallas_call(functools.partial(parent_step, parts, band), out_shape=[sh...  1.36 us
    pallas_call x1, Pallas kernels, shards(): pl.pallas_call(functools.partial(edges, parts, parent_cols), out_shape=[s...  1.2 us
  transfers between devices with their start and end apart: 7, of which 2 were waited for; matrix products, arithmetic and copies ran while one was open for 0% of the time, Pallas kernels for 23%

profile of v4, /device:TPU:0, one launch (start us, length us, event | category | flops | bytes accessed | tf_op | source)
XLA Modules:
  0.0 24.1 jit_solution(14680620606463999802)
XLA Ops:
  0.6 0.0 copy-start
  0.6 0.0 copy-start.1
  0.7 0.0 copy-start.2
  0.7 0.0 copy-start.3
  0.7 0.0 copy-start.5
  0.7 1.6 %pack_pair.1 = f32[72,128]{1,0:T(8,128)S(1)} custom-call(f32[8,72,384]{2,1,0:T(8,128)} %nest.5, f32[8,72,384]{2,1,0:T(8,128)} %source.6, f32[8,24,256]{2,1,0:T(8,128)} %parent.5, f32[8,24,256]{2,1,0:T(8,128)} %source.7), custom_call_target="tpu_custom_call" | custom-call | flops 200000 | bytes 800000 | tf_op jit(solution)/shard_map/pack_pair/pallas_call | solution.py:831
  2.2 0.0 copy-start.4
  2.3 3.0 %collective-permute-start = (f32[72,128]{1,0:T(8,128)S(1)}, f32[72,128]{1,0:T(8,128)S(1)}, u32[]{:S(2)}, u32[]{:S(2)}) collective-permute-start(f32[72,128]{1,0:T(8,128)S(1)} %pack_pair.1), channel_id=1, source_target_pairs={{0,2},{2,0},{1,3},{3,1},{4,6},{6,4},{5,7},{7,5},{8,10},{10,8},{9,1... | collective-permute-start | bytes 110600 | tf_op jit(solution)/shard_map/ppermute | solution.py:810
  5.9 0.0 copy-done
  5.9 0.0 copy-done.1
  5.9 0.0 copy-done.2
  5.9 0.0 copy-done.3
  6.0 0.0 copy-done.5
  6.0 0.0 copy-done.4
  6.0 1.5 %inner_first.1 = (f32[24,128]{1,0:T(8,128)S(1)}, f32[8,72,384]{2,1,0:T(8,128)S(1)}, f32[2,4,8,128]{3,2,1,0:T(8,128)S(1)}, s32[8,128]{1,0:T(8,128)S(1)}) custom-call(s32[1]{0:T(128)S(6)} %copy.13.oy_ref, f32[2,8]{1,0:T(2,128)S(1)} %copy-done.5, f32[2,8]{1,0:T(2,128)S(1)} %copy-done.4, f32[8,72,384]{2,1,0:T(8,128)S(1)} %copy-done, ...), custom_call_target="tpu_custom_call" | custom-call | flops 4000000 | bytes 3000000 | tf_op jit(solution)/shard_map/inner_first/pallas_call | solution.py:869
  7.5 0.0 collective-permute-done.rest_0_.y_left.y_right
  7.5 0.1 pack_rows.1
  7.7 2.8 %collective-permute-start.1 = (f32[56,384]{1,0:T(8,128)S(1)}, f32[56,384]{1,0:T(8,128)S(1)}, u32[]{:S(2)}, u32[]{:S(2)}) collective-permute-start(f32[56,384]{1,0:T(8,128)S(1)} %get-tuple-element.32), channel_id=1, source_target_pairs={{1,4},{4,1},{5,8},{8,5},{9,12},{12,9},{13,0},{0,13},{3,6},{6,3},{7... | collective-permute-start | bytes 258056 | tf_op jit(solution)/shard_map/ppermute | solution.py:1048
  10.5 0.0 collective-permute-start.2
  11.1 2.7 %inner_rest.1 = (f32[8,72,384]{2,1,0:T(8,128)S(1)}, f32[4,72,128]{2,1,0:T(8,128)S(1)}, f32[8,2,8,384]{3,2,1,0:T(8,128)S(1)}, f32[8,2,8,384]{3,2,1,0:T(8,128)S(1)}, f32[3,192,128]{2,1,0:T(8,128)S(1)}) custom-call(f32[2,8]{1,0:T(2,128)S(1)} %copy-done.4, f32[8,72,384]{2,1,0:T(8,128)S(1)} %copy-done, f32[8,72,384]{2,1,0:T(8,128)S(1)} %get-tuple-element.23.first, ...), custom_call_target="tpu_custom_call" | custom-call | flops 8000000 | bytes 6000000 | tf_op jit(solution)/shard_map/inner_rest/pallas_call | solution.py:928
  13.9 0.0 collective-permute-done.1.across
  13.9 0.0 collective-permute-done.2.within
  13.9 1.2 %edges.1 = (f32[2,72,128]{2,1,0:T(8,128)S(1)}, f32[8,2,8,384]{3,2,1,0:T(8,128)S(1)}, f32[8,24,128]{2,1,0:T(8,128)S(1)}, f32[8,128]{1,0:T(8,128)S(1)}) custom-call(s32[1]{0:T(128)S(6)} %copy.12.ox_ref, f32[2,4,8,128]{3,2,1,0:T(8,128)S(1)} %get-tuple-element.22.spread, f32[3,192,128]{2,1,0:T(8,128)S(1)} %get-tuple-element.28.sums, ...), custom_call_target="tpu_custom_call" | custom-call | flops 4000000 | bytes 3000000 | tf_op jit(solution)/shard_map/edges/pallas_call | solution.py:947
  15.1 2.0 %collective-permute-start.4 = (f32[8,24,128]{2,1,0:T(8,128)S(1)}, f32[8,24,128]{2,1,0:T(8,128)S(1)}, u32[]{:S(2)}, u32[]{:S(2)}) collective-permute-start(f32[8,24,128]{2,1,0:T(8,128)S(1)} %get-tuple-element.41.rest_0_), channel_id=1, source_target_pairs={{0,2},{1,3},{2,1},{3,4},{4,6},{5,7},{6,5},{7,8},{8,10},{9,11},{10,... | collective-permute-start | bytes 294920 | tf_op jit(solution)/shard_map/ppermute | solution.py:1061
  17.1 0.0 collective-permute-start.5
  17.1 0.2 collective-permute-start.6
  17.2 3.6 %collective-permute-start.3 = (f32[8,128]{1,0:T(8,128)S(1)}, f32[8,128]{1,0:T(8,128)S(1)}, u32[]{:S(2)}, u32[]{:S(2)}) collective-permute-start(f32[8,128]{1,0:T(8,128)S(1)} %get-tuple-element.40), channel_id=1, source_target_pairs={{0,12},{1,13},{4,0},{5,1},{8,4},{9,5},{12,8},{13,9},{2,14},{3,15},... | collective-permute-start | bytes 12296 | tf_op jit(solution)/shard_map/ppermute | solution.py:810
  20.8 1.4 %parent_step.1 = (f32[8,24,256]{2,1,0:T(8,128)S(1)}, f32[8,72,384]{2,1,0:T(8,128)}, f32[8,256]{1,0:T(8,128)S(1)}) custom-call(s32[1]{0:T(128)S(6)} %copy.12.ox_ref, s32[1]{0:T(128)S(6)} %copy.13.oy_ref, f32[2,4,8,128]{3,2,1,0:T(8,128)S(1)} %get-tuple-element.22.spread, f32[8,72,384]{2,1,0:T(8,128)S(1)} %get-tuple-element.27.third, ...), custom_call_target="tpu_custom_call" | custom-call | flops 800000 | bytes 2500000 | tf_op jit(solution)/shard_map/parent_step/pallas_call | solution.py:991
  22.2 0.0 collective-permute-done.3.beyond
  22.2 0.0 collective-permute-done.4.rest_1_
  22.2 0.7 %collective-permute-done.5.rest_2_ = f32[8,24,128]{2,1,0:T(8,128)S(1)} collective-permute-done((f32[8,24,128]{2,1,0:T(8,128)S(1)}, f32[8,24,128]{2,1,0:T(8,128)S(1)}, u32[]{:S(2)}, u32[]{:S(2)}) %collective-permute-start.5) | collective-permute-done | bytes 98336 | tf_op jit(solution)/shard_map/ppermute | solution.py:810
  22.9 0.3 %collective-permute-done.6.rest_3_ = f32[8,24,128]{2,1,0:T(8,128)S(1)} collective-permute-done((f32[8,24,128]{2,1,0:T(8,128)S(1)}, f32[8,24,128]{2,1,0:T(8,128)S(1)}, u32[]{:S(2)}, u32[]{:S(2)}) %collective-permute-start.6) | collective-permute-done | bytes 98336 | tf_op jit(solution)/shard_map/ppermute | solution.py:1061
  23.2 0.8 %merge.1 = (f32[8,24,256]{2,1,0:T(8,128)}, f32[8,72,384]{2,1,0:T(8,128)}) custom-call(s32[1]{0:T(128)S(6)} %copy.12.ox_ref, s32[1]{0:T(128)S(6)} %copy.13.oy_ref, f32[8,256]{1,0:T(8,128)S(1)} %get-tuple-element.37.late, f32[8,24,256]{2,1,0:T(8,128)S(1)} %get-tuple-element.38.step, ...), custom_call_target="tpu_custom_call", output_to_operand_aliasing={{1}: (4, {})} | custom-call | flops 200000 | bytes 800000 | tf_op jit(solution)/shard_map/merge/pallas_call | solution.py:1022
Async XLA Ops:
  0.6 5.3 %copy-start = (f32[8,72,384]{2,1,0:T(8,128)S(1)}, f32[8,72,384]{2,1,0:T(8,128)}, u32[]{:S(2)}) copy-start(f32[8,72,384]{2,1,0:T(8,128)} %nest.5) | copy-start | bytes 2654212
  0.6 5.3 %copy-start.1 = (f32[8,72,384]{2,1,0:T(8,128)S(1)}, f32[8,72,384]{2,1,0:T(8,128)}, u32[]{:S(2)}) copy-start(f32[8,72,384]{2,1,0:T(8,128)} %source.6) | copy-start | bytes 2654212
  0.7 5.3 %copy-start.2 = (f32[8,24,256]{2,1,0:T(8,128)S(1)}, f32[8,24,256]{2,1,0:T(8,128)}, u32[]{:S(2)}) copy-start(f32[8,24,256]{2,1,0:T(8,128)} %parent.5) | copy-start | bytes 589828
  0.7 5.3 %copy-start.3 = (f32[8,24,256]{2,1,0:T(8,128)S(1)}, f32[8,24,256]{2,1,0:T(8,128)}, u32[]{:S(2)}) copy-start(f32[8,24,256]{2,1,0:T(8,128)} %source.7) | copy-start | bytes 589828
  0.7 5.3 %copy-start.5 = (f32[2,8]{1,0:T(2,128)S(1)}, f32[2,8]{1,0:T(2,128)}, u32[]{:S(2)}) copy-start(f32[2,8]{1,0:T(2,128)} %parent_coefs.1) | copy-start | bytes 196
  2.2 3.7 %copy-start.4 = (f32[2,8]{1,0:T(2,128)S(1)}, f32[2,8]{1,0:T(2,128)}, u32[]{:S(2)}) copy-start(f32[2,8]{1,0:T(2,128)} %coefs.3) | copy-start | bytes 196
  2.3 5.2 %collective-permute-start = (f32[72,128]{1,0:T(8,128)S(1)}, f32[72,128]{1,0:T(8,128)S(1)}, u32[]{:S(2)}, u32[]{:S(2)}) collective-permute-start(f32[72,128]{1,0:T(8,128)S(1)} %pack_pair.1), channel_id=1, source_target_pairs={{0,2},{2,0},{1,3},{3,1},{4,6},{6,4},{5,7},{7,5},{8,10},{10,8},{9,1... | collective-permute-start | bytes 110600 | tf_op jit(solution)/shard_map/ppermute | solution.py:810
  7.7 6.2 %collective-permute-start.1 = (f32[56,384]{1,0:T(8,128)S(1)}, f32[56,384]{1,0:T(8,128)S(1)}, u32[]{:S(2)}, u32[]{:S(2)}) collective-permute-start(f32[56,384]{1,0:T(8,128)S(1)} %get-tuple-element.32), channel_id=1, source_target_pairs={{1,4},{4,1},{5,8},{8,5},{9,12},{12,9},{13,0},{0,13},{3,6},{6,3},{7... | collective-permute-start | bytes 258056 | tf_op jit(solution)/shard_map/ppermute | solution.py:1048
  10.5 3.4 %collective-permute-start.2 = (f32[56,384]{1,0:T(8,128)S(1)}, f32[56,384]{1,0:T(8,128)S(1)}, u32[]{:S(2)}, u32[]{:S(2)}) collective-permute-start(f32[56,384]{1,0:T(8,128)S(1)} %get-tuple-element.33), channel_id=1, source_target_pairs={{0,1},{1,0},{4,5},{5,4},{8,9},{9,8},{12,13},{13,12},{2,3},{3,2},{6... | collective-permute-start | bytes 258056 | tf_op jit(solution)/shard_map/ppermute | solution.py:1048
  15.1 7.1 %collective-permute-start.4 = (f32[8,24,128]{2,1,0:T(8,128)S(1)}, f32[8,24,128]{2,1,0:T(8,128)S(1)}, u32[]{:S(2)}, u32[]{:S(2)}) collective-permute-start(f32[8,24,128]{2,1,0:T(8,128)S(1)} %get-tuple-element.41.rest_0_), channel_id=1, source_target_pairs={{0,2},{1,3},{2,1},{3,4},{4,6},{5,7},{6,5},{7,8},{8,10},{9,11},{10,... | collective-permute-start | bytes 294920 | tf_op jit(solution)/shard_map/ppermute | solution.py:1061
  17.1 5.9 %collective-permute-start.5 = (f32[8,24,128]{2,1,0:T(8,128)S(1)}, f32[8,24,128]{2,1,0:T(8,128)S(1)}, u32[]{:S(2)}, u32[]{:S(2)}) collective-permute-start(f32[8,24,128]{2,1,0:T(8,128)S(1)} %get-tuple-element.41.rest_0_), channel_id=1, source_target_pairs={{0,1},{1,4},{4,5},{5,8},{8,9},{9,12},{12,13},{13,0},{2,3},{3,6},{6... | collective-permute-start | bytes 294920 | tf_op jit(solution)/shard_map/ppermute | solution.py:810
  17.1 6.2 %collective-permute-start.6 = (f32[8,24,128]{2,1,0:T(8,128)S(1)}, f32[8,24,128]{2,1,0:T(8,128)S(1)}, u32[]{:S(2)}, u32[]{:S(2)}) collective-permute-start(f32[8,24,128]{2,1,0:T(8,128)S(1)} %get-tuple-element.41.rest_0_), channel_id=1, source_target_pairs={{0,3},{1,6},{2,0},{3,1},{4,7},{5,10},{6,4},{7,5},{8,11},{9,14},{10... | collective-permute-start | bytes 294920 | tf_op jit(solution)/shard_map/ppermute | solution.py:1061
  17.2 5.0 %collective-permute-start.3 = (f32[8,128]{1,0:T(8,128)S(1)}, f32[8,128]{1,0:T(8,128)S(1)}, u32[]{:S(2)}, u32[]{:S(2)}) collective-permute-start(f32[8,128]{1,0:T(8,128)S(1)} %get-tuple-element.40), channel_id=1, source_target_pairs={{0,12},{1,13},{4,0},{5,1},{8,4},{9,5},{12,8},{13,9},{2,14},{3,15},... | collective-permute-start | bytes 12296 | tf_op jit(solution)/shard_map/ppermute | solution.py:810

commit v5 on v4

--- a/solution.py
+++ b/solution.py
@@ -75,19 +75,22 @@
     levels, rows, cols = nest.shape
     parent_rows, parent_cols = parent.shape[1:]
     right = lax.axis_index("gy") == 0
+    half = levels // 2
+    halves = [range(half), range(half, levels)]
+
+    def load(at, ref, buf):
+        start = pl.multiple_of(jnp.where(right, ref.shape[2] - LANES, 0), LANES)
+        copy = pltpu.make_async_copy(ref.at[:, :, pl.ds(start, LANES)], buf, sems.at[at])
+        copy.start()
+        return copy
+
     loads = []
-    for at, (ref, buf) in enumerate(
-        (
-            (parent, coarse_buf.at[0]),
-            (parent_source, coarse_buf.at[1]),
-            (nest, fine_buf.at[0]),
-            (source, fine_buf.at[1]),
-        )
-    ):
-        start = pl.multiple_of(jnp.where(right, ref.shape[2] - LANES, 0), LANES)
-        loads.append(pltpu.make_async_copy(ref.at[:, :, pl.ds(start, LANES)], buf, sems.at[at]))
-    for copy in loads:
-        copy.start()
+    for part in range(2):
+        span = pl.ds(part * half, half)
+        for at, ref in enumerate((nest, source)):
+            loads.append(load(2 * part + at, ref.at[span], fine_buf.at[at, span]))
+    for at, ref in enumerate((parent, parent_source)):
+        loads.append(load(4 + at, ref, coarse_buf.at[at]))
 
     def columns(value, count, to):
         first = jnp.where(right, LANES - count, 0)
@@ -95,23 +98,24 @@
         value = jnp.where((place >= 0) & (place < count), value, 0.0)
         return pltpu.roll(value, (LANES + to - first) & (LANES - 1), 1)
 
-    part = jnp.zeros((parent_rows, LANES), jnp.float32)
-    loads[0].wait()
-    loads[1].wait()
+    total = jnp.zeros((rows, LANES), jnp.float32)
+    for part in range(2):
+        loads[2 * part].wait()
+        loads[2 * part + 1].wait()
+        for level in halves[part]:
+            base = STRIDE * level
+            total = total + columns(fine_buf[0, level], 3, base)
+            total = total + columns(fine_buf[1, level], 3, base + SOURCE_AT)
+    part = total[:parent_rows]
+    loads[4].wait()
+    loads[5].wait()
     for level in range(levels):
         base = STRIDE * level
         part = part + columns(coarse_buf[0, level], 1, base + PARENT_AT)
         part = part + columns(coarse_buf[0, level], 2, base + STRIP_AT)
         part = part + columns(coarse_buf[1, level], 2, base + STRIP_SOURCE_AT)
-    total = jnp.zeros((rows, LANES), jnp.float32)
-    loads[2].wait()
-    loads[3].wait()
-    for level in range(levels):
-        base = STRIDE * level
-        total = total + columns(fine_buf[0, level], 3, base)
-        total = total + columns(fine_buf[1, level], 3, base + SOURCE_AT)
-    out[...] = total
-    out[:parent_rows, :] += part
+    out[:parent_rows, :] = part
+    out[parent_rows:, :] = total[parent_rows:]
 
 
 def across_border(message, oy, parent_cols, me):
@@ -836,7 +840,7 @@
                 scratch_shapes=[
                     VMEM((2, levels, rows, LANES), f32),
                     VMEM((2, levels, parent_rows, LANES), f32),
-                    pltpu.SemaphoreType.DMA((4,)),
+                    pltpu.SemaphoreType.DMA((6,)),
                 ],
                 compiler_params=params(MOST),
                 cost_estimate=cost(200000, 800000),

time: 24.3 us -> 24.3 us (level)
  no operation moved by 1% of the time
where the time goes in v5:
time: 24.3 us; the launch traced here: 24.2 us
  starting transfers between devices  11.6 us (48%)
  Pallas kernels  9.4 us (39%)
  between operations  2.12 us (9%)
  waiting for transfers between devices  1.06 us (4%)
    ppermute x3, starting transfers between devices, shifted(): return lax.ppermute(value, axis, pairs)  6.61 us
    ppermute x2, starting transfers between devices, swapped(): return lax.ppermute(value, along, pairs)  2.83 us
    pallas_call x1, Pallas kernels, shards(): pl.pallas_call(functools.partial(inner_rest, parts), out_shape=[shape(nes...  2.71 us
    ppermute x2, starting transfers between devices, shifted_both(): return lax.ppermute(value, ('gx', 'gy', 'gz'), pairs)  2.13 us
    pallas_call x1, Pallas kernels, shards(): pl.pallas_call(pack_pair, out_shape=VMEM((rows, LANES), f32), in_specs=[i...  1.63 us
    pallas_call x1, Pallas kernels, shards(): pl.pallas_call(functools.partial(inner_first, band), out_shape=[shape((pa...  1.51 us
    pallas_call x1, Pallas kernels, shards(): pl.pallas_call(functools.partial(parent_step, parts, band), out_shape=[sh...  1.36 us
    pallas_call x1, Pallas kernels, shards(): pl.pallas_call(functools.partial(edges, parts, parent_cols), out_shape=[s...  1.2 us
  transfers between devices with their start and end apart: 7, of which 2 were waited for; matrix products, arithmetic and copies ran while one was open for 0% of the time, Pallas kernels for 23%

profile of v5, /device:TPU:0, one launch (start us, length us, event | category | flops | bytes accessed | tf_op | source)
XLA Modules:
  0.0 24.2 jit_solution(9025947852312080127)
XLA Ops:
  0.6 0.0 copy-start
  0.6 0.0 copy-start.1
  0.7 0.0 copy-start.2
  0.7 0.0 copy-start.3
  0.7 0.0 copy-start.5
  0.7 1.6 %pack_pair.1 = f32[72,128]{1,0:T(8,128)S(1)} custom-call(f32[8,72,384]{2,1,0:T(8,128)} %nest.5, f32[8,72,384]{2,1,0:T(8,128)} %source.6, f32[8,24,256]{2,1,0:T(8,128)} %parent.5, f32[8,24,256]{2,1,0:T(8,128)} %source.7), custom_call_target="tpu_custom_call" | custom-call | flops 200000 | bytes 800000 | tf_op jit(solution)/shard_map/pack_pair/pallas_call | solution.py:835
  2.3 0.0 copy-start.4
  2.3 3.0 %collective-permute-start = (f32[72,128]{1,0:T(8,128)S(1)}, f32[72,128]{1,0:T(8,128)S(1)}, u32[]{:S(2)}, u32[]{:S(2)}) collective-permute-start(f32[72,128]{1,0:T(8,128)S(1)} %pack_pair.1), channel_id=1, source_target_pairs={{0,2},{2,0},{1,3},{3,1},{4,6},{6,4},{5,7},{7,5},{8,10},{10,8},{9,1... | collective-permute-start | bytes 110600 | tf_op jit(solution)/shard_map/ppermute | solution.py:814
  6.0 0.0 copy-done
  6.0 0.0 copy-done.1
  6.0 0.0 copy-done.2
  6.0 0.0 copy-done.3
  6.0 0.0 copy-done.5
  6.0 0.0 copy-done.4
  6.0 1.5 %inner_first.1 = (f32[24,128]{1,0:T(8,128)S(1)}, f32[8,72,384]{2,1,0:T(8,128)S(1)}, f32[2,4,8,128]{3,2,1,0:T(8,128)S(1)}, s32[8,128]{1,0:T(8,128)S(1)}) custom-call(s32[1]{0:T(128)S(6)} %copy.13.oy_ref, f32[2,8]{1,0:T(2,128)S(1)} %copy-done.5, f32[2,8]{1,0:T(2,128)S(1)} %copy-done.4, f32[8,72,384]{2,1,0:T(8,128)S(1)} %copy-done, ...), custom_call_target="tpu_custom_call" | custom-call | flops 4000000 | bytes 3000000 | tf_op jit(solution)/shard_map/inner_first/pallas_call | solution.py:873
  7.6 0.0 collective-permute-done.rest_0_.y_left.y_right
  7.6 0.1 pack_rows.1
  7.7 2.8 %collective-permute-start.1 = (f32[56,384]{1,0:T(8,128)S(1)}, f32[56,384]{1,0:T(8,128)S(1)}, u32[]{:S(2)}, u32[]{:S(2)}) collective-permute-start(f32[56,384]{1,0:T(8,128)S(1)} %get-tuple-element.32), channel_id=1, source_target_pairs={{1,4},{4,1},{5,8},{8,5},{9,12},{12,9},{13,0},{0,13},{3,6},{6,3},{7... | collective-permute-start | bytes 258056 | tf_op jit(solution)/shard_map/ppermute | solution.py:1052
  10.6 0.0 collective-permute-start.2
  11.2 2.7 %inner_rest.1 = (f32[8,72,384]{2,1,0:T(8,128)S(1)}, f32[4,72,128]{2,1,0:T(8,128)S(1)}, f32[8,2,8,384]{3,2,1,0:T(8,128)S(1)}, f32[8,2,8,384]{3,2,1,0:T(8,128)S(1)}, f32[3,192,128]{2,1,0:T(8,128)S(1)}) custom-call(f32[2,8]{1,0:T(2,128)S(1)} %copy-done.4, f32[8,72,384]{2,1,0:T(8,128)S(1)} %copy-done, f32[8,72,384]{2,1,0:T(8,128)S(1)} %get-tuple-element.23.first, ...), custom_call_target="tpu_custom_call" | custom-call | flops 8000000 | bytes 6000000 | tf_op jit(solution)/shard_map/inner_rest/pallas_call | solution.py:932
  13.9 0.0 collective-permute-done.1.across
  13.9 0.0 collective-permute-done.2.within
  13.9 1.2 %edges.1 = (f32[2,72,128]{2,1,0:T(8,128)S(1)}, f32[8,2,8,384]{3,2,1,0:T(8,128)S(1)}, f32[8,24,128]{2,1,0:T(8,128)S(1)}, f32[8,128]{1,0:T(8,128)S(1)}) custom-call(s32[1]{0:T(128)S(6)} %copy.12.ox_ref, f32[2,4,8,128]{3,2,1,0:T(8,128)S(1)} %get-tuple-element.22.spread, f32[3,192,128]{2,1,0:T(8,128)S(1)} %get-tuple-element.28.sums, ...), custom_call_target="tpu_custom_call" | custom-call | flops 4000000 | bytes 3000000 | tf_op jit(solution)/shard_map/edges/pallas_call | solution.py:951
  15.2 2.0 %collective-permute-start.4 = (f32[8,24,128]{2,1,0:T(8,128)S(1)}, f32[8,24,128]{2,1,0:T(8,128)S(1)}, u32[]{:S(2)}, u32[]{:S(2)}) collective-permute-start(f32[8,24,128]{2,1,0:T(8,128)S(1)} %get-tuple-element.41.rest_0_), channel_id=1, source_target_pairs={{0,2},{1,3},{2,1},{3,4},{4,6},{5,7},{6,5},{7,8},{8,10},{9,11},{10,... | collective-permute-start | bytes 294920 | tf_op jit(solution)/shard_map/ppermute | solution.py:1065
  17.1 0.0 collective-permute-start.5
  17.1 0.2 collective-permute-start.6
  17.3 3.6 %collective-permute-start.3 = (f32[8,128]{1,0:T(8,128)S(1)}, f32[8,128]{1,0:T(8,128)S(1)}, u32[]{:S(2)}, u32[]{:S(2)}) collective-permute-start(f32[8,128]{1,0:T(8,128)S(1)} %get-tuple-element.40), channel_id=1, source_target_pairs={{0,12},{1,13},{4,0},{5,1},{8,4},{9,5},{12,8},{13,9},{2,14},{3,15},... | collective-permute-start | bytes 12296 | tf_op jit(solution)/shard_map/ppermute | solution.py:814
  20.9 1.4 %parent_step.1 = (f32[8,24,256]{2,1,0:T(8,128)S(1)}, f32[8,72,384]{2,1,0:T(8,128)}, f32[8,256]{1,0:T(8,128)S(1)}) custom-call(s32[1]{0:T(128)S(6)} %copy.12.ox_ref, s32[1]{0:T(128)S(6)} %copy.13.oy_ref, f32[2,4,8,128]{3,2,1,0:T(8,128)S(1)} %get-tuple-element.22.spread, f32[8,72,384]{2,1,0:T(8,128)S(1)} %get-tuple-element.27.third, ...), custom_call_target="tpu_custom_call" | custom-call | flops 800000 | bytes 2500000 | tf_op jit(solution)/shard_map/parent_step/pallas_call | solution.py:995
  22.3 0.0 collective-permute-done.3.beyond
  22.3 0.0 collective-permute-done.4.rest_1_
  22.3 0.7 %collective-permute-done.5.rest_2_ = f32[8,24,128]{2,1,0:T(8,128)S(1)} collective-permute-done((f32[8,24,128]{2,1,0:T(8,128)S(1)}, f32[8,24,128]{2,1,0:T(8,128)S(1)}, u32[]{:S(2)}, u32[]{:S(2)}) %collective-permute-start.5) | collective-permute-done | bytes 98336 | tf_op jit(solution)/shard_map/ppermute | solution.py:814
  23.0 0.3 %collective-permute-done.6.rest_3_ = f32[8,24,128]{2,1,0:T(8,128)S(1)} collective-permute-done((f32[8,24,128]{2,1,0:T(8,128)S(1)}, f32[8,24,128]{2,1,0:T(8,128)S(1)}, u32[]{:S(2)}, u32[]{:S(2)}) %collective-permute-start.6) | collective-permute-done | bytes 98336 | tf_op jit(solution)/shard_map/ppermute | solution.py:1065
  23.3 0.8 %merge.1 = (f32[8,24,256]{2,1,0:T(8,128)}, f32[8,72,384]{2,1,0:T(8,128)}) custom-call(s32[1]{0:T(128)S(6)} %copy.12.ox_ref, s32[1]{0:T(128)S(6)} %copy.13.oy_ref, f32[8,256]{1,0:T(8,128)S(1)} %get-tuple-element.37.late, f32[8,24,256]{2,1,0:T(8,128)S(1)} %get-tuple-element.38.step, ...), custom_call_target="tpu_custom_call", output_to_operand_aliasing={{1}: (4, {})} | custom-call | flops 200000 | bytes 800000 | tf_op jit(solution)/shard_map/merge/pallas_call | solution.py:1026
Async XLA Ops:
  0.6 5.4 %copy-start = (f32[8,72,384]{2,1,0:T(8,128)S(1)}, f32[8,72,384]{2,1,0:T(8,128)}, u32[]{:S(2)}) copy-start(f32[8,72,384]{2,1,0:T(8,128)} %nest.5) | copy-start | bytes 2654212
  0.6 5.4 %copy-start.1 = (f32[8,72,384]{2,1,0:T(8,128)S(1)}, f32[8,72,384]{2,1,0:T(8,128)}, u32[]{:S(2)}) copy-start(f32[8,72,384]{2,1,0:T(8,128)} %source.6) | copy-start | bytes 2654212
  0.7 5.4 %copy-start.2 = (f32[8,24,256]{2,1,0:T(8,128)S(1)}, f32[8,24,256]{2,1,0:T(8,128)}, u32[]{:S(2)}) copy-start(f32[8,24,256]{2,1,0:T(8,128)} %parent.5) | copy-start | bytes 589828
  0.7 5.4 %copy-start.3 = (f32[8,24,256]{2,1,0:T(8,128)S(1)}, f32[8,24,256]{2,1,0:T(8,128)}, u32[]{:S(2)}) copy-start(f32[8,24,256]{2,1,0:T(8,128)} %source.7) | copy-start | bytes 589828
  0.7 5.4 %copy-start.5 = (f32[2,8]{1,0:T(2,128)S(1)}, f32[2,8]{1,0:T(2,128)}, u32[]{:S(2)}) copy-start(f32[2,8]{1,0:T(2,128)} %parent_coefs.1) | copy-start | bytes 196
  2.3 3.7 %copy-start.4 = (f32[2,8]{1,0:T(2,128)S(1)}, f32[2,8]{1,0:T(2,128)}, u32[]{:S(2)}) copy-start(f32[2,8]{1,0:T(2,128)} %coefs.3) | copy-start | bytes 196
  2.3 5.2 %collective-permute-start = (f32[72,128]{1,0:T(8,128)S(1)}, f32[72,128]{1,0:T(8,128)S(1)}, u32[]{:S(2)}, u32[]{:S(2)}) collective-permute-start(f32[72,128]{1,0:T(8,128)S(1)} %pack_pair.1), channel_id=1, source_target_pairs={{0,2},{2,0},{1,3},{3,1},{4,6},{6,4},{5,7},{7,5},{8,10},{10,8},{9,1... | collective-permute-start | bytes 110600 | tf_op jit(solution)/shard_map/ppermute | solution.py:814
  7.7 6.2 %collective-permute-start.1 = (f32[56,384]{1,0:T(8,128)S(1)}, f32[56,384]{1,0:T(8,128)S(1)}, u32[]{:S(2)}, u32[]{:S(2)}) collective-permute-start(f32[56,384]{1,0:T(8,128)S(1)} %get-tuple-element.32), channel_id=1, source_target_pairs={{1,4},{4,1},{5,8},{8,5},{9,12},{12,9},{13,0},{0,13},{3,6},{6,3},{7... | collective-permute-start | bytes 258056 | tf_op jit(solution)/shard_map/ppermute | solution.py:1052
  10.6 3.4 %collective-permute-start.2 = (f32[56,384]{1,0:T(8,128)S(1)}, f32[56,384]{1,0:T(8,128)S(1)}, u32[]{:S(2)}, u32[]{:S(2)}) collective-permute-start(f32[56,384]{1,0:T(8,128)S(1)} %get-tuple-element.33), channel_id=1, source_target_pairs={{0,1},{1,0},{4,5},{5,4},{8,9},{9,8},{12,13},{13,12},{2,3},{3,2},{6... | collective-permute-start | bytes 258056 | tf_op jit(solution)/shard_map/ppermute | solution.py:1052
  15.2 7.1 %collective-permute-start.4 = (f32[8,24,128]{2,1,0:T(8,128)S(1)}, f32[8,24,128]{2,1,0:T(8,128)S(1)}, u32[]{:S(2)}, u32[]{:S(2)}) collective-permute-start(f32[8,24,128]{2,1,0:T(8,128)S(1)} %get-tuple-element.41.rest_0_), channel_id=1, source_target_pairs={{0,2},{1,3},{2,1},{3,4},{4,6},{5,7},{6,5},{7,8},{8,10},{9,11},{10,... | collective-permute-start | bytes 294920 | tf_op jit(solution)/shard_map/ppermute | solution.py:1065
  17.1 5.9 %collective-permute-start.5 = (f32[8,24,128]{2,1,0:T(8,128)S(1)}, f32[8,24,128]{2,1,0:T(8,128)S(1)}, u32[]{:S(2)}, u32[]{:S(2)}) collective-permute-start(f32[8,24,128]{2,1,0:T(8,128)S(1)} %get-tuple-element.41.rest_0_), channel_id=1, source_target_pairs={{0,1},{1,4},{4,5},{5,8},{8,9},{9,12},{12,13},{13,0},{2,3},{3,6},{6... | collective-permute-start | bytes 294920 | tf_op jit(solution)/shard_map/ppermute | solution.py:814
  17.1 6.2 %collective-permute-start.6 = (f32[8,24,128]{2,1,0:T(8,128)S(1)}, f32[8,24,128]{2,1,0:T(8,128)S(1)}, u32[]{:S(2)}, u32[]{:S(2)}) collective-permute-start(f32[8,24,128]{2,1,0:T(8,128)S(1)} %get-tuple-element.41.rest_0_), channel_id=1, source_target_pairs={{0,3},{1,6},{2,0},{3,1},{4,7},{5,10},{6,4},{7,5},{8,11},{9,14},{10... | collective-permute-start | bytes 294920 | tf_op jit(solution)/shard_map/ppermute | solution.py:1065
  17.3 5.0 %collective-permute-start.3 = (f32[8,128]{1,0:T(8,128)S(1)}, f32[8,128]{1,0:T(8,128)S(1)}, u32[]{:S(2)}, u32[]{:S(2)}) collective-permute-start(f32[8,128]{1,0:T(8,128)S(1)} %get-tuple-element.40), channel_id=1, source_target_pairs={{0,12},{1,13},{4,0},{5,1},{8,4},{9,5},{12,8},{13,9},{2,14},{3,15},... | collective-permute-start | bytes 12296 | tf_op jit(solution)/shard_map/ppermute | solution.py:814

commit v6 on v4

--- a/solution.py
+++ b/solution.py
@@ -770,7 +770,7 @@
     oy = oy_ref[0]
     joined[0, :, rows:, :] = rest[0][...]
     if parts == 2:
-        mixed, straight, other = arrived
+        straight, mixed, other = arrived
         joined[0, :, :rows, :] = straight[...]
         joined[1, :, :rows, :] = jnp.where(me == 0, mixed[...], other[...])
         joined[1, :, rows:, :] = jnp.where(me == 0, other[...], mixed[...])
@@ -979,8 +979,8 @@
     )
     if parts == 2:
         arrived = [
+            shifted(coarse, along, 1),
             shifted_both(coarse, 1, (0, 1)),
-            shifted(coarse, along, 1),
             shifted_both(coarse, 1, (1, 0)),
         ]
     else:

time: 24.3 us -> 24.5 us (level)
  waiting for transfers between devices: 1.06 us -> 1.46 us
    ppermute x2, waiting for transfers between devices: 0.3 us -> 1.45 us  [shifted_both(): return lax.ppermute(value, ('gx', 'gy', 'gz'), pairs)]
    ppermute x3, waiting for transfers between devices: 0.75 us -> 0.01 us  [shifted(): return lax.ppermute(value, axis, pairs)]
    ppermute x2, starting transfers between devices: 2.13 us -> 1.52 us  [shifted_both(): return lax.ppermute(value, ('gx', 'gy', 'gz'), pairs)]
    ppermute x3, starting transfers between devices: 6.61 us -> 7.05 us  [shifted(): return lax.ppermute(value, axis, pairs)]
  transfers between devices with their start and end apart: 7 -> 7, of which waited for: 2 -> 1; matrix products, arithmetic and copies ran while one was open for 0% -> 0% of each run, Pallas kernels for 23% -> 23%
where the time goes in v6:
time: 24.5 us; the launch traced here: 24.3 us
  starting transfers between devices  11.4 us (47%)
  Pallas kernels  9.33 us (38%)
  between operations  2.12 us (9%)
  waiting for transfers between devices  1.46 us (6%)
    ppermute x3, starting transfers between devices, shifted(): return lax.ppermute(value, axis, pairs)  7.05 us
    ppermute x2, starting transfers between devices, swapped(): return lax.ppermute(value, along, pairs)  2.83 us
    pallas_call x1, Pallas kernels, shards(): pl.pallas_call(functools.partial(inner_rest, parts), out_shape=[shape(nes...  2.71 us
    pallas_call x1, Pallas kernels, shards(): pl.pallas_call(pack_pair, out_shape=VMEM((rows, LANES), f32), in_specs=[i...  1.56 us
    ppermute x2, starting transfers between devices, shifted_both(): return lax.ppermute(value, ('gx', 'gy', 'gz'), pairs)  1.52 us
    pallas_call x1, Pallas kernels, shards(): pl.pallas_call(functools.partial(inner_first, band), out_shape=[shape((pa...  1.51 us
    ppermute x2, waiting for transfers between devices, shifted_both(): return lax.ppermute(value, ('gx', 'gy', 'gz'), pairs)  1.45 us
    pallas_call x1, Pallas kernels, shards(): pl.pallas_call(functools.partial(parent_step, parts, band), out_shape=[sh...  1.36 us
  transfers between devices with their start and end apart: 7, of which 1 were waited for; matrix products, arithmetic and copies ran while one was open for 0% of the time, Pallas kernels for 23%

profile of v6, /device:TPU:0, one launch (start us, length us, event | category | flops | bytes accessed | tf_op | source)
XLA Modules:
  0.0 24.3 jit_solution(8089375757936454035)
XLA Ops:
  0.6 0.0 copy-start
  0.6 0.0 copy-start.1
  0.7 0.0 copy-start.2
  0.7 0.0 copy-start.3
  0.7 0.0 copy-start.5
  0.7 1.6 %pack_pair.1 = f32[72,128]{1,0:T(8,128)S(1)} custom-call(f32[8,72,384]{2,1,0:T(8,128)} %nest.5, f32[8,72,384]{2,1,0:T(8,128)} %source.6, f32[8,24,256]{2,1,0:T(8,128)} %parent.5, f32[8,24,256]{2,1,0:T(8,128)} %source.7), custom_call_target="tpu_custom_call" | custom-call | flops 200000 | bytes 800000 | tf_op jit(solution)/shard_map/pack_pair/pallas_call | solution.py:831
  2.2 0.0 copy-start.4
  2.3 3.0 %collective-permute-start = (f32[72,128]{1,0:T(8,128)S(1)}, f32[72,128]{1,0:T(8,128)S(1)}, u32[]{:S(2)}, u32[]{:S(2)}) collective-permute-start(f32[72,128]{1,0:T(8,128)S(1)} %pack_pair.1), channel_id=1, source_target_pairs={{0,2},{2,0},{1,3},{3,1},{4,6},{6,4},{5,7},{7,5},{8,10},{10,8},{9,1... | collective-permute-start | bytes 110600 | tf_op jit(solution)/shard_map/ppermute | solution.py:810
  5.9 0.0 copy-done
  5.9 0.0 copy-done.1
  5.9 0.0 copy-done.2
  5.9 0.0 copy-done.3
  6.0 0.0 copy-done.5
  6.0 0.0 copy-done.4
  6.0 1.5 %inner_first.1 = (f32[24,128]{1,0:T(8,128)S(1)}, f32[8,72,384]{2,1,0:T(8,128)S(1)}, f32[2,4,8,128]{3,2,1,0:T(8,128)S(1)}, s32[8,128]{1,0:T(8,128)S(1)}) custom-call(s32[1]{0:T(128)S(6)} %copy.13.oy_ref, f32[2,8]{1,0:T(2,128)S(1)} %copy-done.5, f32[2,8]{1,0:T(2,128)S(1)} %copy-done.4, f32[8,72,384]{2,1,0:T(8,128)S(1)} %copy-done, ...), custom_call_target="tpu_custom_call" | custom-call | flops 4000000 | bytes 3000000 | tf_op jit(solution)/shard_map/inner_first/pallas_call | solution.py:869
  7.5 0.0 collective-permute-done.rest_0_.y_left.y_right
  7.5 0.1 pack_rows.1
  7.7 2.8 %collective-permute-start.1 = (f32[56,384]{1,0:T(8,128)S(1)}, f32[56,384]{1,0:T(8,128)S(1)}, u32[]{:S(2)}, u32[]{:S(2)}) collective-permute-start(f32[56,384]{1,0:T(8,128)S(1)} %get-tuple-element.32), channel_id=1, source_target_pairs={{1,4},{4,1},{5,8},{8,5},{9,12},{12,9},{13,0},{0,13},{3,6},{6,3},{7... | collective-permute-start | bytes 258056 | tf_op jit(solution)/shard_map/ppermute | solution.py:1048
  10.5 0.0 collective-permute-start.2
  11.1 2.7 %inner_rest.1 = (f32[8,72,384]{2,1,0:T(8,128)S(1)}, f32[4,72,128]{2,1,0:T(8,128)S(1)}, f32[8,2,8,384]{3,2,1,0:T(8,128)S(1)}, f32[8,2,8,384]{3,2,1,0:T(8,128)S(1)}, f32[3,192,128]{2,1,0:T(8,128)S(1)}) custom-call(f32[2,8]{1,0:T(2,128)S(1)} %copy-done.4, f32[8,72,384]{2,1,0:T(8,128)S(1)} %copy-done, f32[8,72,384]{2,1,0:T(8,128)S(1)} %get-tuple-element.23.first, ...), custom_call_target="tpu_custom_call" | custom-call | flops 8000000 | bytes 6000000 | tf_op jit(solution)/shard_map/inner_rest/pallas_call | solution.py:928
  13.9 0.0 collective-permute-done.1.across
  13.9 0.0 collective-permute-done.2.within
  13.9 1.2 %edges.1 = (f32[2,72,128]{2,1,0:T(8,128)S(1)}, f32[8,2,8,384]{3,2,1,0:T(8,128)S(1)}, f32[8,24,128]{2,1,0:T(8,128)S(1)}, f32[8,128]{1,0:T(8,128)S(1)}) custom-call(s32[1]{0:T(128)S(6)} %copy.12.ox_ref, f32[2,4,8,128]{3,2,1,0:T(8,128)S(1)} %get-tuple-element.22.spread, f32[3,192,128]{2,1,0:T(8,128)S(1)} %get-tuple-element.28.sums, ...), custom_call_target="tpu_custom_call" | custom-call | flops 4000000 | bytes 3000000 | tf_op jit(solution)/shard_map/edges/pallas_call | solution.py:947
  15.1 0.6 %collective-permute-start.4 = (f32[8,24,128]{2,1,0:T(8,128)S(1)}, f32[8,24,128]{2,1,0:T(8,128)S(1)}, u32[]{:S(2)}, u32[]{:S(2)}) collective-permute-start(f32[8,24,128]{2,1,0:T(8,128)S(1)} %get-tuple-element.41.rest_0_), channel_id=1, source_target_pairs={{0,1},{1,4},{4,5},{5,8},{8,9},{9,12},{12,13},{13,0},{2,3},{3,6},{6... | collective-permute-start | bytes 294920 | tf_op jit(solution)/shard_map/ppermute | solution.py:810
  15.6 1.5 %collective-permute-start.5 = (f32[8,24,128]{2,1,0:T(8,128)S(1)}, f32[8,24,128]{2,1,0:T(8,128)S(1)}, u32[]{:S(2)}, u32[]{:S(2)}) collective-permute-start(f32[8,24,128]{2,1,0:T(8,128)S(1)} %get-tuple-element.41.rest_0_), channel_id=1, source_target_pairs={{0,2},{1,3},{2,1},{3,4},{4,6},{5,7},{6,5},{7,8},{8,10},{9,11},{10,... | collective-permute-start | bytes 294920 | tf_op jit(solution)/shard_map/ppermute | solution.py:1061
  17.1 0.0 collective-permute-start.6
  17.2 3.5 %collective-permute-start.3 = (f32[8,128]{1,0:T(8,128)S(1)}, f32[8,128]{1,0:T(8,128)S(1)}, u32[]{:S(2)}, u32[]{:S(2)}) collective-permute-start(f32[8,128]{1,0:T(8,128)S(1)} %get-tuple-element.40), channel_id=1, source_target_pairs={{0,12},{1,13},{4,0},{5,1},{8,4},{9,5},{12,8},{13,9},{2,14},{3,15},... | collective-permute-start | bytes 12296 | tf_op jit(solution)/shard_map/ppermute | solution.py:810
  20.6 1.4 %parent_step.1 = (f32[8,24,256]{2,1,0:T(8,128)S(1)}, f32[8,72,384]{2,1,0:T(8,128)}, f32[8,256]{1,0:T(8,128)S(1)}) custom-call(s32[1]{0:T(128)S(6)} %copy.12.ox_ref, s32[1]{0:T(128)S(6)} %copy.13.oy_ref, f32[2,4,8,128]{3,2,1,0:T(8,128)S(1)} %get-tuple-element.22.spread, f32[8,72,384]{2,1,0:T(8,128)S(1)} %get-tuple-element.27.third, ...), custom_call_target="tpu_custom_call" | custom-call | flops 800000 | bytes 2500000 | tf_op jit(solution)/shard_map/parent_step/pallas_call | solution.py:991
  22.0 0.0 collective-permute-done.3.beyond
  22.0 0.0 collective-permute-done.4.rest_1_
  22.0 1.4 %collective-permute-done.5.rest_2_ = f32[8,24,128]{2,1,0:T(8,128)S(1)} collective-permute-done((f32[8,24,128]{2,1,0:T(8,128)S(1)}, f32[8,24,128]{2,1,0:T(8,128)S(1)}, u32[]{:S(2)}, u32[]{:S(2)}) %collective-permute-start.5) | collective-permute-done | bytes 98336 | tf_op jit(solution)/shard_map/ppermute | solution.py:1061
  23.5 0.0 collective-permute-done.6.rest_3_
  23.5 0.8 %merge.1 = (f32[8,24,256]{2,1,0:T(8,128)}, f32[8,72,384]{2,1,0:T(8,128)}) custom-call(s32[1]{0:T(128)S(6)} %copy.12.ox_ref, s32[1]{0:T(128)S(6)} %copy.13.oy_ref, f32[8,256]{1,0:T(8,128)S(1)} %get-tuple-element.37.late, f32[8,24,256]{2,1,0:T(8,128)S(1)} %get-tuple-element.38.step, ...), custom_call_target="tpu_custom_call", output_to_operand_aliasing={{1}: (4, {})} | custom-call | flops 200000 | bytes 800000 | tf_op jit(solution)/shard_map/merge/pallas_call | solution.py:1022
Async XLA Ops:
  0.6 5.3 %copy-start = (f32[8,72,384]{2,1,0:T(8,128)S(1)}, f32[8,72,384]{2,1,0:T(8,128)}, u32[]{:S(2)}) copy-start(f32[8,72,384]{2,1,0:T(8,128)} %nest.5) | copy-start | bytes 2654212
  0.6 5.3 %copy-start.1 = (f32[8,72,384]{2,1,0:T(8,128)S(1)}, f32[8,72,384]{2,1,0:T(8,128)}, u32[]{:S(2)}) copy-start(f32[8,72,384]{2,1,0:T(8,128)} %source.6) | copy-start | bytes 2654212
  0.7 5.3 %copy-start.2 = (f32[8,24,256]{2,1,0:T(8,128)S(1)}, f32[8,24,256]{2,1,0:T(8,128)}, u32[]{:S(2)}) copy-start(f32[8,24,256]{2,1,0:T(8,128)} %parent.5) | copy-start | bytes 589828
  0.7 5.3 %copy-start.3 = (f32[8,24,256]{2,1,0:T(8,128)S(1)}, f32[8,24,256]{2,1,0:T(8,128)}, u32[]{:S(2)}) copy-start(f32[8,24,256]{2,1,0:T(8,128)} %source.7) | copy-start | bytes 589828
  0.7 5.3 %copy-start.5 = (f32[2,8]{1,0:T(2,128)S(1)}, f32[2,8]{1,0:T(2,128)}, u32[]{:S(2)}) copy-start(f32[2,8]{1,0:T(2,128)} %parent_coefs.1) | copy-start | bytes 196
  2.2 3.7 %copy-start.4 = (f32[2,8]{1,0:T(2,128)S(1)}, f32[2,8]{1,0:T(2,128)}, u32[]{:S(2)}) copy-start(f32[2,8]{1,0:T(2,128)} %coefs.3) | copy-start | bytes 196
  2.3 5.2 %collective-permute-start = (f32[72,128]{1,0:T(8,128)S(1)}, f32[72,128]{1,0:T(8,128)S(1)}, u32[]{:S(2)}, u32[]{:S(2)}) collective-permute-start(f32[72,128]{1,0:T(8,128)S(1)} %pack_pair.1), channel_id=1, source_target_pairs={{0,2},{2,0},{1,3},{3,1},{4,6},{6,4},{5,7},{7,5},{8,10},{10,8},{9,1... | collective-permute-start | bytes 110600 | tf_op jit(solution)/shard_map/ppermute | solution.py:810
  7.7 6.2 %collective-permute-start.1 = (f32[56,384]{1,0:T(8,128)S(1)}, f32[56,384]{1,0:T(8,128)S(1)}, u32[]{:S(2)}, u32[]{:S(2)}) collective-permute-start(f32[56,384]{1,0:T(8,128)S(1)} %get-tuple-element.32), channel_id=1, source_target_pairs={{1,4},{4,1},{5,8},{8,5},{9,12},{12,9},{13,0},{0,13},{3,6},{6,3},{7... | collective-permute-start | bytes 258056 | tf_op jit(solution)/shard_map/ppermute | solution.py:1048
  10.5 3.4 %collective-permute-start.2 = (f32[56,384]{1,0:T(8,128)S(1)}, f32[56,384]{1,0:T(8,128)S(1)}, u32[]{:S(2)}, u32[]{:S(2)}) collective-permute-start(f32[56,384]{1,0:T(8,128)S(1)} %get-tuple-element.33), channel_id=1, source_target_pairs={{0,1},{1,0},{4,5},{5,4},{8,9},{9,8},{12,13},{13,12},{2,3},{3,2},{6... | collective-permute-start | bytes 258056 | tf_op jit(solution)/shard_map/ppermute | solution.py:1048
  15.1 6.9 %collective-permute-start.4 = (f32[8,24,128]{2,1,0:T(8,128)S(1)}, f32[8,24,128]{2,1,0:T(8,128)S(1)}, u32[]{:S(2)}, u32[]{:S(2)}) collective-permute-start(f32[8,24,128]{2,1,0:T(8,128)S(1)} %get-tuple-element.41.rest_0_), channel_id=1, source_target_pairs={{0,1},{1,4},{4,5},{5,8},{8,9},{9,12},{12,13},{13,0},{2,3},{3,6},{6... | collective-permute-start | bytes 294920 | tf_op jit(solution)/shard_map/ppermute | solution.py:810
  15.6 7.8 %collective-permute-start.5 = (f32[8,24,128]{2,1,0:T(8,128)S(1)}, f32[8,24,128]{2,1,0:T(8,128)S(1)}, u32[]{:S(2)}, u32[]{:S(2)}) collective-permute-start(f32[8,24,128]{2,1,0:T(8,128)S(1)} %get-tuple-element.41.rest_0_), channel_id=1, source_target_pairs={{0,2},{1,3},{2,1},{3,4},{4,6},{5,7},{6,5},{7,8},{8,10},{9,11},{10,... | collective-permute-start | bytes 294920 | tf_op jit(solution)/shard_map/ppermute | solution.py:1061
  17.1 6.3 %collective-permute-start.6 = (f32[8,24,128]{2,1,0:T(8,128)S(1)}, f32[8,24,128]{2,1,0:T(8,128)S(1)}, u32[]{:S(2)}, u32[]{:S(2)}) collective-permute-start(f32[8,24,128]{2,1,0:T(8,128)S(1)} %get-tuple-element.41.rest_0_), channel_id=1, source_target_pairs={{0,3},{1,6},{2,0},{3,1},{4,7},{5,10},{6,4},{7,5},{8,11},{9,14},{10... | collective-permute-start | bytes 294920 | tf_op jit(solution)/shard_map/ppermute | solution.py:1061
  17.2 4.9 %collective-permute-start.3 = (f32[8,128]{1,0:T(8,128)S(1)}, f32[8,128]{1,0:T(8,128)S(1)}, u32[]{:S(2)}, u32[]{:S(2)}) collective-permute-start(f32[8,128]{1,0:T(8,128)S(1)} %get-tuple-element.40), channel_id=1, source_target_pairs={{0,12},{1,13},{4,0},{5,1},{8,4},{9,5},{12,8},{13,9},{2,14},{3,15},... | collective-permute-start | bytes 12296 | tf_op jit(solution)/shard_map/ppermute | solution.py:810

commit v7 on v4

--- a/solution.py
+++ b/solution.py
@@ -215,8 +215,7 @@
     return high + (middle + low)
 
 
-def sum_rows(ref):
-    count = ref.shape[0] // RATIO
+def sum_rows(ref, count):
     first, second, third = (ref[pl.ds(at, count, RATIO), :] for at in range(RATIO))
     return first + second + third
 
@@ -360,7 +359,7 @@
         for piece in range(cols // LANES):
             split[piece, level * rows : (level + 1) * rows, :] = tile(third, level, piece)
     for piece in range(cols // LANES):
-        sums[piece] = sum_rows(split.at[piece])
+        sums[piece] = sum_rows(split.at[piece], levels * rows // RATIO)
 
 
 def with_columns(tiles, left, right, me, parts, place):
@@ -460,7 +459,7 @@
 ):
     levels = ping.shape[0]
     width = ping.shape[3]
-    rows = sides.shape[1]
+    rows = packs.shape[1]
     cols = sums.shape[0] * LANES
     pieces = cols // LANES
     me = lax.axis_index("gy")
@@ -540,7 +539,7 @@
         for substep in range(1, SUBSTEPS + 1):
             value = centre * value + ch * around(value) + (cv * stacked(value) + forcing)
             value = jnp.where(rim, rim_old + (substep / SUBSTEPS) * rim_diff, value)
-        sides[side] = value
+        sides[side, :rows, :] = value
 
     sub = iota((8, width), 0)
     lane = iota((8, LANES), 1)
@@ -605,7 +604,7 @@
     parent_rows = rows // RATIO
     lane = iota((parent_rows, LANES), 1)
     row = iota((parent_rows, LANES), 0)
-    side_sums = [sum_rows(sides.at[side]) for side in range(2)]
+    side_sums = [sum_rows(sides.at[side], parent_rows) for side in range(2)]
     replaced = [[] for _ in range(pieces)]
     for level in range(levels):
         span = slice(level * parent_rows, (level + 1) * parent_rows)
@@ -638,11 +637,11 @@
     lane = iota((rows, LANES), 1)
     sub = iota((8, cols), 0)
     for level in range(levels):
-        fixed = turned(sides[0], -STRIDE * level - LEFT_AT)
+        fixed = turned(sides[0, :rows, :], -STRIDE * level - LEFT_AT)
         result[level, :, :LANES] = jnp.where(lane < FIXED, fixed, tile(third, level, 0))
         for piece in range(1, pieces - 1):
             result[level, :, piece * LANES : (piece + 1) * LANES] = tile(third, level, piece)
-        fixed = turned(sides[1], -STRIDE * level - RIGHT_OWN)
+        fixed = turned(sides[1, :rows, :], -STRIDE * level - RIGHT_OWN)
         result[level, :, cols - LANES :] = jnp.where(
             lane >= LANES - FIXED, fixed, tile(third, level, pieces - 1)
         )
@@ -938,7 +937,7 @@
         out_specs=[whole()] * 5,
         scratch_shapes=[
             VMEM(nest_old.shape, f32),
-            VMEM((cols // LANES, levels * rows, LANES), f32),
+            VMEM((cols // LANES, levels * rows + 8, LANES), f32),
         ],
         compiler_params=params(),
         cost_estimate=cost(8000000, 6000000),
@@ -947,7 +946,7 @@
     sides, windows, coarse, far = pl.pallas_call(
         functools.partial(edges, parts, parent_cols),
         out_shape=[
-            shape((2, rows, LANES), f32),
+            shape((2, rows + 8, LANES), f32),
             shape((levels, 2, 8, width), f32),
             shape((levels, parent_rows, foot), f32),
             shape((8, LANES), f32),

time: 24.3 us -> 24.2 us (level)
  no operation moved by 1% of the time
where the time goes in v7:
time: 24.2 us; the launch traced here: 24.1 us
  starting transfers between devices  11.6 us (48%)
  Pallas kernels  9.32 us (39%)
  between operations  2.12 us (9%)
  waiting for transfers between devices  1.05 us (4%)
    ppermute x3, starting transfers between devices, shifted(): return lax.ppermute(value, axis, pairs)  6.61 us
    ppermute x2, starting transfers between devices, swapped(): return lax.ppermute(value, along, pairs)  2.83 us
    pallas_call x1, Pallas kernels, shards(): pl.pallas_call(functools.partial(inner_rest, parts), out_shape=[shape(nes...  2.71 us
    ppermute x2, starting transfers between devices, shifted_both(): return lax.ppermute(value, ('gx', 'gy', 'gz'), pairs)  2.13 us
    pallas_call x1, Pallas kernels, shards(): pl.pallas_call(pack_pair, out_shape=VMEM((rows, LANES), f32), in_specs=[i...  1.56 us
    pallas_call x1, Pallas kernels, shards(): pl.pallas_call(functools.partial(inner_first, band), out_shape=[shape((pa...  1.51 us
    pallas_call x1, Pallas kernels, shards(): pl.pallas_call(functools.partial(parent_step, parts, band), out_shape=[sh...  1.36 us
    pallas_call x1, Pallas kernels, shards(): pl.pallas_call(functools.partial(edges, parts, parent_cols), out_shape=[s...  1.18 us
  transfers between devices with their start and end apart: 7, of which 2 were waited for; matrix products, arithmetic and copies ran while one was open for 0% of the time, Pallas kernels for 23%

profile of v7, /device:TPU:0, one launch (start us, length us, event | category | flops | bytes accessed | tf_op | source)
XLA Modules:
  0.0 24.1 jit_solution(13952299303133078672)
XLA Ops:
  0.6 0.0 copy-start
  0.6 0.0 copy-start.1
  0.7 0.0 copy-start.2
  0.7 0.0 copy-start.3
  0.7 0.0 copy-start.5
  0.7 1.6 %pack_pair.1 = f32[72,128]{1,0:T(8,128)S(1)} custom-call(f32[8,72,384]{2,1,0:T(8,128)} %nest.5, f32[8,72,384]{2,1,0:T(8,128)} %source.6, f32[8,24,256]{2,1,0:T(8,128)} %parent.5, f32[8,24,256]{2,1,0:T(8,128)} %source.7), custom_call_target="tpu_custom_call" | custom-call | flops 200000 | bytes 800000 | tf_op jit(solution)/shard_map/pack_pair/pallas_call | solution.py:830
  2.2 0.0 copy-start.4
  2.3 3.0 %collective-permute-start = (f32[72,128]{1,0:T(8,128)S(1)}, f32[72,128]{1,0:T(8,128)S(1)}, u32[]{:S(2)}, u32[]{:S(2)}) collective-permute-start(f32[72,128]{1,0:T(8,128)S(1)} %pack_pair.1), channel_id=1, source_target_pairs={{0,2},{2,0},{1,3},{3,1},{4,6},{6,4},{5,7},{7,5},{8,10},{10,8},{9,1... | collective-permute-start | bytes 110600 | tf_op jit(solution)/shard_map/ppermute | solution.py:809
  5.9 0.0 copy-done
  5.9 0.0 copy-done.1
  5.9 0.0 copy-done.2
  5.9 0.0 copy-done.3
  6.0 0.0 copy-done.5
  6.0 0.0 copy-done.4
  6.0 1.5 %inner_first.1 = (f32[24,128]{1,0:T(8,128)S(1)}, f32[8,72,384]{2,1,0:T(8,128)S(1)}, f32[2,4,8,128]{3,2,1,0:T(8,128)S(1)}, s32[8,128]{1,0:T(8,128)S(1)}) custom-call(s32[1]{0:T(128)S(6)} %copy.13.oy_ref, f32[2,8]{1,0:T(2,128)S(1)} %copy-done.5, f32[2,8]{1,0:T(2,128)S(1)} %copy-done.4, f32[8,72,384]{2,1,0:T(8,128)S(1)} %copy-done, ...), custom_call_target="tpu_custom_call" | custom-call | flops 4000000 | bytes 3000000 | tf_op jit(solution)/shard_map/inner_first/pallas_call | solution.py:868
  7.5 0.0 collective-permute-done.rest_0_.y_left.y_right
  7.5 0.1 pack_rows.1
  7.7 2.8 %collective-permute-start.1 = (f32[56,384]{1,0:T(8,128)S(1)}, f32[56,384]{1,0:T(8,128)S(1)}, u32[]{:S(2)}, u32[]{:S(2)}) collective-permute-start(f32[56,384]{1,0:T(8,128)S(1)} %get-tuple-element.32), channel_id=1, source_target_pairs={{1,4},{4,1},{5,8},{8,5},{9,12},{12,9},{13,0},{0,13},{3,6},{6,3},{7... | collective-permute-start | bytes 258056 | tf_op jit(solution)/shard_map/ppermute | solution.py:1047
  10.5 0.0 collective-permute-start.2
  11.1 2.7 %inner_rest.1 = (f32[8,72,384]{2,1,0:T(8,128)S(1)}, f32[4,72,128]{2,1,0:T(8,128)S(1)}, f32[8,2,8,384]{3,2,1,0:T(8,128)S(1)}, f32[8,2,8,384]{3,2,1,0:T(8,128)S(1)}, f32[3,192,128]{2,1,0:T(8,128)S(1)}) custom-call(f32[2,8]{1,0:T(2,128)S(1)} %copy-done.4, f32[8,72,384]{2,1,0:T(8,128)S(1)} %copy-done, f32[8,72,384]{2,1,0:T(8,128)S(1)} %get-tuple-element.23.first, ...), custom_call_target="tpu_custom_call" | custom-call | flops 8000000 | bytes 6000000 | tf_op jit(solution)/shard_map/inner_rest/pallas_call | solution.py:927
  13.9 0.0 collective-permute-done.1.across
  13.9 0.0 collective-permute-done.2.within
  13.9 1.2 %edges.1 = (f32[2,80,128]{2,1,0:T(8,128)S(1)}, f32[8,2,8,384]{3,2,1,0:T(8,128)S(1)}, f32[8,24,128]{2,1,0:T(8,128)S(1)}, f32[8,128]{1,0:T(8,128)S(1)}) custom-call(s32[1]{0:T(128)S(6)} %copy.12.ox_ref, f32[2,4,8,128]{3,2,1,0:T(8,128)S(1)} %get-tuple-element.22.spread, f32[3,192,128]{2,1,0:T(8,128)S(1)} %get-tuple-element.28.sums, ...), custom_call_target="tpu_custom_call" | custom-call | flops 4000000 | bytes 3000000 | tf_op jit(solution)/shard_map/edges/pallas_call | solution.py:946
  15.1 2.0 %collective-permute-start.4 = (f32[8,24,128]{2,1,0:T(8,128)S(1)}, f32[8,24,128]{2,1,0:T(8,128)S(1)}, u32[]{:S(2)}, u32[]{:S(2)}) collective-permute-start(f32[8,24,128]{2,1,0:T(8,128)S(1)} %get-tuple-element.41.rest_0_), channel_id=1, source_target_pairs={{0,2},{1,3},{2,1},{3,4},{4,6},{5,7},{6,5},{7,8},{8,10},{9,11},{10,... | collective-permute-start | bytes 294920 | tf_op jit(solution)/shard_map/ppermute | solution.py:1060
  17.0 0.0 collective-permute-start.5
  17.1 0.2 collective-permute-start.6
  17.2 3.6 %collective-permute-start.3 = (f32[8,128]{1,0:T(8,128)S(1)}, f32[8,128]{1,0:T(8,128)S(1)}, u32[]{:S(2)}, u32[]{:S(2)}) collective-permute-start(f32[8,128]{1,0:T(8,128)S(1)} %get-tuple-element.40), channel_id=1, source_target_pairs={{0,12},{1,13},{4,0},{5,1},{8,4},{9,5},{12,8},{13,9},{2,14},{3,15},... | collective-permute-start | bytes 12296 | tf_op jit(solution)/shard_map/ppermute | solution.py:809
  20.8 1.4 %parent_step.1 = (f32[8,24,256]{2,1,0:T(8,128)S(1)}, f32[8,72,384]{2,1,0:T(8,128)}, f32[8,256]{1,0:T(8,128)S(1)}) custom-call(s32[1]{0:T(128)S(6)} %copy.12.ox_ref, s32[1]{0:T(128)S(6)} %copy.13.oy_ref, f32[2,4,8,128]{3,2,1,0:T(8,128)S(1)} %get-tuple-element.22.spread, f32[8,72,384]{2,1,0:T(8,128)S(1)} %get-tuple-element.27.third, ...), custom_call_target="tpu_custom_call" | custom-call | flops 800000 | bytes 2500000 | tf_op jit(solution)/shard_map/parent_step/pallas_call | solution.py:990
  22.2 0.0 collective-permute-done.3.beyond
  22.2 0.0 collective-permute-done.4.rest_1_
  22.2 0.7 %collective-permute-done.5.rest_2_ = f32[8,24,128]{2,1,0:T(8,128)S(1)} collective-permute-done((f32[8,24,128]{2,1,0:T(8,128)S(1)}, f32[8,24,128]{2,1,0:T(8,128)S(1)}, u32[]{:S(2)}, u32[]{:S(2)}) %collective-permute-start.5) | collective-permute-done | bytes 98336 | tf_op jit(solution)/shard_map/ppermute | solution.py:809
  22.9 0.3 %collective-permute-done.6.rest_3_ = f32[8,24,128]{2,1,0:T(8,128)S(1)} collective-permute-done((f32[8,24,128]{2,1,0:T(8,128)S(1)}, f32[8,24,128]{2,1,0:T(8,128)S(1)}, u32[]{:S(2)}, u32[]{:S(2)}) %collective-permute-start.6) | collective-permute-done | bytes 98336 | tf_op jit(solution)/shard_map/ppermute | solution.py:1060
  23.2 0.8 %merge.1 = (f32[8,24,256]{2,1,0:T(8,128)}, f32[8,72,384]{2,1,0:T(8,128)}) custom-call(s32[1]{0:T(128)S(6)} %copy.12.ox_ref, s32[1]{0:T(128)S(6)} %copy.13.oy_ref, f32[8,256]{1,0:T(8,128)S(1)} %get-tuple-element.37.late, f32[8,24,256]{2,1,0:T(8,128)S(1)} %get-tuple-element.38.step, ...), custom_call_target="tpu_custom_call", output_to_operand_aliasing={{1}: (4, {})} | custom-call | flops 200000 | bytes 800000 | tf_op jit(solution)/shard_map/merge/pallas_call | solution.py:1021
Async XLA Ops:
  0.6 5.3 %copy-start = (f32[8,72,384]{2,1,0:T(8,128)S(1)}, f32[8,72,384]{2,1,0:T(8,128)}, u32[]{:S(2)}) copy-start(f32[8,72,384]{2,1,0:T(8,128)} %nest.5) | copy-start | bytes 2654212
  0.6 5.3 %copy-start.1 = (f32[8,72,384]{2,1,0:T(8,128)S(1)}, f32[8,72,384]{2,1,0:T(8,128)}, u32[]{:S(2)}) copy-start(f32[8,72,384]{2,1,0:T(8,128)} %source.6) | copy-start | bytes 2654212
  0.7 5.3 %copy-start.2 = (f32[8,24,256]{2,1,0:T(8,128)S(1)}, f32[8,24,256]{2,1,0:T(8,128)}, u32[]{:S(2)}) copy-start(f32[8,24,256]{2,1,0:T(8,128)} %parent.5) | copy-start | bytes 589828
  0.7 5.3 %copy-start.3 = (f32[8,24,256]{2,1,0:T(8,128)S(1)}, f32[8,24,256]{2,1,0:T(8,128)}, u32[]{:S(2)}) copy-start(f32[8,24,256]{2,1,0:T(8,128)} %source.7) | copy-start | bytes 589828
  0.7 5.3 %copy-start.5 = (f32[2,8]{1,0:T(2,128)S(1)}, f32[2,8]{1,0:T(2,128)}, u32[]{:S(2)}) copy-start(f32[2,8]{1,0:T(2,128)} %parent_coefs.1) | copy-start | bytes 196
  2.2 3.7 %copy-start.4 = (f32[2,8]{1,0:T(2,128)S(1)}, f32[2,8]{1,0:T(2,128)}, u32[]{:S(2)}) copy-start(f32[2,8]{1,0:T(2,128)} %coefs.3) | copy-start | bytes 196
  2.3 5.2 %collective-permute-start = (f32[72,128]{1,0:T(8,128)S(1)}, f32[72,128]{1,0:T(8,128)S(1)}, u32[]{:S(2)}, u32[]{:S(2)}) collective-permute-start(f32[72,128]{1,0:T(8,128)S(1)} %pack_pair.1), channel_id=1, source_target_pairs={{0,2},{2,0},{1,3},{3,1},{4,6},{6,4},{5,7},{7,5},{8,10},{10,8},{9,1... | collective-permute-start | bytes 110600 | tf_op jit(solution)/shard_map/ppermute | solution.py:809
  7.7 6.2 %collective-permute-start.1 = (f32[56,384]{1,0:T(8,128)S(1)}, f32[56,384]{1,0:T(8,128)S(1)}, u32[]{:S(2)}, u32[]{:S(2)}) collective-permute-start(f32[56,384]{1,0:T(8,128)S(1)} %get-tuple-element.32), channel_id=1, source_target_pairs={{1,4},{4,1},{5,8},{8,5},{9,12},{12,9},{13,0},{0,13},{3,6},{6,3},{7... | collective-permute-start | bytes 258056 | tf_op jit(solution)/shard_map/ppermute | solution.py:1047
  10.5 3.4 %collective-permute-start.2 = (f32[56,384]{1,0:T(8,128)S(1)}, f32[56,384]{1,0:T(8,128)S(1)}, u32[]{:S(2)}, u32[]{:S(2)}) collective-permute-start(f32[56,384]{1,0:T(8,128)S(1)} %get-tuple-element.33), channel_id=1, source_target_pairs={{0,1},{1,0},{4,5},{5,4},{8,9},{9,8},{12,13},{13,12},{2,3},{3,2},{6... | collective-permute-start | bytes 258056 | tf_op jit(solution)/shard_map/ppermute | solution.py:1047
  15.1 7.1 %collective-permute-start.4 = (f32[8,24,128]{2,1,0:T(8,128)S(1)}, f32[8,24,128]{2,1,0:T(8,128)S(1)}, u32[]{:S(2)}, u32[]{:S(2)}) collective-permute-start(f32[8,24,128]{2,1,0:T(8,128)S(1)} %get-tuple-element.41.rest_0_), channel_id=1, source_target_pairs={{0,2},{1,3},{2,1},{3,4},{4,6},{5,7},{6,5},{7,8},{8,10},{9,11},{10,... | collective-permute-start | bytes 294920 | tf_op jit(solution)/shard_map/ppermute | solution.py:1060
  17.0 5.9 %collective-permute-start.5 = (f32[8,24,128]{2,1,0:T(8,128)S(1)}, f32[8,24,128]{2,1,0:T(8,128)S(1)}, u32[]{:S(2)}, u32[]{:S(2)}) collective-permute-start(f32[8,24,128]{2,1,0:T(8,128)S(1)} %get-tuple-element.41.rest_0_), channel_id=1, source_target_pairs={{0,1},{1,4},{4,5},{5,8},{8,9},{9,12},{12,13},{13,0},{2,3},{3,6},{6... | collective-permute-start | bytes 294920 | tf_op jit(solution)/shard_map/ppermute | solution.py:809
  17.1 6.2 %collective-permute-start.6 = (f32[8,24,128]{2,1,0:T(8,128)S(1)}, f32[8,24,128]{2,1,0:T(8,128)S(1)}, u32[]{:S(2)}, u32[]{:S(2)}) collective-permute-start(f32[8,24,128]{2,1,0:T(8,128)S(1)} %get-tuple-element.41.rest_0_), channel_id=1, source_target_pairs={{0,3},{1,6},{2,0},{3,1},{4,7},{5,10},{6,4},{7,5},{8,11},{9,14},{10... | collective-permute-start | bytes 294920 | tf_op jit(solution)/shard_map/ppermute | solution.py:1060
  17.2 5.0 %collective-permute-start.3 = (f32[8,128]{1,0:T(8,128)S(1)}, f32[8,128]{1,0:T(8,128)S(1)}, u32[]{:S(2)}, u32[]{:S(2)}) collective-permute-start(f32[8,128]{1,0:T(8,128)S(1)} %get-tuple-element.40), channel_id=1, source_target_pairs={{0,12},{1,13},{4,0},{5,1},{8,4},{9,5},{12,8},{13,9},{2,14},{3,15},... | collective-permute-start | bytes 12296 | tf_op jit(solution)/shard_map/ppermute | solution.py:809

commit v8 on v7

--- a/solution.py
+++ b/solution.py
@@ -769,10 +769,10 @@
     oy = oy_ref[0]
     joined[0, :, rows:, :] = rest[0][...]
     if parts == 2:
-        mixed, straight, other = arrived
+        diagonal, straight, beside = arrived
         joined[0, :, :rows, :] = straight[...]
-        joined[1, :, :rows, :] = jnp.where(me == 0, mixed[...], other[...])
-        joined[1, :, rows:, :] = jnp.where(me == 0, other[...], mixed[...])
+        joined[1, :, :rows, :] = diagonal[...]
+        joined[1, :, rows:, :] = beside[...]
     else:
         for k in range(parts):
             joined[k, :, :rows, :] = arrived[k][...]
@@ -978,9 +978,9 @@
     )
     if parts == 2:
         arrived = [
-            shifted_both(coarse, 1, (0, 1)),
+            shifted_both(coarse, 1),
             shifted(coarse, along, 1),
-            shifted_both(coarse, 1, (1, 0)),
+            shifted(coarse, "gy", 1),
         ]
     else:
         arrived = [shifted(coarse, along, 1)]

time: 24.2 us -> 24.4 us (level)
  waiting for transfers between devices: 1.05 us -> 1.5 us
  starting transfers between devices: 11.6 us -> 11.3 us
    ppermute x2 -> x1, starting transfers between devices: 2.13 us -> 1 us  [shifted_both(): return lax.ppermute(value, ('gx', 'gy', 'gz'), pairs)]
    ppermute x3 -> x4, starting transfers between devices: 6.61 us -> 7.48 us  [shifted(): return lax.ppermute(value, axis, pairs)]
    ppermute x3 -> x4, waiting for transfers between devices: 0.74 us -> 1.45 us  [shifted(): return lax.ppermute(value, axis, pairs)]
    ppermute x2 -> x1, waiting for transfers between devices: 0.3 us -> 0.04 us  [shifted_both(): return lax.ppermute(value, ('gx', 'gy', 'gz'), pairs)]
  transfers between devices with their start and end apart: 7 -> 7, of which waited for: 2 -> 1; matrix products, arithmetic and copies ran while one was open for 0% -> 0% of each run, Pallas kernels for 23% -> 23%
where the time goes in v8:
time: 24.4 us; the launch traced here: 24.3 us
  starting transfers between devices  11.3 us (46%)
  Pallas kernels  9.32 us (38%)
  between operations  2.11 us (9%)
  waiting for transfers between devices  1.5 us (6%)
    ppermute x4, starting transfers between devices, shifted(): return lax.ppermute(value, axis, pairs)  7.48 us
    ppermute x2, starting transfers between devices, swapped(): return lax.ppermute(value, along, pairs)  2.83 us
    pallas_call x1, Pallas kernels, shards(): pl.pallas_call(functools.partial(inner_rest, parts), out_shape=[shape(nes...  2.71 us
    pallas_call x1, Pallas kernels, shards(): pl.pallas_call(pack_pair, out_shape=VMEM((rows, LANES), f32), in_specs=[i...  1.56 us
    pallas_call x1, Pallas kernels, shards(): pl.pallas_call(functools.partial(inner_first, band), out_shape=[shape((pa...  1.51 us
    ppermute x4, waiting for transfers between devices, shifted(): return lax.ppermute(value, axis, pairs)  1.45 us
    pallas_call x1, Pallas kernels, shards(): pl.pallas_call(functools.partial(parent_step, parts, band), out_shape=[sh...  1.36 us
    pallas_call x1, Pallas kernels, shards(): pl.pallas_call(functools.partial(edges, parts, parent_cols), out_shape=[s...  1.18 us
  transfers between devices with their start and end apart: 7, of which 1 were waited for; matrix products, arithmetic and copies ran while one was open for 0% of the time, Pallas kernels for 23%

profile of v8, /device:TPU:0, one launch (start us, length us, event | category | flops | bytes accessed | tf_op | source)
XLA Modules:
  0.0 24.3 jit_solution(2189345322647484921)
XLA Ops:
  0.6 0.0 copy-start
  0.6 0.0 copy-start.1
  0.7 0.0 copy-start.2
  0.7 0.0 copy-start.3
  0.7 0.0 copy-start.5
  0.7 1.6 %pack_pair.1 = f32[72,128]{1,0:T(8,128)S(1)} custom-call(f32[8,72,384]{2,1,0:T(8,128)} %nest.5, f32[8,72,384]{2,1,0:T(8,128)} %source.6, f32[8,24,256]{2,1,0:T(8,128)} %parent.5, f32[8,24,256]{2,1,0:T(8,128)} %source.7), custom_call_target="tpu_custom_call" | custom-call | flops 200000 | bytes 800000 | tf_op jit(solution)/shard_map/pack_pair/pallas_call | solution.py:830
  2.2 0.0 copy-start.4
  2.3 3.0 %collective-permute-start = (f32[72,128]{1,0:T(8,128)S(1)}, f32[72,128]{1,0:T(8,128)S(1)}, u32[]{:S(2)}, u32[]{:S(2)}) collective-permute-start(f32[72,128]{1,0:T(8,128)S(1)} %pack_pair.1), channel_id=1, source_target_pairs={{0,2},{2,0},{1,3},{3,1},{4,6},{6,4},{5,7},{7,5},{8,10},{10,8},{9,1... | collective-permute-start | bytes 110600 | tf_op jit(solution)/shard_map/ppermute | solution.py:809
  5.9 0.0 copy-done
  5.9 0.0 copy-done.1
  5.9 0.0 copy-done.2
  5.9 0.0 copy-done.3
  6.0 0.0 copy-done.5
  6.0 0.0 copy-done.4
  6.0 1.5 %inner_first.1 = (f32[24,128]{1,0:T(8,128)S(1)}, f32[8,72,384]{2,1,0:T(8,128)S(1)}, f32[2,4,8,128]{3,2,1,0:T(8,128)S(1)}, s32[8,128]{1,0:T(8,128)S(1)}) custom-call(s32[1]{0:T(128)S(6)} %copy.13.oy_ref, f32[2,8]{1,0:T(2,128)S(1)} %copy-done.5, f32[2,8]{1,0:T(2,128)S(1)} %copy-done.4, f32[8,72,384]{2,1,0:T(8,128)S(1)} %copy-done, ...), custom_call_target="tpu_custom_call" | custom-call | flops 4000000 | bytes 3000000 | tf_op jit(solution)/shard_map/inner_first/pallas_call | solution.py:868
  7.5 0.0 collective-permute-done.rest_0_.y_left.y_right
  7.5 0.1 pack_rows.1
  7.7 2.8 %collective-permute-start.1 = (f32[56,384]{1,0:T(8,128)S(1)}, f32[56,384]{1,0:T(8,128)S(1)}, u32[]{:S(2)}, u32[]{:S(2)}) collective-permute-start(f32[56,384]{1,0:T(8,128)S(1)} %get-tuple-element.32), channel_id=1, source_target_pairs={{1,4},{4,1},{5,8},{8,5},{9,12},{12,9},{13,0},{0,13},{3,6},{6,3},{7... | collective-permute-start | bytes 258056 | tf_op jit(solution)/shard_map/ppermute | solution.py:1047
  10.5 0.0 collective-permute-start.2
  11.1 2.7 %inner_rest.1 = (f32[8,72,384]{2,1,0:T(8,128)S(1)}, f32[4,72,128]{2,1,0:T(8,128)S(1)}, f32[8,2,8,384]{3,2,1,0:T(8,128)S(1)}, f32[8,2,8,384]{3,2,1,0:T(8,128)S(1)}, f32[3,192,128]{2,1,0:T(8,128)S(1)}) custom-call(f32[2,8]{1,0:T(2,128)S(1)} %copy-done.4, f32[8,72,384]{2,1,0:T(8,128)S(1)} %copy-done, f32[8,72,384]{2,1,0:T(8,128)S(1)} %get-tuple-element.23.first, ...), custom_call_target="tpu_custom_call" | custom-call | flops 8000000 | bytes 6000000 | tf_op jit(solution)/shard_map/inner_rest/pallas_call | solution.py:927
  13.9 0.0 collective-permute-done.1.across
  13.9 0.0 collective-permute-done.2.within
  13.9 1.2 %edges.1 = (f32[2,80,128]{2,1,0:T(8,128)S(1)}, f32[8,2,8,384]{3,2,1,0:T(8,128)S(1)}, f32[8,24,128]{2,1,0:T(8,128)S(1)}, f32[8,128]{1,0:T(8,128)S(1)}) custom-call(s32[1]{0:T(128)S(6)} %copy.12.ox_ref, f32[2,4,8,128]{3,2,1,0:T(8,128)S(1)} %get-tuple-element.22.spread, f32[3,192,128]{2,1,0:T(8,128)S(1)} %get-tuple-element.28.sums, ...), custom_call_target="tpu_custom_call" | custom-call | flops 4000000 | bytes 3000000 | tf_op jit(solution)/shard_map/edges/pallas_call | solution.py:946
  15.1 1.0 %collective-permute-start.4 = (f32[8,24,128]{2,1,0:T(8,128)S(1)}, f32[8,24,128]{2,1,0:T(8,128)S(1)}, u32[]{:S(2)}, u32[]{:S(2)}) collective-permute-start(f32[8,24,128]{2,1,0:T(8,128)S(1)} %get-tuple-element.41.rest_0_), channel_id=1, source_target_pairs={{0,3},{1,6},{2,1},{3,4},{4,7},{5,10},{6,5},{7,8},{8,11},{9,14},{10... | collective-permute-start | bytes 294920 | tf_op jit(solution)/shard_map/ppermute | solution.py:1060
  16.1 0.8 %collective-permute-start.5 = (f32[8,24,128]{2,1,0:T(8,128)S(1)}, f32[8,24,128]{2,1,0:T(8,128)S(1)}, u32[]{:S(2)}, u32[]{:S(2)}) collective-permute-start(f32[8,24,128]{2,1,0:T(8,128)S(1)} %get-tuple-element.41.rest_0_), channel_id=1, source_target_pairs={{0,1},{1,4},{4,5},{5,8},{8,9},{9,12},{12,13},{13,0},{2,3},{3,6},{6... | collective-permute-start | bytes 294920 | tf_op jit(solution)/shard_map/ppermute | solution.py:809
  16.9 0.5 %collective-permute-start.6 = (f32[8,24,128]{2,1,0:T(8,128)S(1)}, f32[8,24,128]{2,1,0:T(8,128)S(1)}, u32[]{:S(2)}, u32[]{:S(2)}) collective-permute-start(f32[8,24,128]{2,1,0:T(8,128)S(1)} %get-tuple-element.41.rest_0_), channel_id=1, source_target_pairs={{0,2},{2,0},{1,3},{3,1},{4,6},{6,4},{5,7},{7,5},{8,10},{10,8},{9,1... | collective-permute-start | bytes 294920 | tf_op jit(solution)/shard_map/ppermute | solution.py:809
  17.4 3.1 %collective-permute-start.3 = (f32[8,128]{1,0:T(8,128)S(1)}, f32[8,128]{1,0:T(8,128)S(1)}, u32[]{:S(2)}, u32[]{:S(2)}) collective-permute-start(f32[8,128]{1,0:T(8,128)S(1)} %get-tuple-element.40), channel_id=1, source_target_pairs={{0,12},{1,13},{4,0},{5,1},{8,4},{9,5},{12,8},{13,9},{2,14},{3,15},... | collective-permute-start | bytes 12296 | tf_op jit(solution)/shard_map/ppermute | solution.py:809
  20.6 1.4 %parent_step.1 = (f32[8,24,256]{2,1,0:T(8,128)S(1)}, f32[8,72,384]{2,1,0:T(8,128)}, f32[8,256]{1,0:T(8,128)S(1)}) custom-call(s32[1]{0:T(128)S(6)} %copy.12.ox_ref, s32[1]{0:T(128)S(6)} %copy.13.oy_ref, f32[2,4,8,128]{3,2,1,0:T(8,128)S(1)} %get-tuple-element.22.spread, f32[8,72,384]{2,1,0:T(8,128)S(1)} %get-tuple-element.27.third, ...), custom_call_target="tpu_custom_call" | custom-call | flops 800000 | bytes 2500000 | tf_op jit(solution)/shard_map/parent_step/pallas_call | solution.py:990
  21.9 0.0 collective-permute-done.3.beyond
  21.9 0.0 collective-permute-done.4.rest_1_
  22.0 1.4 %collective-permute-done.5.rest_2_ = f32[8,24,128]{2,1,0:T(8,128)S(1)} collective-permute-done((f32[8,24,128]{2,1,0:T(8,128)S(1)}, f32[8,24,128]{2,1,0:T(8,128)S(1)}, u32[]{:S(2)}, u32[]{:S(2)}) %collective-permute-start.5) | collective-permute-done | bytes 98336 | tf_op jit(solution)/shard_map/ppermute | solution.py:809
  23.4 0.0 collective-permute-done.6.rest_3_
  23.4 0.8 %merge.1 = (f32[8,24,256]{2,1,0:T(8,128)}, f32[8,72,384]{2,1,0:T(8,128)}) custom-call(s32[1]{0:T(128)S(6)} %copy.12.ox_ref, s32[1]{0:T(128)S(6)} %copy.13.oy_ref, f32[8,256]{1,0:T(8,128)S(1)} %get-tuple-element.37.late, f32[8,24,256]{2,1,0:T(8,128)S(1)} %get-tuple-element.38.step, ...), custom_call_target="tpu_custom_call", output_to_operand_aliasing={{1}: (4, {})} | custom-call | flops 200000 | bytes 800000 | tf_op jit(solution)/shard_map/merge/pallas_call | solution.py:1021
Async XLA Ops:
  0.6 5.3 %copy-start = (f32[8,72,384]{2,1,0:T(8,128)S(1)}, f32[8,72,384]{2,1,0:T(8,128)}, u32[]{:S(2)}) copy-start(f32[8,72,384]{2,1,0:T(8,128)} %nest.5) | copy-start | bytes 2654212
  0.6 5.3 %copy-start.1 = (f32[8,72,384]{2,1,0:T(8,128)S(1)}, f32[8,72,384]{2,1,0:T(8,128)}, u32[]{:S(2)}) copy-start(f32[8,72,384]{2,1,0:T(8,128)} %source.6) | copy-start | bytes 2654212
  0.7 5.3 %copy-start.2 = (f32[8,24,256]{2,1,0:T(8,128)S(1)}, f32[8,24,256]{2,1,0:T(8,128)}, u32[]{:S(2)}) copy-start(f32[8,24,256]{2,1,0:T(8,128)} %parent.5) | copy-start | bytes 589828
  0.7 5.3 %copy-start.3 = (f32[8,24,256]{2,1,0:T(8,128)S(1)}, f32[8,24,256]{2,1,0:T(8,128)}, u32[]{:S(2)}) copy-start(f32[8,24,256]{2,1,0:T(8,128)} %source.7) | copy-start | bytes 589828
  0.7 5.3 %copy-start.5 = (f32[2,8]{1,0:T(2,128)S(1)}, f32[2,8]{1,0:T(2,128)}, u32[]{:S(2)}) copy-start(f32[2,8]{1,0:T(2,128)} %parent_coefs.1) | copy-start | bytes 196
  2.2 3.7 %copy-start.4 = (f32[2,8]{1,0:T(2,128)S(1)}, f32[2,8]{1,0:T(2,128)}, u32[]{:S(2)}) copy-start(f32[2,8]{1,0:T(2,128)} %coefs.3) | copy-start | bytes 196
  2.3 5.2 %collective-permute-start = (f32[72,128]{1,0:T(8,128)S(1)}, f32[72,128]{1,0:T(8,128)S(1)}, u32[]{:S(2)}, u32[]{:S(2)}) collective-permute-start(f32[72,128]{1,0:T(8,128)S(1)} %pack_pair.1), channel_id=1, source_target_pairs={{0,2},{2,0},{1,3},{3,1},{4,6},{6,4},{5,7},{7,5},{8,10},{10,8},{9,1... | collective-permute-start | bytes 110600 | tf_op jit(solution)/shard_map/ppermute | solution.py:809
  7.7 6.2 %collective-permute-start.1 = (f32[56,384]{1,0:T(8,128)S(1)}, f32[56,384]{1,0:T(8,128)S(1)}, u32[]{:S(2)}, u32[]{:S(2)}) collective-permute-start(f32[56,384]{1,0:T(8,128)S(1)} %get-tuple-element.32), channel_id=1, source_target_pairs={{1,4},{4,1},{5,8},{8,5},{9,12},{12,9},{13,0},{0,13},{3,6},{6,3},{7... | collective-permute-start | bytes 258056 | tf_op jit(solution)/shard_map/ppermute | solution.py:1047
  10.5 3.4 %collective-permute-start.2 = (f32[56,384]{1,0:T(8,128)S(1)}, f32[56,384]{1,0:T(8,128)S(1)}, u32[]{:S(2)}, u32[]{:S(2)}) collective-permute-start(f32[56,384]{1,0:T(8,128)S(1)} %get-tuple-element.33), channel_id=1, source_target_pairs={{0,1},{1,0},{4,5},{5,4},{8,9},{9,8},{12,13},{13,12},{2,3},{3,2},{6... | collective-permute-start | bytes 258056 | tf_op jit(solution)/shard_map/ppermute | solution.py:1047
  15.1 6.9 %collective-permute-start.4 = (f32[8,24,128]{2,1,0:T(8,128)S(1)}, f32[8,24,128]{2,1,0:T(8,128)S(1)}, u32[]{:S(2)}, u32[]{:S(2)}) collective-permute-start(f32[8,24,128]{2,1,0:T(8,128)S(1)} %get-tuple-element.41.rest_0_), channel_id=1, source_target_pairs={{0,3},{1,6},{2,1},{3,4},{4,7},{5,10},{6,5},{7,8},{8,11},{9,14},{10... | collective-permute-start | bytes 294920 | tf_op jit(solution)/shard_map/ppermute | solution.py:1060
  16.1 7.3 %collective-permute-start.5 = (f32[8,24,128]{2,1,0:T(8,128)S(1)}, f32[8,24,128]{2,1,0:T(8,128)S(1)}, u32[]{:S(2)}, u32[]{:S(2)}) collective-permute-start(f32[8,24,128]{2,1,0:T(8,128)S(1)} %get-tuple-element.41.rest_0_), channel_id=1, source_target_pairs={{0,1},{1,4},{4,5},{5,8},{8,9},{9,12},{12,13},{13,0},{2,3},{3,6},{6... | collective-permute-start | bytes 294920 | tf_op jit(solution)/shard_map/ppermute | solution.py:809
  16.9 6.5 %collective-permute-start.6 = (f32[8,24,128]{2,1,0:T(8,128)S(1)}, f32[8,24,128]{2,1,0:T(8,128)S(1)}, u32[]{:S(2)}, u32[]{:S(2)}) collective-permute-start(f32[8,24,128]{2,1,0:T(8,128)S(1)} %get-tuple-element.41.rest_0_), channel_id=1, source_target_pairs={{0,2},{2,0},{1,3},{3,1},{4,6},{6,4},{5,7},{7,5},{8,10},{10,8},{9,1... | collective-permute-start | bytes 294920 | tf_op jit(solution)/shard_map/ppermute | solution.py:809
  17.4 4.5 %collective-permute-start.3 = (f32[8,128]{1,0:T(8,128)S(1)}, f32[8,128]{1,0:T(8,128)S(1)}, u32[]{:S(2)}, u32[]{:S(2)}) collective-permute-start(f32[8,128]{1,0:T(8,128)S(1)} %get-tuple-element.40), channel_id=1, source_target_pairs={{0,12},{1,13},{4,0},{5,1},{8,4},{9,5},{12,8},{13,9},{2,14},{3,15},... | collective-permute-start | bytes 12296 | tf_op jit(solution)/shard_map/ppermute | solution.py:809

commit v9 on v7

--- a/solution.py
+++ b/solution.py
@@ -280,7 +280,6 @@
 def inner_first(
     band,
     oy_ref,
-    parent_coefs,
     coefs,
     nest,
     source,
@@ -288,12 +287,10 @@
     parent_source,
     strip,
     first,
-    spread,
     oy_rows,
 ):
     oy = oy_ref[0]
     oy_rows[...] = jnp.full(oy_rows.shape, oy, jnp.int32)
-    spread_coefs(parent_coefs, coefs, spread)
     strip[...] = edge_strip(lax.axis_index("gy"), band, oy, parent, parent_source)
     inner_substep(coefs, nest, source, first)
 
@@ -325,6 +322,7 @@
 
 def inner_rest(
     parts,
+    parent_coefs,
     coefs,
     nest,
     first,
@@ -337,10 +335,12 @@
     window_old,
     window_src,
     sums,
+    spread,
     second,
     split,
 ):
     levels, rows, cols = nest.shape
+    spread_coefs(parent_coefs, coefs, spread)
     own_windows(parts, nest, source, y_left, y_right, window_old, window_src)
     lane = iota((rows, LANES), 1)
     for at, ref in enumerate((nest, source)):
@@ -586,10 +586,8 @@
                         up = jnp.where(sub == 0, pltpu.roll(beyond_row, 1, 0), up)
                 beside = pltpu.roll(now, 1, 1) + pltpu.roll(now, width - 1, 1)
                 value = c_0 * now + c_h * ((up + down) + beside) + src[level, window]
-                if level > 0:
-                    value = value + c_v * here[level - 1, window]
-                if level < levels - 1:
-                    value = value + c_v * here[level + 1, window]
+                near = [here[at, window] for at in (level - 1, level + 1) if 0 <= at < levels]
+                value = value + c_v * sum(near[1:], near[0])
                 rim_o, rim_d = rims[level, window]
                 rim = rim_o + weight * rim_d
                 for piece in range(width // LANES):
@@ -865,22 +863,20 @@
             name="pack_columns",
         )(offset_y, nest_old, nest_source, parent_old, parent_source)
     columns = [shifted(packed[k - 1], "gy", k) for k in range(1, parts)]
-    own_strip, first, spread, oy_rows = pl.pallas_call(
+    own_strip, first, oy_rows = pl.pallas_call(
         functools.partial(inner_first, band),
         out_shape=[
             shape((parent_rows, LANES), f32),
             shape(nest_old.shape, f32),
-            shape((2, 4, levels, LANES), f32),
             shape((8, LANES), jnp.int32),
         ],
-        in_specs=[scalars()] * 3 + [whole()] * 4,
-        out_specs=[whole()] * 4,
+        in_specs=[scalars()] * 2 + [whole()] * 4,
+        out_specs=[whole()] * 3,
         compiler_params=params(),
         cost_estimate=cost(4000000, 3000000),
         name="inner_first",
     )(
         offset_y,
-        parent_coefs,
         nest_coefs,
         nest_old,
         nest_source,
@@ -924,7 +920,7 @@
     )(nest_old, nest_old, nest_source, nest_source, parent_old, parent_old, own_strip, oy_rows, *columns)
     across = swapped(across, 1)
     within = swapped(within, 0)
-    third, packs, window_old, window_src, sums = pl.pallas_call(
+    third, packs, window_old, window_src, sums, spread = pl.pallas_call(
         functools.partial(inner_rest, parts),
         out_shape=[
             shape(nest_old.shape, f32),
@@ -932,9 +928,10 @@
             shape((levels, 2, 8, width), f32),
             shape((levels, 2, 8, width), f32),
             shape((cols // LANES, levels * parent_rows, LANES), f32),
+            shape((2, 4, levels, LANES), f32),
         ],
-        in_specs=[scalars()] + [whole()] * 5 + [anywhere],
-        out_specs=[whole()] * 5,
+        in_specs=[scalars()] * 2 + [whole()] * 5 + [anywhere],
+        out_specs=[whole()] * 6,
         scratch_shapes=[
             VMEM(nest_old.shape, f32),
             VMEM((cols // LANES, levels * rows + 8, LANES), f32),
@@ -942,7 +939,7 @@
         compiler_params=params(),
         cost_estimate=cost(8000000, 6000000),
         name="inner_rest",
-    )(nest_coefs, nest_old, first, nest_source, columns[0], columns[-1], strips)
+    )(parent_coefs, nest_coefs, nest_old, first, nest_source, columns[0], columns[-1], strips)
     sides, windows, coarse, far = pl.pallas_call(
         functools.partial(edges, parts, parent_cols),
         out_shape=[

time: 24.2 us -> 25 us (1.033); the launches traced: 24.1 us -> 24.6 us
  local copies, waits for them, and re-layouts: 0.03 us -> 0.7 us
  waiting for transfers between devices: 1.05 us -> 0.79 us
    unnamed x12, local copies, waits for them, and re-layouts: 0.03 us -> 0.7 us
    ppermute x3, waiting for transfers between devices: 0.74 us -> 0.11 us  [shifted(): return lax.ppermute(value, axis, pairs)]
    ppermute x2, waiting for transfers between devices: 0.3 us -> 0.68 us  [shifted_both(): return lax.ppermute(value, ('gx', 'gy', 'gz'), pairs)]
where the time goes in v9:
time: 25 us; the launch traced here: 24.6 us
  starting transfers between devices  11.6 us (46%)
  Pallas kernels  9.39 us (38%)
  between operations  2.11 us (8%)
  waiting for transfers between devices  0.79 us (3%)
  local copies, waits for them, and re-layouts  0.7 us (3%)
    ppermute x3, starting transfers between devices, shifted(): return lax.ppermute(value, axis, pairs)  6.58 us
    ppermute x2, starting transfers between devices, swapped(): return lax.ppermute(value, along, pairs)  2.83 us
    pallas_call x1, Pallas kernels, shards(): pl.pallas_call(functools.partial(inner_rest, parts), out_shape=[shape(nes...  2.71 us
    ppermute x2, starting transfers between devices, shifted_both(): return lax.ppermute(value, ('gx', 'gy', 'gz'), pairs)  2.16 us
    pallas_call x1, Pallas kernels, shards(): pl.pallas_call(pack_pair, out_shape=VMEM((rows, LANES), f32), in_specs=[i...  1.56 us
    pallas_call x1, Pallas kernels, shards(): pl.pallas_call(functools.partial(inner_first, band), out_shape=[shape((pa...  1.5 us
    pallas_call x1, Pallas kernels, shards(): pl.pallas_call(functools.partial(parent_step, parts, band), out_shape=[sh...  1.36 us
    pallas_call x1, Pallas kernels, shards(): pl.pallas_call(functools.partial(edges, parts, parent_cols), out_shape=[s...  1.26 us
  transfers between devices with their start and end apart: 7, of which 2 were waited for; matrix products, arithmetic and copies ran while one was open for 0% of the time, Pallas kernels for 23%

profile of v9, /device:TPU:0, one launch (start us, length us, event | category | flops | bytes accessed | tf_op | source)
XLA Modules:
  0.0 24.6 jit_solution(16067385036004454026)
XLA Ops:
  0.6 0.0 copy-start
  0.6 0.0 copy-start.1
  0.7 0.0 copy-start.2
  0.7 0.0 copy-start.3
  0.7 1.6 %pack_pair.1 = f32[72,128]{1,0:T(8,128)S(1)} custom-call(f32[8,72,384]{2,1,0:T(8,128)} %nest.5, f32[8,72,384]{2,1,0:T(8,128)} %source.6, f32[8,24,256]{2,1,0:T(8,128)} %parent.5, f32[8,24,256]{2,1,0:T(8,128)} %source.7), custom_call_target="tpu_custom_call" | custom-call | flops 200000 | bytes 800000 | tf_op jit(solution)/shard_map/pack_pair/pallas_call | solution.py:828
  2.2 0.0 copy-start.4
  2.3 3.0 %collective-permute-start = (f32[72,128]{1,0:T(8,128)S(1)}, f32[72,128]{1,0:T(8,128)S(1)}, u32[]{:S(2)}, u32[]{:S(2)}) collective-permute-start(f32[72,128]{1,0:T(8,128)S(1)} %pack_pair.1), channel_id=1, source_target_pairs={{0,2},{2,0},{1,3},{3,1},{4,6},{6,4},{5,7},{7,5},{8,10},{10,8},{9,1... | collective-permute-start | bytes 110600 | tf_op jit(solution)/shard_map/ppermute | solution.py:807
  5.9 0.0 copy-done
  5.9 0.0 copy-done.1
  5.9 0.0 copy-done.2
  5.9 0.0 copy-done.3
  5.9 0.0 copy-done.4
  6.0 1.5 %inner_first.1 = (f32[24,128]{1,0:T(8,128)S(1)}, f32[8,72,384]{2,1,0:T(8,128)S(1)}, s32[8,128]{1,0:T(8,128)S(1)}) custom-call(s32[1]{0:T(128)S(6)} %copy.13.oy_ref, f32[2,8]{1,0:T(2,128)S(1)} %copy-done.4, f32[8,72,384]{2,1,0:T(8,128)S(1)} %copy-done, f32[8,72,384]{2,1,0:T(8,128)S(1)} %copy-done.1, f32[8,24,256]{2,1,0:T(8,128)S(1)} %copy-done.2, ...), custom_call_target="tpu_custom_call" | custom-call | flops 4000000 | bytes 3000000 | tf_op jit(solution)/shard_map/inner_first/pallas_call | solution.py:866
  7.5 0.0 collective-permute-done.rest_0_.y_left.y_right
  7.5 0.1 pack_rows.1
  7.6 2.8 %collective-permute-start.1 = (f32[56,384]{1,0:T(8,128)S(1)}, f32[56,384]{1,0:T(8,128)S(1)}, u32[]{:S(2)}, u32[]{:S(2)}) collective-permute-start(f32[56,384]{1,0:T(8,128)S(1)} %get-tuple-element.32), channel_id=1, source_target_pairs={{1,4},{4,1},{5,8},{8,5},{9,12},{12,9},{13,0},{0,13},{3,6},{6,3},{7... | collective-permute-start | bytes 258056 | tf_op jit(solution)/shard_map/ppermute | solution.py:1044
  10.5 0.0 collective-permute-start.2
  11.1 0.0 copy-start.5
  11.1 0.7 %copy-done.5 = f32[2,8]{1,0:T(2,128)S(1)} copy-done((f32[2,8]{1,0:T(2,128)S(1)}, f32[2,8]{1,0:T(2,128)}, u32[]{:S(2)}) %copy-start.5) | copy-done | bytes 88
  11.8 2.7 %inner_rest.1 = (f32[8,72,384]{2,1,0:T(8,128)S(1)}, f32[4,72,128]{2,1,0:T(8,128)S(1)}, f32[8,2,8,384]{3,2,1,0:T(8,128)S(1)}, f32[8,2,8,384]{3,2,1,0:T(8,128)S(1)...) custom-call(f32[2,8]{1,0:T(2,128)S(1)} %copy-done.5, f32[2,8]{1,0:T(2,128)S(1)} %copy-done.4, ...), custom_call_target="tpu_custom_call" | custom-call | flops 8000000 | bytes 6000000 | tf_op jit(solution)/shard_map/inner_rest/pallas_call | solution.py:923
  14.5 0.0 collective-permute-done.1.across
  14.5 0.0 collective-permute-done.2.within
  14.5 1.3 %edges.1 = (f32[2,80,128]{2,1,0:T(8,128)S(1)}, f32[8,2,8,384]{3,2,1,0:T(8,128)S(1)}, f32[8,24,128]{2,1,0:T(8,128)S(1)}, f32[8,128]{1,0:T(8,128)S(1)}) custom-call(s32[1]{0:T(128)S(6)} %copy.12.ox_ref, f32[2,4,8,128]{3,2,1,0:T(8,128)S(1)} %get-tuple-element.26.spread, f32[3,192,128]{2,1,0:T(8,128)S(1)} %get-tuple-element.28.sums, ...), custom_call_target="tpu_custom_call" | custom-call | flops 4000000 | bytes 3000000 | tf_op jit(solution)/shard_map/edges/pallas_call | solution.py:943
  15.8 1.3 %collective-permute-start.4 = (f32[8,24,128]{2,1,0:T(8,128)S(1)}, f32[8,24,128]{2,1,0:T(8,128)S(1)}, u32[]{:S(2)}, u32[]{:S(2)}) collective-permute-start(f32[8,24,128]{2,1,0:T(8,128)S(1)} %get-tuple-element.41.rest_0_), channel_id=1, source_target_pairs={{0,2},{1,3},{2,1},{3,4},{4,6},{5,7},{6,5},{7,8},{8,10},{9,11},{10,... | collective-permute-start | bytes 294920 | tf_op jit(solution)/shard_map/ppermute | solution.py:1057
  17.1 0.0 collective-permute-start.5
  17.1 0.8 %collective-permute-start.6 = (f32[8,24,128]{2,1,0:T(8,128)S(1)}, f32[8,24,128]{2,1,0:T(8,128)S(1)}, u32[]{:S(2)}, u32[]{:S(2)}) collective-permute-start(f32[8,24,128]{2,1,0:T(8,128)S(1)} %get-tuple-element.41.rest_0_), channel_id=1, source_target_pairs={{0,3},{1,6},{2,0},{3,1},{4,7},{5,10},{6,4},{7,5},{8,11},{9,14},{10... | collective-permute-start | bytes 294920 | tf_op jit(solution)/shard_map/ppermute | solution.py:1057
  18.0 3.6 %collective-permute-start.3 = (f32[8,128]{1,0:T(8,128)S(1)}, f32[8,128]{1,0:T(8,128)S(1)}, u32[]{:S(2)}, u32[]{:S(2)}) collective-permute-start(f32[8,128]{1,0:T(8,128)S(1)} %get-tuple-element.40), channel_id=1, source_target_pairs={{0,12},{1,13},{4,0},{5,1},{8,4},{9,5},{12,8},{13,9},{2,14},{3,15},... | collective-permute-start | bytes 12296 | tf_op jit(solution)/shard_map/ppermute | solution.py:807
  21.5 1.4 %parent_step.1 = (f32[8,24,256]{2,1,0:T(8,128)S(1)}, f32[8,72,384]{2,1,0:T(8,128)}, f32[8,256]{1,0:T(8,128)S(1)}) custom-call(s32[1]{0:T(128)S(6)} %copy.12.ox_ref, s32[1]{0:T(128)S(6)} %copy.13.oy_ref, f32[2,4,8,128]{3,2,1,0:T(8,128)S(1)} %get-tuple-element.26.spread, f32[8,72,384]{2,1,0:T(8,128)S(1)} %get-tuple-element.27.third, ...), custom_call_target="tpu_custom_call" | custom-call | flops 800000 | bytes 2500000 | tf_op jit(solution)/shard_map/parent_step/pallas_call | solution.py:987
  22.9 0.0 collective-permute-done.3.beyond
  22.9 0.0 collective-permute-done.4.rest_1_
  22.9 0.1 collective-permute-done.5.rest_2_
  23.0 0.7 %collective-permute-done.6.rest_3_ = f32[8,24,128]{2,1,0:T(8,128)S(1)} collective-permute-done((f32[8,24,128]{2,1,0:T(8,128)S(1)}, f32[8,24,128]{2,1,0:T(8,128)S(1)}, u32[]{:S(2)}, u32[]{:S(2)}) %collective-permute-start.6) | collective-permute-done | bytes 98336 | tf_op jit(solution)/shard_map/ppermute | solution.py:1057
  23.7 0.8 %merge.1 = (f32[8,24,256]{2,1,0:T(8,128)}, f32[8,72,384]{2,1,0:T(8,128)}) custom-call(s32[1]{0:T(128)S(6)} %copy.12.ox_ref, s32[1]{0:T(128)S(6)} %copy.13.oy_ref, f32[8,256]{1,0:T(8,128)S(1)} %get-tuple-element.37.late, f32[8,24,256]{2,1,0:T(8,128)S(1)} %get-tuple-element.38.step, ...), custom_call_target="tpu_custom_call", output_to_operand_aliasing={{1}: (4, {})} | custom-call | flops 200000 | bytes 800000 | tf_op jit(solution)/shard_map/merge/pallas_call | solution.py:1018
Async XLA Ops:
  0.6 5.3 %copy-start = (f32[8,72,384]{2,1,0:T(8,128)S(1)}, f32[8,72,384]{2,1,0:T(8,128)}, u32[]{:S(2)}) copy-start(f32[8,72,384]{2,1,0:T(8,128)} %nest.5) | copy-start | bytes 2654212
  0.6 5.3 %copy-start.1 = (f32[8,72,384]{2,1,0:T(8,128)S(1)}, f32[8,72,384]{2,1,0:T(8,128)}, u32[]{:S(2)}) copy-start(f32[8,72,384]{2,1,0:T(8,128)} %source.6) | copy-start | bytes 2654212
  0.7 5.3 %copy-start.2 = (f32[8,24,256]{2,1,0:T(8,128)S(1)}, f32[8,24,256]{2,1,0:T(8,128)}, u32[]{:S(2)}) copy-start(f32[8,24,256]{2,1,0:T(8,128)} %parent.5) | copy-start | bytes 589828
  0.7 5.3 %copy-start.3 = (f32[8,24,256]{2,1,0:T(8,128)S(1)}, f32[8,24,256]{2,1,0:T(8,128)}, u32[]{:S(2)}) copy-start(f32[8,24,256]{2,1,0:T(8,128)} %source.7) | copy-start | bytes 589828
  2.2 3.7 %copy-start.4 = (f32[2,8]{1,0:T(2,128)S(1)}, f32[2,8]{1,0:T(2,128)}, u32[]{:S(2)}) copy-start(f32[2,8]{1,0:T(2,128)} %coefs.3) | copy-start | bytes 196
  2.3 5.2 %collective-permute-start = (f32[72,128]{1,0:T(8,128)S(1)}, f32[72,128]{1,0:T(8,128)S(1)}, u32[]{:S(2)}, u32[]{:S(2)}) collective-permute-start(f32[72,128]{1,0:T(8,128)S(1)} %pack_pair.1), channel_id=1, source_target_pairs={{0,2},{2,0},{1,3},{3,1},{4,6},{6,4},{5,7},{7,5},{8,10},{10,8},{9,1... | collective-permute-start | bytes 110600 | tf_op jit(solution)/shard_map/ppermute | solution.py:807
  7.6 6.9 %collective-permute-start.1 = (f32[56,384]{1,0:T(8,128)S(1)}, f32[56,384]{1,0:T(8,128)S(1)}, u32[]{:S(2)}, u32[]{:S(2)}) collective-permute-start(f32[56,384]{1,0:T(8,128)S(1)} %get-tuple-element.32), channel_id=1, source_target_pairs={{1,4},{4,1},{5,8},{8,5},{9,12},{12,9},{13,0},{0,13},{3,6},{6,3},{7... | collective-permute-start | bytes 258056 | tf_op jit(solution)/shard_map/ppermute | solution.py:1044
  10.5 4.1 %collective-permute-start.2 = (f32[56,384]{1,0:T(8,128)S(1)}, f32[56,384]{1,0:T(8,128)S(1)}, u32[]{:S(2)}, u32[]{:S(2)}) collective-permute-start(f32[56,384]{1,0:T(8,128)S(1)} %get-tuple-element.33), channel_id=1, source_target_pairs={{0,1},{1,0},{4,5},{5,4},{8,9},{9,8},{12,13},{13,12},{2,3},{3,2},{6... | collective-permute-start | bytes 258056 | tf_op jit(solution)/shard_map/ppermute | solution.py:1044
  11.1 0.7 %copy-start.5 = (f32[2,8]{1,0:T(2,128)S(1)}, f32[2,8]{1,0:T(2,128)}, u32[]{:S(2)}) copy-start(f32[2,8]{1,0:T(2,128)} %parent_coefs.1) | copy-start | bytes 196
  15.8 7.1 %collective-permute-start.4 = (f32[8,24,128]{2,1,0:T(8,128)S(1)}, f32[8,24,128]{2,1,0:T(8,128)S(1)}, u32[]{:S(2)}, u32[]{:S(2)}) collective-permute-start(f32[8,24,128]{2,1,0:T(8,128)S(1)} %get-tuple-element.41.rest_0_), channel_id=1, source_target_pairs={{0,2},{1,3},{2,1},{3,4},{4,6},{5,7},{6,5},{7,8},{8,10},{9,11},{10,... | collective-permute-start | bytes 294920 | tf_op jit(solution)/shard_map/ppermute | solution.py:1057
  17.1 5.9 %collective-permute-start.5 = (f32[8,24,128]{2,1,0:T(8,128)S(1)}, f32[8,24,128]{2,1,0:T(8,128)S(1)}, u32[]{:S(2)}, u32[]{:S(2)}) collective-permute-start(f32[8,24,128]{2,1,0:T(8,128)S(1)} %get-tuple-element.41.rest_0_), channel_id=1, source_target_pairs={{0,1},{1,4},{4,5},{5,8},{8,9},{9,12},{12,13},{13,0},{2,3},{3,6},{6... | collective-permute-start | bytes 294920 | tf_op jit(solution)/shard_map/ppermute | solution.py:807
  17.1 6.6 %collective-permute-start.6 = (f32[8,24,128]{2,1,0:T(8,128)S(1)}, f32[8,24,128]{2,1,0:T(8,128)S(1)}, u32[]{:S(2)}, u32[]{:S(2)}) collective-permute-start(f32[8,24,128]{2,1,0:T(8,128)S(1)} %get-tuple-element.41.rest_0_), channel_id=1, source_target_pairs={{0,3},{1,6},{2,0},{3,1},{4,7},{5,10},{6,4},{7,5},{8,11},{9,14},{10... | collective-permute-start | bytes 294920 | tf_op jit(solution)/shard_map/ppermute | solution.py:1057
  18.0 4.9 %collective-permute-start.3 = (f32[8,128]{1,0:T(8,128)S(1)}, f32[8,128]{1,0:T(8,128)S(1)}, u32[]{:S(2)}, u32[]{:S(2)}) collective-permute-start(f32[8,128]{1,0:T(8,128)S(1)} %get-tuple-element.40), channel_id=1, source_target_pairs={{0,12},{1,13},{4,0},{5,1},{8,4},{9,5},{12,8},{13,9},{2,14},{3,15},... | collective-permute-start | bytes 12296 | tf_op jit(solution)/shard_map/ppermute | solution.py:807

commit v10 on v7

--- a/solution.py
+++ b/solution.py
@@ -586,10 +586,8 @@
                         up = jnp.where(sub == 0, pltpu.roll(beyond_row, 1, 0), up)
                 beside = pltpu.roll(now, 1, 1) + pltpu.roll(now, width - 1, 1)
                 value = c_0 * now + c_h * ((up + down) + beside) + src[level, window]
-                if level > 0:
-                    value = value + c_v * here[level - 1, window]
-                if level < levels - 1:
-                    value = value + c_v * here[level + 1, window]
+                near = [here[at, window] for at in (level - 1, level + 1) if 0 <= at < levels]
+                value = value + c_v * sum(near[1:], near[0])
                 rim_o, rim_d = rims[level, window]
                 rim = rim_o + weight * rim_d
                 for piece in range(width // LANES):

time: 24.2 us -> 24.3 us (level)
  no operation moved by 1% of the time
where the time goes in v10:
time: 24.3 us; the launch traced here: 24.1 us
  starting transfers between devices  11.6 us (48%)
  Pallas kernels  9.38 us (39%)
  between operations  2.12 us (9%)
  waiting for transfers between devices  1.05 us (4%)
    ppermute x3, starting transfers between devices, shifted(): return lax.ppermute(value, axis, pairs)  6.61 us
    ppermute x2, starting transfers between devices, swapped(): return lax.ppermute(value, along, pairs)  2.83 us
    pallas_call x1, Pallas kernels, shards(): pl.pallas_call(functools.partial(inner_rest, parts), out_shape=[shape(nes...  2.71 us
    ppermute x2, starting transfers between devices, shifted_both(): return lax.ppermute(value, ('gx', 'gy', 'gz'), pairs)  2.14 us
    pallas_call x1, Pallas kernels, shards(): pl.pallas_call(pack_pair, out_shape=VMEM((rows, LANES), f32), in_specs=[i...  1.56 us
    pallas_call x1, Pallas kernels, shards(): pl.pallas_call(functools.partial(inner_first, band), out_shape=[shape((pa...  1.51 us
    pallas_call x1, Pallas kernels, shards(): pl.pallas_call(functools.partial(parent_step, parts, band), out_shape=[sh...  1.36 us
    pallas_call x1, Pallas kernels, shards(): pl.pallas_call(functools.partial(edges, parts, parent_cols), out_shape=[s...  1.24 us
  transfers between devices with their start and end apart: 7, of which 2 were waited for; matrix products, arithmetic and copies ran while one was open for 0% of the time, Pallas kernels for 23%

profile of v10, /device:TPU:0, one launch (start us, length us, event | category | flops | bytes accessed | tf_op | source)
XLA Modules:
  0.0 24.1 jit_solution(14174209286303775742)
XLA Ops:
  0.6 0.0 copy-start
  0.6 0.0 copy-start.1
  0.7 0.0 copy-start.2
  0.7 0.0 copy-start.3
  0.7 0.0 copy-start.5
  0.7 1.6 %pack_pair.1 = f32[72,128]{1,0:T(8,128)S(1)} custom-call(f32[8,72,384]{2,1,0:T(8,128)} %nest.5, f32[8,72,384]{2,1,0:T(8,128)} %source.6, f32[8,24,256]{2,1,0:T(8,128)} %parent.5, f32[8,24,256]{2,1,0:T(8,128)} %source.7), custom_call_target="tpu_custom_call" | custom-call | flops 200000 | bytes 800000 | tf_op jit(solution)/shard_map/pack_pair/pallas_call | solution.py:828
  2.2 0.0 copy-start.4
  2.3 3.0 %collective-permute-start = (f32[72,128]{1,0:T(8,128)S(1)}, f32[72,128]{1,0:T(8,128)S(1)}, u32[]{:S(2)}, u32[]{:S(2)}) collective-permute-start(f32[72,128]{1,0:T(8,128)S(1)} %pack_pair.1), channel_id=1, source_target_pairs={{0,2},{2,0},{1,3},{3,1},{4,6},{6,4},{5,7},{7,5},{8,10},{10,8},{9,1... | collective-permute-start | bytes 110600 | tf_op jit(solution)/shard_map/ppermute | solution.py:807
  5.9 0.0 copy-done
  5.9 0.0 copy-done.1
  5.9 0.0 copy-done.2
  5.9 0.0 copy-done.3
  6.0 0.0 copy-done.5
  6.0 0.0 copy-done.4
  6.0 1.5 %inner_first.1 = (f32[24,128]{1,0:T(8,128)S(1)}, f32[8,72,384]{2,1,0:T(8,128)S(1)}, f32[2,4,8,128]{3,2,1,0:T(8,128)S(1)}, s32[8,128]{1,0:T(8,128)S(1)}) custom-call(s32[1]{0:T(128)S(6)} %copy.13.oy_ref, f32[2,8]{1,0:T(2,128)S(1)} %copy-done.5, f32[2,8]{1,0:T(2,128)S(1)} %copy-done.4, f32[8,72,384]{2,1,0:T(8,128)S(1)} %copy-done, ...), custom_call_target="tpu_custom_call" | custom-call | flops 4000000 | bytes 3000000 | tf_op jit(solution)/shard_map/inner_first/pallas_call | solution.py:866
  7.5 0.0 collective-permute-done.rest_0_.y_left.y_right
  7.5 0.1 pack_rows.1
  7.7 2.8 %collective-permute-start.1 = (f32[56,384]{1,0:T(8,128)S(1)}, f32[56,384]{1,0:T(8,128)S(1)}, u32[]{:S(2)}, u32[]{:S(2)}) collective-permute-start(f32[56,384]{1,0:T(8,128)S(1)} %get-tuple-element.32), channel_id=1, source_target_pairs={{1,4},{4,1},{5,8},{8,5},{9,12},{12,9},{13,0},{0,13},{3,6},{6,3},{7... | collective-permute-start | bytes 258056 | tf_op jit(solution)/shard_map/ppermute | solution.py:1045
  10.5 0.0 collective-permute-start.2
  11.1 2.7 %inner_rest.1 = (f32[8,72,384]{2,1,0:T(8,128)S(1)}, f32[4,72,128]{2,1,0:T(8,128)S(1)}, f32[8,2,8,384]{3,2,1,0:T(8,128)S(1)}, f32[8,2,8,384]{3,2,1,0:T(8,128)S(1)}, f32[3,192,128]{2,1,0:T(8,128)S(1)}) custom-call(f32[2,8]{1,0:T(2,128)S(1)} %copy-done.4, f32[8,72,384]{2,1,0:T(8,128)S(1)} %copy-done, f32[8,72,384]{2,1,0:T(8,128)S(1)} %get-tuple-element.23.first, ...), custom_call_target="tpu_custom_call" | custom-call | flops 8000000 | bytes 6000000 | tf_op jit(solution)/shard_map/inner_rest/pallas_call | solution.py:925
  13.9 0.0 collective-permute-done.1.across
  13.9 0.0 collective-permute-done.2.within
  13.9 1.2 %edges.1 = (f32[2,80,128]{2,1,0:T(8,128)S(1)}, f32[8,2,8,384]{3,2,1,0:T(8,128)S(1)}, f32[8,24,128]{2,1,0:T(8,128)S(1)}, f32[8,128]{1,0:T(8,128)S(1)}) custom-call(s32[1]{0:T(128)S(6)} %copy.12.ox_ref, f32[2,4,8,128]{3,2,1,0:T(8,128)S(1)} %get-tuple-element.22.spread, f32[3,192,128]{2,1,0:T(8,128)S(1)} %get-tuple-element.28.sums, ...), custom_call_target="tpu_custom_call" | custom-call | flops 4000000 | bytes 3000000 | tf_op jit(solution)/shard_map/edges/pallas_call | solution.py:944
  15.1 2.0 %collective-permute-start.4 = (f32[8,24,128]{2,1,0:T(8,128)S(1)}, f32[8,24,128]{2,1,0:T(8,128)S(1)}, u32[]{:S(2)}, u32[]{:S(2)}) collective-permute-start(f32[8,24,128]{2,1,0:T(8,128)S(1)} %get-tuple-element.41.rest_0_), channel_id=1, source_target_pairs={{0,2},{1,3},{2,1},{3,4},{4,6},{5,7},{6,5},{7,8},{8,10},{9,11},{10,... | collective-permute-start | bytes 294920 | tf_op jit(solution)/shard_map/ppermute | solution.py:1058
  17.1 0.0 collective-permute-start.5
  17.1 0.2 collective-permute-start.6
  17.3 3.6 %collective-permute-start.3 = (f32[8,128]{1,0:T(8,128)S(1)}, f32[8,128]{1,0:T(8,128)S(1)}, u32[]{:S(2)}, u32[]{:S(2)}) collective-permute-start(f32[8,128]{1,0:T(8,128)S(1)} %get-tuple-element.40), channel_id=1, source_target_pairs={{0,12},{1,13},{4,0},{5,1},{8,4},{9,5},{12,8},{13,9},{2,14},{3,15},... | collective-permute-start | bytes 12296 | tf_op jit(solution)/shard_map/ppermute | solution.py:807
  20.9 1.4 %parent_step.1 = (f32[8,24,256]{2,1,0:T(8,128)S(1)}, f32[8,72,384]{2,1,0:T(8,128)}, f32[8,256]{1,0:T(8,128)S(1)}) custom-call(s32[1]{0:T(128)S(6)} %copy.12.ox_ref, s32[1]{0:T(128)S(6)} %copy.13.oy_ref, f32[2,4,8,128]{3,2,1,0:T(8,128)S(1)} %get-tuple-element.22.spread, f32[8,72,384]{2,1,0:T(8,128)S(1)} %get-tuple-element.27.third, ...), custom_call_target="tpu_custom_call" | custom-call | flops 800000 | bytes 2500000 | tf_op jit(solution)/shard_map/parent_step/pallas_call | solution.py:988
  22.2 0.0 collective-permute-done.3.beyond
  22.3 0.0 collective-permute-done.4.rest_1_
  22.3 0.7 %collective-permute-done.5.rest_2_ = f32[8,24,128]{2,1,0:T(8,128)S(1)} collective-permute-done((f32[8,24,128]{2,1,0:T(8,128)S(1)}, f32[8,24,128]{2,1,0:T(8,128)S(1)}, u32[]{:S(2)}, u32[]{:S(2)}) %collective-permute-start.5) | collective-permute-done | bytes 98336 | tf_op jit(solution)/shard_map/ppermute | solution.py:807
  23.0 0.3 %collective-permute-done.6.rest_3_ = f32[8,24,128]{2,1,0:T(8,128)S(1)} collective-permute-done((f32[8,24,128]{2,1,0:T(8,128)S(1)}, f32[8,24,128]{2,1,0:T(8,128)S(1)}, u32[]{:S(2)}, u32[]{:S(2)}) %collective-permute-start.6) | collective-permute-done | bytes 98336 | tf_op jit(solution)/shard_map/ppermute | solution.py:1058
  23.3 0.8 %merge.1 = (f32[8,24,256]{2,1,0:T(8,128)}, f32[8,72,384]{2,1,0:T(8,128)}) custom-call(s32[1]{0:T(128)S(6)} %copy.12.ox_ref, s32[1]{0:T(128)S(6)} %copy.13.oy_ref, f32[8,256]{1,0:T(8,128)S(1)} %get-tuple-element.37.late, f32[8,24,256]{2,1,0:T(8,128)S(1)} %get-tuple-element.38.step, ...), custom_call_target="tpu_custom_call", output_to_operand_aliasing={{1}: (4, {})} | custom-call | flops 200000 | bytes 800000 | tf_op jit(solution)/shard_map/merge/pallas_call | solution.py:1019
Async XLA Ops:
  0.6 5.3 %copy-start = (f32[8,72,384]{2,1,0:T(8,128)S(1)}, f32[8,72,384]{2,1,0:T(8,128)}, u32[]{:S(2)}) copy-start(f32[8,72,384]{2,1,0:T(8,128)} %nest.5) | copy-start | bytes 2654212
  0.6 5.3 %copy-start.1 = (f32[8,72,384]{2,1,0:T(8,128)S(1)}, f32[8,72,384]{2,1,0:T(8,128)}, u32[]{:S(2)}) copy-start(f32[8,72,384]{2,1,0:T(8,128)} %source.6) | copy-start | bytes 2654212
  0.7 5.3 %copy-start.2 = (f32[8,24,256]{2,1,0:T(8,128)S(1)}, f32[8,24,256]{2,1,0:T(8,128)}, u32[]{:S(2)}) copy-start(f32[8,24,256]{2,1,0:T(8,128)} %parent.5) | copy-start | bytes 589828
  0.7 5.3 %copy-start.3 = (f32[8,24,256]{2,1,0:T(8,128)S(1)}, f32[8,24,256]{2,1,0:T(8,128)}, u32[]{:S(2)}) copy-start(f32[8,24,256]{2,1,0:T(8,128)} %source.7) | copy-start | bytes 589828
  0.7 5.3 %copy-start.5 = (f32[2,8]{1,0:T(2,128)S(1)}, f32[2,8]{1,0:T(2,128)}, u32[]{:S(2)}) copy-start(f32[2,8]{1,0:T(2,128)} %parent_coefs.1) | copy-start | bytes 196
  2.2 3.7 %copy-start.4 = (f32[2,8]{1,0:T(2,128)S(1)}, f32[2,8]{1,0:T(2,128)}, u32[]{:S(2)}) copy-start(f32[2,8]{1,0:T(2,128)} %coefs.3) | copy-start | bytes 196
  2.3 5.2 %collective-permute-start = (f32[72,128]{1,0:T(8,128)S(1)}, f32[72,128]{1,0:T(8,128)S(1)}, u32[]{:S(2)}, u32[]{:S(2)}) collective-permute-start(f32[72,128]{1,0:T(8,128)S(1)} %pack_pair.1), channel_id=1, source_target_pairs={{0,2},{2,0},{1,3},{3,1},{4,6},{6,4},{5,7},{7,5},{8,10},{10,8},{9,1... | collective-permute-start | bytes 110600 | tf_op jit(solution)/shard_map/ppermute | solution.py:807
  7.7 6.2 %collective-permute-start.1 = (f32[56,384]{1,0:T(8,128)S(1)}, f32[56,384]{1,0:T(8,128)S(1)}, u32[]{:S(2)}, u32[]{:S(2)}) collective-permute-start(f32[56,384]{1,0:T(8,128)S(1)} %get-tuple-element.32), channel_id=1, source_target_pairs={{1,4},{4,1},{5,8},{8,5},{9,12},{12,9},{13,0},{0,13},{3,6},{6,3},{7... | collective-permute-start | bytes 258056 | tf_op jit(solution)/shard_map/ppermute | solution.py:1045
  10.5 3.4 %collective-permute-start.2 = (f32[56,384]{1,0:T(8,128)S(1)}, f32[56,384]{1,0:T(8,128)S(1)}, u32[]{:S(2)}, u32[]{:S(2)}) collective-permute-start(f32[56,384]{1,0:T(8,128)S(1)} %get-tuple-element.33), channel_id=1, source_target_pairs={{0,1},{1,0},{4,5},{5,4},{8,9},{9,8},{12,13},{13,12},{2,3},{3,2},{6... | collective-permute-start | bytes 258056 | tf_op jit(solution)/shard_map/ppermute | solution.py:1045
  15.1 7.1 %collective-permute-start.4 = (f32[8,24,128]{2,1,0:T(8,128)S(1)}, f32[8,24,128]{2,1,0:T(8,128)S(1)}, u32[]{:S(2)}, u32[]{:S(2)}) collective-permute-start(f32[8,24,128]{2,1,0:T(8,128)S(1)} %get-tuple-element.41.rest_0_), channel_id=1, source_target_pairs={{0,2},{1,3},{2,1},{3,4},{4,6},{5,7},{6,5},{7,8},{8,10},{9,11},{10,... | collective-permute-start | bytes 294920 | tf_op jit(solution)/shard_map/ppermute | solution.py:1058
  17.1 5.9 %collective-permute-start.5 = (f32[8,24,128]{2,1,0:T(8,128)S(1)}, f32[8,24,128]{2,1,0:T(8,128)S(1)}, u32[]{:S(2)}, u32[]{:S(2)}) collective-permute-start(f32[8,24,128]{2,1,0:T(8,128)S(1)} %get-tuple-element.41.rest_0_), channel_id=1, source_target_pairs={{0,1},{1,4},{4,5},{5,8},{8,9},{9,12},{12,13},{13,0},{2,3},{3,6},{6... | collective-permute-start | bytes 294920 | tf_op jit(solution)/shard_map/ppermute | solution.py:807
  17.1 6.2 %collective-permute-start.6 = (f32[8,24,128]{2,1,0:T(8,128)S(1)}, f32[8,24,128]{2,1,0:T(8,128)S(1)}, u32[]{:S(2)}, u32[]{:S(2)}) collective-permute-start(f32[8,24,128]{2,1,0:T(8,128)S(1)} %get-tuple-element.41.rest_0_), channel_id=1, source_target_pairs={{0,3},{1,6},{2,0},{3,1},{4,7},{5,10},{6,4},{7,5},{8,11},{9,14},{10... | collective-permute-start | bytes 294920 | tf_op jit(solution)/shard_map/ppermute | solution.py:1058
  17.3 5.0 %collective-permute-start.3 = (f32[8,128]{1,0:T(8,128)S(1)}, f32[8,128]{1,0:T(8,128)S(1)}, u32[]{:S(2)}, u32[]{:S(2)}) collective-permute-start(f32[8,128]{1,0:T(8,128)S(1)} %get-tuple-element.40), channel_id=1, source_target_pairs={{0,12},{1,13},{4,0},{5,1},{8,4},{9,5},{12,8},{13,9},{2,14},{3,15},... | collective-permute-start | bytes 12296 | tf_op jit(solution)/shard_map/ppermute | solution.py:807
